TPU v7x, 512 devices: a whole 4x4x16 slice. The times are simulated.
512 devices in a mesh: tm: 16 (over y_hi, x, core), rows: 32 (over y_lo, z).
Axes of the slice: x: 4, y: 4 (y_hi: 2, y_lo: 2; y = y_hi * 2 + y_lo), z: 16, core: 2. Of those that a mesh axis runs over, the one named last changes fastest.
Arguments:
- features: bfloat16 [64, 96, 128, 128], P('tm', None, 'rows'), may hold values from -6 to 6
- weights: bfloat16 [3, 3, 3, 96, 96], replicated, may hold values from -0.125 to 0.125
- cotangent: bfloat16 [64, 96, 128, 128], P('tm', None, 'rows'), may hold values from -6 to 6
Outputs:
- input_grad: bfloat16 [64, 96, 128, 128], P('tm', None, 'rows')
- weight_grad: float32 [3, 3, 3, 96, 96], replicated
All inputs are finite; a program needn't handle non-finite values.
Results may differ from a plain program's by a relative error of at most 0.004.
Values may be sent and summed in bfloat16 or wider, within the bound.
No kernel may reach another device: no remote copies, remote signals or barrier semaphores. Data moves between devices by JAX's collectives and lax.ppermute only.
A program may use at most 64 MiB of HBM per device.

v0:
```python
import jax
import jax.numpy as jnp
from jax import lax
from jax.sharding import PartitionSpec as P


def from_behind(value, axis, steps):
    count = lax.axis_size(axis)
    leading, last = (max(0, -steps), min(count, count - steps))
    return lax.ppermute(value, axis, [(source, source + steps) for source in range(leading, last)])


def padded(cells, sides, width):
    for axis, dim in sides:
        count = lax.axis_size(axis)
        ends = count - 1
        head = lax.slice_in_dim(cells, 0, width, axis=dim)
        tail = lax.slice_in_dim(cells, cells.shape[dim] - width, cells.shape[dim], axis=dim)
        cells = jnp.concatenate(
            [
                lax.ppermute(tail, axis, [(i, (i + 1) % count) for i in range(ends)]),
                cells,
                lax.ppermute(head, axis, [((i + 1) % count, i) for i in range(ends)]),
            ],
            axis=dim,
        )
    return cells


def normalize(features):
    values = features.astype(jnp.float32)
    scale = lax.rsqrt(jnp.mean(values * values, axis=1, keepdims=True) + 1e-06)
    return (values * scale, scale)


def transposed(grad_pad, weights, out_frames, height, width):
    total = jnp.zeros((out_frames, weights.shape[4], height, width), jnp.float32)
    for time_tap in range(3):
        for row_tap in range(3):
            for col_tap in range(3):
                window = grad_pad[
                    2 - time_tap : 2 - time_tap + out_frames,
                    :,
                    2 - row_tap : 2 - row_tap + height,
                    2 - col_tap : 2 - col_tap + width,
                ]
                total = total + jnp.einsum(
                    "oc,fohw->fchw",
                    weights[time_tap, row_tap, col_tap],
                    window,
                    preferred_element_type=jnp.float32,
                )
    return total


def terms_active_rows(cotangent, act_pad, weights, frames, height, width):
    pieces = []
    for time_tap in range(3):
        for row_tap in range(3):
            for col_tap in range(3):
                source = act_pad[
                    time_tap : time_tap + frames,
                    :,
                    row_tap : row_tap + height,
                    col_tap : col_tap + width,
                ]
                pieces.append(
                    jnp.einsum(
                        "fohw,fchw->oc", cotangent, source, preferred_element_type=jnp.float32
                    )
                )
    return jnp.stack(pieces).reshape(weights.shape)


def local(features, weights, cotangent):
    normed, scale = normalize(features)
    active = jax.nn.silu(normed).astype(jnp.bfloat16)
    frames, channels, height, width = features.shape
    cached = from_behind(active[frames - 2 :], "tm", 1)
    act_ext = jnp.concatenate([cached, active], axis=0)
    total_cells = frames * lax.axis_size("tm") * height * lax.axis_size("rows") * width
    norm_factor = 1.0 / jnp.sqrt(jnp.float32(total_cells))
    grad_halo = padded(cotangent, (("rows", 2),), 1)
    grad_pad = jnp.pad(grad_halo, ((2, 2), (0, 0), (0, 0), (1, 1)))
    grad_ext = transposed(grad_pad, weights, frames + 2, height, width)
    incoming = from_behind(grad_ext[:2].astype(jnp.bfloat16), "tm", -1).astype(jnp.float32)
    active_grad = grad_ext[2:].at[frames - 2 :].add(incoming)
    act_halo = padded(act_ext, (("rows", 2),), 1)
    act_pad = jnp.pad(act_halo, ((0, 0), (0, 0), (0, 0), (1, 1)))
    local_sum = terms_active_rows(cotangent, act_pad, weights, frames, height, width)
    weight_grad = lax.psum(local_sum, ("tm", "rows")) * norm_factor
    sigma = jax.nn.sigmoid(normed)
    normed_grad = active_grad * sigma * (1.0 + normed * (1.0 - sigma))
    inner = jnp.mean(normed_grad * normed, axis=1, keepdims=True)
    input_grad = scale * (normed_grad - normed * inner) + cotangent.astype(jnp.float32)
    return (input_grad.astype(jnp.bfloat16), weight_grad)


def solution(mesh):
    return jax.shard_map(
        local,
        mesh=mesh,
        in_specs=(P("tm", None, "rows", None), P(), P("tm", None, "rows", None)),
        out_specs=(P("tm", None, "rows", None), P()),
        check_vma=False,
    )
```

profile of v0, /device:TPU:1, one launch (start us, length us, event | category | flops | bytes accessed | tf_op | source)
XLA Modules:
  0.0 566.2 jit_solution(1731954056661822266)
XLA Ops:
  8.3 4.4 collective-permute-start
  12.7 1.3 collective-permute-start.1
  14.3 3.9 collective-permute-done.1
  25.4 1.4 fusion.112
  26.8 1.4 fusion.114
  28.2 1.4 fusion.116
  29.7 1.5 fusion.118
  31.1 1.4 fusion.120
  32.5 1.4 fusion.90
  33.9 1.4 fusion.92
  35.4 1.4 fusion.94
  36.7 1.4 fusion.96
  38.2 1.4 fusion.98
  39.6 7.2 %fusion.35 = f32[6,96,4,128]{3,1,2,0:T(8,128)S(1)} fusion(f32[6,96,4,128]{3,1,2,0:T(8,128)S(1)} %convolution_bitcast_fusion, f32[6,96,4,128]{3,1,2,0:T(8,128)S(1)} %convolution_bitcast_fusion.1, f32[6,96,4,128]{3,1,2,0:T(8,128)S(1)} %convolution_bitcast_fusion.2, f32[6,96,4,128]{3,1,2,0:T(8,128)S(1)} %convolution_bitcast_fusion.3, ...), kind=kOutput, calls=%fused_computation.56 | convolution fusion | flops 64290816 | bytes 32464896 | tf_op jit(solution)/shard_map/oc,fohw->fchw/dot_general | solution.py:47
  46.8 7.0 %collective-permute-start.2 = (bf16[2,96,4,128]{3,1,2,0:T(8,128)(2,1)S(1)}, bf16[2,96,4,128]{3,1,2,0:T(8,128)(2,1)S(1)}, u32[]{:S(2)}, u32[]{:S(2)}) collective-permute-start(bf16[2,96,4,128]{3,1,2,0:T(8,128)(2,1)S(1)} %slice.652), channel_id=1, source_target_pairs={{32,0},{64,32},{96,64},{128,96},{160,128},{192,160},{224,192},{256... | collective-permute-start | bytes 589832 | tf_op jit(solution)/shard_map/ppermute | solution.py:10
  53.9 1.3 collective-permute-done.2
  56.2 1.9 collective-permute-start.3
  58.1 2.6 collective-permute-done.3
  60.8 3.5 collective-permute-start.4
  65.6 1.8 collective-permute-done.4
  67.4 5.1 collective-permute-done.5
  81.4 1.5 copy.64
  83.8 473.1 %all-reduce.4.cloned.1.call-done = f32[3,3,3,96,96]{4,3,2,1,0:T(8,128)} async-done(((f32[3,3,3,96,96]{4,3,2,1,0:T(8,128)}), f32[3,3,3,96,96]{4,3,2,1,0:T(8,128)}) %all-reduce.4.cloned.1.call-update) | async-done | bytes 995344 | tf_op jit(solution)/shard_map/psum | solution.py:91
  556.9 2.5 broadcast_multiply_fusion
  (70 shorter events, 20.5 us)
Async XLA Ops:
  7.2 6.9 %copy-start = (bf16[4,96,4,128]{3,2,1,0:T(4,128)(2,1)S(1)}, bf16[4,96,4,128]{3,2,1,0:T(4,128)(2,1)}, u32[]{:S(2)}) copy-start(bf16[4,96,4,128]{3,2,1,0:T(4,128)(2,1)} %param.5) | copy-start | bytes 1179652
  7.2 549.7 %all-reduce.4.cloned.1.call-start = ((), (), s32[]{:S(2)}) async-start(), calls=%async_computation | async-start | bytes 2654208 | tf_op jit(solution)/shard_map/psum | solution.py:91
  8.3 6.0 %collective-permute-start = (bf16[4,96,1,128]{3,1,2,0:T(8,128)(2,1)S(1)}, bf16[4,96,1,128]{3,1,2,0:T(8,128)(2,1)S(1)}, u32[]{:S(2)}, u32[]{:S(2)}) collective-permute-start(bf16[4,96,1,128]{3,1,2,0:T(8,128)(2,1)S(1)} %get-tuple-element.20), channel_id=1, source_target_pairs={{0,1},{1,2},{2,3},{3,4},{4,5},{5,6},{6,7},{7,8},{8,9},{9,10},{10,1... | collective-permute-start | bytes 294920 | tf_op jit(solution)/shard_map/ppermute | solution.py:21
  12.7 5.5 collective-permute-start.1
  14.1 5.1 copy-start.3
  46.8 8.5 %copy-start.1 = (bf16[4,96,4,128]{3,2,1,0:T(4,128)(2,1)S(1)}, bf16[4,96,4,128]{3,2,1,0:T(4,128)(2,1)}, u32[]{:S(2)}) copy-start(bf16[4,96,4,128]{3,2,1,0:T(4,128)(2,1)} %param.5) | copy-start | bytes 1179652
  46.8 8.4 %collective-permute-start.2 = (bf16[2,96,4,128]{3,1,2,0:T(8,128)(2,1)S(1)}, bf16[2,96,4,128]{3,1,2,0:T(8,128)(2,1)S(1)}, u32[]{:S(2)}, u32[]{:S(2)}) collective-permute-start(bf16[2,96,4,128]{3,1,2,0:T(8,128)(2,1)S(1)} %slice.652), channel_id=1, source_target_pairs={{32,0},{64,32},{96,64},{128,96},{160,128},{192,160},{224,192},{256... | collective-permute-start | bytes 589832 | tf_op jit(solution)/shard_map/ppermute | solution.py:10
  53.9 1.8 copy-start.2
  56.2 4.5 collective-permute-start.3
  60.8 6.6 %collective-permute-start.4 = (bf16[6,96,1,128]{3,1,2,0:T(8,128)(2,1)S(1)}, bf16[6,96,1,128]{3,1,2,0:T(8,128)(2,1)S(1)}, u32[]{:S(2)}, u32[]{:S(2)}) collective-permute-start(bf16[6,96,1,128]{3,1,2,0:T(8,128)(2,1)S(1)} %get-tuple-element.16), channel_id=1, source_target_pairs={{0,1},{1,2},{2,3},{3,4},{4,5},{5,6},{6,7},{7,8},{8,9},{9,10},{10,1... | collective-permute-start | bytes 442376 | tf_op jit(solution)/shard_map/ppermute | solution.py:21
  64.3 8.2 %collective-permute-start.5 = (bf16[6,96,1,128]{3,1,2,0:T(8,128)(2,1)S(1)}, bf16[6,96,1,128]{3,1,2,0:T(8,128)(2,1)S(1)}, u32[]{:S(2)}, u32[]{:S(2)}) collective-permute-start(bf16[6,96,1,128]{3,1,2,0:T(8,128)(2,1)S(1)} %get-tuple-element.17), channel_id=1, source_target_pairs={{1,0},{2,1},{3,2},{4,3},{5,4},{6,5},{7,6},{8,7},{9,8},{10,9},{11,1... | collective-permute-start | bytes 442376 | tf_op jit(solution)/shard_map/ppermute | solution.py:23
Sparse Core Ops, SparseCore 0:
  83.0 473.8 all-reduce.3
where the time goes:
time: 567 us; the launch traced here: 566 us
  waiting for transfers between devices  488 us (86%)
  matrix products  35.2 us (6%)
  starting transfers between devices  19.4 us (3%)
  between operations  14.5 us (3%)
    psum x1, waiting for transfers between devices, local(): weight_grad = lax.psum(local_sum, ('tm', 'rows')) * norm_factor  473 us
    dot_general x27, matrix products, transposed(): jnp.einsum('oc,fohw->fchw', weights[time_tap, row_tap, col_tap], window,...  27.5 us
  transfers between devices with their start and end apart: 7, of which 7 were waited for; matrix products, arithmetic and copies ran while one was open for 0% of the time, Pallas kernels for 0%

commit v1 on v0

v1 whole, which is shorter than its diff:
```python
import jax
import jax.numpy as jnp
from jax import lax
from jax.experimental import pallas as pl
from jax.experimental.pallas import tpu as pltpu
from jax.sharding import Mesh, PartitionSpec as P

TM = ("y_hi", "x", "core")
ROWS = ("y_lo", "z")
PLANE = ("y_hi", "x", "core", "y_lo")
CH = 96
W = 128
F = 4
H = 4
FE = F + 2
HE = H + 2
PACKED = 2048
F32 = jnp.float32
BF16 = jnp.bfloat16


def dot(a, b, dims):
    return lax.dot_general(a, b, (dims, ((), ())), preferred_element_type=F32)


def row_picker(h):
    pair = lax.broadcasted_iota(jnp.int32, (CH, H * CH), 1)
    channel = lax.broadcasted_iota(jnp.int32, (CH, H * CH), 0)
    return jnp.where(pair == channel * H + h, 1.0, 0.0).astype(BF16)


def row_placer(h):
    pair = lax.broadcasted_iota(jnp.int32, (H * CH, CH), 0)
    channel = lax.broadcasted_iota(jnp.int32, (H * CH, CH), 1)
    return jnp.where(pair == channel * H + h, 1.0, 0.0).astype(BF16)


def compute_kernel(feat, cot, next_frames, above, below, weights, grad_out, packed, win, act, normed, sigma, scale, wsum):
    lane = lax.broadcasted_iota(jnp.int32, (CH, W), 1)

    cot_all = jnp.concatenate([cot[f] for f in range(F)] + [next_frames[f] for f in range(2)], axis=1)
    feat_all = jnp.concatenate([feat[f] for f in range(F)], axis=1)
    for row in range(HE):
        if row == 0:
            plain = jnp.concatenate([above[f] for f in range(FE)], axis=1).astype(F32)
        elif row == HE - 1:
            plain = jnp.concatenate([below[f] for f in range(FE)], axis=1).astype(F32)
        else:
            plain = dot(row_picker(row - 1), cot_all, ((1,), (0,)))
        base = row * 3 * CH
        win[base + CH : base + 2 * CH, :] = plain.astype(BF16)
        for f in range(FE):
            part = plain[:, f * W : (f + 1) * W]
            left = jnp.where(lane == W - 1, 0.0, pltpu.roll(part, W - 1, 1))
            right = jnp.where(lane == 0, 0.0, pltpu.roll(part, 1, 1))
            win[base : base + CH, f * W : (f + 1) * W] = left.astype(BF16)
            win[base + 2 * CH : base + 3 * CH, f * W : (f + 1) * W] = right.astype(BF16)

    for h in range(H):
        values = dot(row_picker(h), feat_all, ((1,), (0,)))
        s = lax.rsqrt(jnp.sum(values * values, axis=0, keepdims=True) * (1.0 / CH) + 1e-06)
        n = values * s
        sig = 1.0 / (1.0 + jnp.exp(-n))
        act[h] = (n * sig).astype(BF16)
        normed[h] = n
        sigma[h] = sig
        scale[h] = s

    for t in range(3):
        total = None
        for h in range(H):
            window = win[h * 3 * CH : (h + 3) * 3 * CH, (2 - t) * W : (2 - t) * W + F * W]
            term = dot(window, act[h], ((1,), (1,)))
            total = term if total is None else total + term
        wsum[t * 9 * CH : (t + 1) * 9 * CH, :] = total

    third = CH // 3
    for group in range(6):
        last = wsum[(group * 4 + 3) * CH : (group * 4 + 4) * CH, :]
        for k in range(3):
            own = wsum[(group * 4 + k) * CH : (group * 4 + k + 1) * CH, :]
            tile = jnp.concatenate([own, last[:, k * third : (k + 1) * third]], axis=1)
            packed[(group * 3 + k) * CH : (group * 3 + k + 1) * CH, :] = tile.astype(BF16)
    for k in range(3):
        own = wsum[(24 + k) * CH : (25 + k) * CH, :]
        tile = jnp.concatenate([own, jnp.zeros((CH, W - CH), F32)], axis=1)
        packed[(18 + k) * CH : (19 + k) * CH, :] = tile.astype(BF16)
    packed[21 * CH :, :] = jnp.zeros((PACKED - 21 * CH, W), BF16)

    by_time = []
    for t in range(3):
        stacked = jnp.concatenate([weights[t * 9 + r * 3 + c] for r in (2, 1, 0) for c in range(3)], axis=0)
        by_time.append(stacked.T)
    placed = None
    for h in range(H):
        grad = None
        for t in range(3):
            window = win[h * 3 * CH : (h + 3) * 3 * CH, (2 - t) * W : (2 - t) * W + F * W]
            term = dot(by_time[t], window, ((1,), (0,)))
            grad = term if grad is None else grad + term
        n, sig = normed[h], sigma[h]
        grad = grad * sig * (1.0 + n * (1.0 - sig))
        inner = jnp.sum(grad * n, axis=0, keepdims=True) * (1.0 / CH)
        own = win[(h + 1) * 3 * CH + CH : (h + 1) * 3 * CH + 2 * CH, : F * W].astype(F32)
        result = (scale[h] * (grad - n * inner) + own).astype(BF16)
        term = dot(row_placer(h), result, ((1,), (0,)))
        placed = term if placed is None else placed + term
    for f in range(F):
        grad_out[f] = placed[:, f * W : (f + 1) * W].astype(BF16)


def unpack_kernel(norm_factor, packed, out):
    third = CH // 3

    def place(position, value):
        t, k, c = position // 9, position // 3 % 3, position % 3
        out[t * 9 + (2 - k) * 3 + c] = value * norm_factor

    for group in range(6):
        tiles = [packed[(group * 3 + k) * CH : (group * 3 + k + 1) * CH, :].astype(F32) for k in range(3)]
        for k in range(3):
            place(group * 4 + k, tiles[k][:, :CH])
        place(group * 4 + 3, jnp.concatenate([tile[:, CH:] for tile in tiles], axis=1))
    for k in range(3):
        place(24 + k, packed[(18 + k) * CH : (19 + k) * CH, :].astype(F32)[:, :CH])


def vmem(count):
    return [pl.BlockSpec(memory_space=pltpu.VMEM)] * count


def spread(value, count):
    return jnp.broadcast_to(value, (count,) + value.shape)


def local(features, weights, cotangent):
    tm, rows = lax.axis_size(TM), lax.axis_size(ROWS)
    plane, depth = lax.axis_size(PLANE), lax.axis_size("z")
    cells = F * tm * H * rows * W

    next_frames = lax.ppermute(cotangent[:2], TM, [(i + 1, i) for i in range(tm - 1)])
    ext = jnp.concatenate([cotangent, next_frames], axis=0)
    above = lax.ppermute(ext[:, :, H - 1, :], ROWS, [(i, i + 1) for i in range(rows - 1)])
    below = lax.ppermute(ext[:, :, 0, :], ROWS, [(i + 1, i) for i in range(rows - 1)])

    input_grad, packed = pl.pallas_call(
        compute_kernel,
        out_shape=(
            jax.ShapeDtypeStruct((F, CH * H, W), BF16),
            jax.ShapeDtypeStruct((PACKED, W), BF16),
        ),
        in_specs=vmem(6),
        out_specs=tuple(vmem(2)),
        scratch_shapes=[
            pltpu.VMEM((HE * 3 * CH, FE * W), BF16),
            pltpu.VMEM((H, CH, F * W), BF16),
            pltpu.VMEM((H, CH, F * W), F32),
            pltpu.VMEM((H, CH, F * W), F32),
            pltpu.VMEM((H, 1, F * W), F32),
            pltpu.VMEM((27 * CH, CH), F32),
        ],
        compiler_params=pltpu.CompilerParams(vmem_limit_bytes=40 << 20),
        name="compute",
    )(
        features.reshape(F, CH * H, W),
        cotangent.reshape(F, CH * H, W),
        next_frames.reshape(2, CH * H, W),
        above,
        below,
        weights.reshape(27, CH, CH),
    )

    part = PACKED // plane
    parts = lax.all_to_all(packed.reshape(plane, part, W), PLANE, 0, 0)
    mine = jnp.sum(parts.astype(F32), axis=0).astype(BF16)
    slabs = lax.all_to_all(spread(mine, depth), "z", 0, 0)
    mine = jnp.sum(slabs.astype(F32), axis=0).astype(BF16)
    whole = lax.all_to_all(spread(mine, plane), PLANE, 0, 0).reshape(PACKED, W)

    weight_grad = pl.pallas_call(
        lambda *refs: unpack_kernel(1.0 / float(cells) ** 0.5, *refs),
        out_shape=jax.ShapeDtypeStruct((27, CH, CH), F32),
        in_specs=vmem(1),
        out_specs=vmem(1)[0],
        compiler_params=pltpu.CompilerParams(vmem_limit_bytes=40 << 20),
        name="unpack",
    )(whole)
    return (input_grad.reshape(F, CH, H, W), weight_grad.reshape(3, 3, 3, CH, CH))


def solution(mesh):
    fine = Mesh(mesh.devices.reshape(2, 4, 2, 2, 16), ("y_hi", "x", "core", "y_lo", "z"))
    return jax.shard_map(
        local,
        mesh=fine,
        in_specs=(P(TM, None, ROWS, None), P(), P(TM, None, ROWS, None)),
        out_specs=(P(TM, None, ROWS, None), P()),
        check_vma=False,
    )
```

time: 567 us -> 95.7 us (0.17)
  waiting for transfers between devices: 488 us -> 2.38 us
  blocking collectives: 0 us -> 67.4 us
  matrix products: 35.2 us -> 0 us
  between operations: 14.5 us -> 0.74 us
  Pallas kernels: 0 us -> 8.04 us
    psum x1 -> x0, waiting for transfers between devices: 473 us -> none  [local(): weight_grad = lax.psum(local_sum, ('tm', 'rows')) * norm_factor]
    all_to_all x0 -> x3, blocking collectives: none -> 67.4 us  [the longest x1 28.7 us: local(): parts = lax.all_to_all(packed.reshape(plane, part, W), PLANE, 0, 0)]
    dot_general x54 -> x0, matrix products: 35.2 us -> none  [the longest x27 27.5 us: transposed(): jnp.einsum('oc,fohw->fchw', weights[time_tap, row_tap, col_tap], window,...]
    ppermute x6 -> x3, waiting for transfers between devices: 14.9 us -> 2.38 us  [the longest x1 1.51 us: local(): lax.ppermute(ext[:, :, 0, :], ROWS, [(i + 1, i) for i in range(rows - 1)])]
    pallas_call x0 -> x2, Pallas kernels: none -> 8.04 us  [the longest x1 6.79 us: local(): pl.pallas_call(compute_kernel, out_shape=(jax.ShapeDtypeStruct((F, CH * H...]
    ppermute x6 -> x3, starting transfers between devices: 19.4 us -> 14.2 us  [the longest x1 8.92 us: local(): lax.ppermute(cotangent[:2], TM, [(i + 1, i) for i in range(tm - 1)])]
  transfers between devices with their start and end apart: 7 -> 3, of which waited for: 7 -> 2; matrix products, arithmetic and copies ran while one was open for 0% -> 1% of each run, Pallas kernels for 0% -> 0%
where the time goes in v1:
time: 95.7 us; the launch traced here: 95.3 us
  blocking collectives  67.4 us (70%)
  starting transfers between devices  14.2 us (15%)
  Pallas kernels  8.04 us (8%)
  local copies, waits for them, and re-layouts  2.46 us (3%)
  waiting for transfers between devices  2.38 us (2%)
    all_to_all x1, blocking collectives, local(): parts = lax.all_to_all(packed.reshape(plane, part, W), PLANE, 0, 0)  28.7 us
    all_to_all x1, blocking collectives, local(): whole = lax.all_to_all(spread(mine, plane), PLANE, 0, 0).reshape(PACKED, W)  21.2 us
    all_to_all x1, blocking collectives, local(): slabs = lax.all_to_all(spread(mine, depth), 'z', 0, 0)  17.5 us
    ppermute x1, starting transfers between devices, local(): lax.ppermute(cotangent[:2], TM, [(i + 1, i) for i in range(tm - 1)])  8.92 us
    pallas_call x1, Pallas kernels, local(): pl.pallas_call(compute_kernel, out_shape=(jax.ShapeDtypeStruct((F, CH * H...  6.79 us
    ppermute x1, starting transfers between devices, local(): lax.ppermute(ext[:, :, H - 1, :], ROWS, [(i, i + 1) for i in range(rows -...  3.99 us
  transfers between devices with their start and end apart: 3, of which 2 were waited for; matrix products, arithmetic and copies ran while one was open for 1% of the time, Pallas kernels for 0%

profile of v1, /device:TPU:1, one launch (start us, length us, event | category | flops | bytes accessed | tf_op | source)
XLA Modules:
  0.0 95.3 jit_solution(8926679846711799793)
XLA Ops:
  0.6 1.0 %slice.12 = bf16[2,96,4,128]{3,2,1,0:T(4,128)(2,1)S(1)} slice(bf16[4,96,4,128]{3,2,1,0:T(4,128)(2,1)} %param.5), slice={[0:2], [0:96], [0:4], [0:128]} | slice | bytes 393216 | tf_op jit(solution)/shard_map/slice | solution.py:141
  1.6 0.0 copy-start
  1.6 0.0 copy-start.1
  1.7 0.0 copy-start.2
  1.7 8.9 %collective-permute-start = (bf16[2,96,4,128]{3,1,0,2:T(8,128)(2,1)S(1)}, bf16[2,96,4,128]{3,1,0,2:T(8,128)(2,1)S(1)}, u32[]{:S(2)}, u32[]{:S(2)}) collective-permute-start(bf16[2,96,4,128]{3,1,0,2:T(8,128)(2,1)S(1)} %copy.14), channel_id=1, source_target_pairs={{32,0},{64,32},{96,64},{128,96},{160,128},{192,160},{224,192},{256... | collective-permute-start | bytes 589832 | tf_op jit(solution)/shard_map/ppermute | solution.py:141
  10.6 1.1 %constant_dynamic-update-slice_fusion.1 = bf16[6,96,4,128]{3,1,0,2:T(8,128)(2,1)S(1)} fusion(bf16[4,96,4,128]{3,2,1,0:T(4,128)(2,1)} %param.5), kind=kLoop, calls=%fused_computation.3 | loop fusion | bytes 786432
  11.7 0.0 collective-permute-done
  11.8 1.3 %collective-permute-start.2 = (bf16[6,96,128]{2,1,0:T(8,128)(2,1)S(1)}, bf16[6,96,128]{2,1,0:T(8,128)(2,1)S(1)}, u32[]{:S(2)}, u32[]{:S(2)}) collective-permute-start(bf16[6,96,128]{2,1,0:T(8,128)(2,1)S(1)} %get-tuple-element.6), channel_id=1, source_target_pairs={{1,0},{2,1},{3,2},{4,3},{5,4},{6,5},{7,6},{8,7},{9,8},{10,9},{11,1... | collective-permute-start | bytes 442376 | tf_op jit(solution)/shard_map/ppermute | solution.py:144
  13.1 4.0 %collective-permute-start.1 = (bf16[6,96,128]{2,1,0:T(8,128)(2,1)S(1)}, bf16[6,96,128]{2,1,0:T(8,128)(2,1)S(1)}, u32[]{:S(2)}, u32[]{:S(2)}) collective-permute-start(bf16[6,96,128]{2,1,0:T(8,128)(2,1)S(1)} %get-tuple-element.7), channel_id=1, source_target_pairs={{0,1},{1,2},{2,3},{3,4},{4,5},{5,6},{6,7},{7,8},{8,9},{9,10},{10,1... | collective-permute-start | bytes 442376 | tf_op jit(solution)/shard_map/ppermute | solution.py:143
  17.1 0.2 copy.11
  17.2 1.5 %collective-permute-done.2.below = bf16[6,96,128]{2,1,0:T(8,128)(2,1)S(1)} collective-permute-done((bf16[6,96,128]{2,1,0:T(8,128)(2,1)S(1)}, bf16[6,96,128]{2,1,0:T(8,128)(2,1)S(1)}, u32[]{:S(2)}, u32[]{:S(2)}) %collective-permute-start.2) | collective-permute-done | bytes 147488 | tf_op jit(solution)/shard_map/ppermute | solution.py:144
  18.7 0.9 collective-permute-done.1.above
  19.6 0.0 copy-done
  19.6 0.0 copy-done.1
  19.6 0.0 copy-done.2
  19.6 6.8 %compute.1 = (bf16[4,384,128]{2,1,0:T(8,128)(2,1)}, bf16[2048,128]{1,0:T(8,128)(2,1)S(1)}) custom-call(bf16[4,384,128]{2,1,0:T(8,128)(2,1)S(1)} %bitcast.17, bf16[4,384,128]{2,1,0:T(8,128)(2,1)S(1)} %bitcast.12, bf16[2,384,128]{2,1,0:T(8,128)(2,1)S(1)} %bitcast.14, bf16[6,96,128]{2,1,0:T(8,128)(2,1)S(1)} %collective-permute-done.1.above, ...), custom_call_target="tpu_custom_call" | custom-call | tf_op jit(solution)/shard_map/compute/pallas_call | solution.py:146
  26.4 28.7 %all_to_all.15 = bf16[32,64,128]{2,1,0:T(8,128)(2,1)S(1)} all-to-all(bf16[32,64,128]{2,1,0:T(8,128)(2,1)S(1)} %bitcast.16), channel_id=1, replica_groups=mesh['y_hi'=2,'x'=4,'core'=2,'y_lo'=2,'z'=16] {'y_hi','x','core','y_lo'}, dimensions={0} | all-to-all | bytes 1048576 | tf_op jit(solution)/shard_map/all_to_all | solution.py:174
  55.1 0.1 reduce_sum.24
  55.2 17.5 %all_to_all.16 = bf16[16,64,128]{2,1,0:T(8,128)(2,1)S(1)} all-to-all(bf16[16,64,128]{2,1,0:T(8,128)(2,1)S(1)} %broadcast_in_dim.6), channel_id=1, replica_groups=mesh['y_hi'=2,'x'=4,'core'=2,'y_lo'=2,'z'=16] {'z'}, dimensions={0} | all-to-all | bytes 524288 | tf_op jit(solution)/shard_map/all_to_all | solution.py:176
  72.8 0.1 broadcast_in_dim.7
  72.9 21.2 %all_to_all.17 = bf16[32,64,128]{2,1,0:T(8,128)(2,1)S(1)} all-to-all(bf16[32,64,128]{2,1,0:T(8,128)(2,1)S(1)} %broadcast_in_dim.7), channel_id=1, replica_groups=mesh['y_hi'=2,'x'=4,'core'=2,'y_lo'=2,'z'=16] {'y_hi','x','core','y_lo'}, dimensions={0} | all-to-all | bytes 1048576 | tf_op jit(solution)/shard_map/all_to_all | solution.py:178
  94.1 1.2 %unpack.1 = f32[27,96,96]{2,1,0:T(8,128)} custom-call(bf16[2048,128]{1,0:T(8,128)(2,1)S(1)} %bitcast.13), custom_call_target="tpu_custom_call" | custom-call | tf_op jit(solution)/shard_map/unpack/pallas_call | solution.py:180
  (5 shorter events, 0.2 us)
Async XLA Ops:
  1.6 18.0 %copy-start = (bf16[4,96,4,128]{3,2,1,0:T(4,128)(2,1)S(1)}, bf16[4,96,4,128]{3,2,1,0:T(4,128)(2,1)}, u32[]{:S(2)}) copy-start(bf16[4,96,4,128]{3,2,1,0:T(4,128)(2,1)} %param.5) | copy-start | bytes 1179652
  1.6 18.0 %copy-start.1 = (bf16[3,3,3,96,96]{4,3,2,1,0:T(8,128)(2,1)S(1)}, bf16[3,3,3,96,96]{4,3,2,1,0:T(8,128)(2,1)}, u32[]{:S(2)}) copy-start(bf16[3,3,3,96,96]{4,3,2,1,0:T(8,128)(2,1)} %param.4) | copy-start | bytes 1492996
  1.7 18.0 %copy-start.2 = (bf16[4,96,4,128]{3,2,1,0:T(4,128)(2,1)S(1)}, bf16[4,96,4,128]{3,2,1,0:T(4,128)(2,1)}, u32[]{:S(2)}) copy-start(bf16[4,96,4,128]{3,2,1,0:T(4,128)(2,1)} %param.3) | copy-start | bytes 1179652
  1.7 10.0 %collective-permute-start = (bf16[2,96,4,128]{3,1,0,2:T(8,128)(2,1)S(1)}, bf16[2,96,4,128]{3,1,0,2:T(8,128)(2,1)S(1)}, u32[]{:S(2)}, u32[]{:S(2)}) collective-permute-start(bf16[2,96,4,128]{3,1,0,2:T(8,128)(2,1)S(1)} %copy.14), channel_id=1, source_target_pairs={{32,0},{64,32},{96,64},{128,96},{160,128},{192,160},{224,192},{256... | collective-permute-start | bytes 589832 | tf_op jit(solution)/shard_map/ppermute | solution.py:141
  11.8 7.0 %collective-permute-start.2 = (bf16[6,96,128]{2,1,0:T(8,128)(2,1)S(1)}, bf16[6,96,128]{2,1,0:T(8,128)(2,1)S(1)}, u32[]{:S(2)}, u32[]{:S(2)}) collective-permute-start(bf16[6,96,128]{2,1,0:T(8,128)(2,1)S(1)} %get-tuple-element.6), channel_id=1, source_target_pairs={{1,0},{2,1},{3,2},{4,3},{5,4},{6,5},{7,6},{8,7},{9,8},{10,9},{11,1... | collective-permute-start | bytes 442376 | tf_op jit(solution)/shard_map/ppermute | solution.py:144
  13.1 6.5 %collective-permute-start.1 = (bf16[6,96,128]{2,1,0:T(8,128)(2,1)S(1)}, bf16[6,96,128]{2,1,0:T(8,128)(2,1)S(1)}, u32[]{:S(2)}, u32[]{:S(2)}) collective-permute-start(bf16[6,96,128]{2,1,0:T(8,128)(2,1)S(1)} %get-tuple-element.7), channel_id=1, source_target_pairs={{0,1},{1,2},{2,3},{3,4},{4,5},{5,6},{6,7},{7,8},{8,9},{9,10},{10,1... | collective-permute-start | bytes 442376 | tf_op jit(solution)/shard_map/ppermute | solution.py:143

commit v2 on v1

--- a/solution.py
+++ b/solution.py
@@ -6,8 +6,8 @@
 from jax.sharding import Mesh, PartitionSpec as P
 
 TM = ("y_hi", "x", "core")
-ROWS = ("y_lo", "z")
-PLANE = ("y_hi", "x", "core", "y_lo")
+ROWS = ("y_lo", "z_pair", "z_in")
+PLANE = ("y_hi", "x", "core", "y_lo", "z_in")
 CH = 96
 W = 128
 F = 4
@@ -135,7 +135,7 @@
 
 def local(features, weights, cotangent):
     tm, rows = lax.axis_size(TM), lax.axis_size(ROWS)
-    plane, depth = lax.axis_size(PLANE), lax.axis_size("z")
+    plane, depth = lax.axis_size(PLANE), lax.axis_size("z_pair")
     cells = F * tm * H * rows * W
 
     next_frames = lax.ppermute(cotangent[:2], TM, [(i + 1, i) for i in range(tm - 1)])
@@ -173,7 +173,7 @@
     part = PACKED // plane
     parts = lax.all_to_all(packed.reshape(plane, part, W), PLANE, 0, 0)
     mine = jnp.sum(parts.astype(F32), axis=0).astype(BF16)
-    slabs = lax.all_to_all(spread(mine, depth), "z", 0, 0)
+    slabs = lax.all_to_all(spread(mine, depth), "z_pair", 0, 0)
     mine = jnp.sum(slabs.astype(F32), axis=0).astype(BF16)
     whole = lax.all_to_all(spread(mine, plane), PLANE, 0, 0).reshape(PACKED, W)
 
@@ -189,7 +189,7 @@
 
 
 def solution(mesh):
-    fine = Mesh(mesh.devices.reshape(2, 4, 2, 2, 16), ("y_hi", "x", "core", "y_lo", "z"))
+    fine = Mesh(mesh.devices.reshape(2, 4, 2, 2, 8, 2), ("y_hi", "x", "core", "y_lo", "z_pair", "z_in"))
     return jax.shard_map(
         local,
         mesh=fine,

time: 95.7 us -> 94.2 us (0.984)
  blocking collectives: 67.4 us -> 66 us
    all_to_all x1, blocking collectives: 21.2 us -> 18.4 us  [local(): whole = lax.all_to_all(spread(mine, plane), PLANE, 0, 0).reshape(PACKED, W)]
    all_to_all x1, blocking collectives: 28.7 us -> 31 us  [local(): parts = lax.all_to_all(packed.reshape(plane, part, W), PLANE, 0, 0)]
where the time goes in v2:
time: 94.2 us; the launch traced here: 93.9 us
  blocking collectives  66 us (70%)
  starting transfers between devices  14.2 us (15%)
  Pallas kernels  8.04 us (9%)
  local copies, waits for them, and re-layouts  2.39 us (3%)
  waiting for transfers between devices  2.38 us (3%)
    all_to_all x1, blocking collectives, local(): parts = lax.all_to_all(packed.reshape(plane, part, W), PLANE, 0, 0)  31 us
    all_to_all x1, blocking collectives, local(): whole = lax.all_to_all(spread(mine, plane), PLANE, 0, 0).reshape(PACKED, W)  18.4 us
    all_to_all x1, blocking collectives, local(): slabs = lax.all_to_all(spread(mine, depth), 'z_pair', 0, 0)  16.6 us
    ppermute x1, starting transfers between devices, local(): lax.ppermute(cotangent[:2], TM, [(i + 1, i) for i in range(tm - 1)])  8.92 us
    pallas_call x1, Pallas kernels, local(): pl.pallas_call(compute_kernel, out_shape=(jax.ShapeDtypeStruct((F, CH * H...  6.79 us
    ppermute x1, starting transfers between devices, local(): lax.ppermute(ext[:, :, H - 1, :], ROWS, [(i, i + 1) for i in range(rows -...  3.99 us
  transfers between devices with their start and end apart: 3, of which 2 were waited for; matrix products, arithmetic and copies ran while one was open for 1% of the time, Pallas kernels for 0%

profile of v2, /device:TPU:1, one launch (start us, length us, event | category | flops | bytes accessed | tf_op | source)
XLA Modules:
  0.0 93.9 jit_solution(11925274014068726399)
XLA Ops:
  0.6 1.0 %slice.12 = bf16[2,96,4,128]{3,2,1,0:T(4,128)(2,1)S(1)} slice(bf16[4,96,4,128]{3,2,1,0:T(4,128)(2,1)} %param.5), slice={[0:2], [0:96], [0:4], [0:128]} | slice | bytes 393216 | tf_op jit(solution)/shard_map/slice | solution.py:141
  1.6 0.0 copy-start
  1.6 0.0 copy-start.1
  1.7 0.0 copy-start.2
  1.7 8.9 %collective-permute-start = (bf16[2,96,4,128]{3,1,0,2:T(8,128)(2,1)S(1)}, bf16[2,96,4,128]{3,1,0,2:T(8,128)(2,1)S(1)}, u32[]{:S(2)}, u32[]{:S(2)}) collective-permute-start(bf16[2,96,4,128]{3,1,0,2:T(8,128)(2,1)S(1)} %copy.14), channel_id=1, source_target_pairs={{32,0},{64,32},{96,64},{128,96},{160,128},{192,160},{224,192},{256... | collective-permute-start | bytes 589832 | tf_op jit(solution)/shard_map/ppermute | solution.py:141
  10.6 1.1 %constant_dynamic-update-slice_fusion.1 = bf16[6,96,4,128]{3,1,0,2:T(8,128)(2,1)S(1)} fusion(bf16[4,96,4,128]{3,2,1,0:T(4,128)(2,1)} %param.5), kind=kLoop, calls=%fused_computation.3 | loop fusion | bytes 786432
  11.7 0.0 collective-permute-done
  11.8 1.3 %collective-permute-start.2 = (bf16[6,96,128]{2,1,0:T(8,128)(2,1)S(1)}, bf16[6,96,128]{2,1,0:T(8,128)(2,1)S(1)}, u32[]{:S(2)}, u32[]{:S(2)}) collective-permute-start(bf16[6,96,128]{2,1,0:T(8,128)(2,1)S(1)} %get-tuple-element.6), channel_id=1, source_target_pairs={{1,0},{2,1},{3,2},{4,3},{5,4},{6,5},{7,6},{8,7},{9,8},{10,9},{11,1... | collective-permute-start | bytes 442376 | tf_op jit(solution)/shard_map/ppermute | solution.py:144
  13.1 4.0 %collective-permute-start.1 = (bf16[6,96,128]{2,1,0:T(8,128)(2,1)S(1)}, bf16[6,96,128]{2,1,0:T(8,128)(2,1)S(1)}, u32[]{:S(2)}, u32[]{:S(2)}) collective-permute-start(bf16[6,96,128]{2,1,0:T(8,128)(2,1)S(1)} %get-tuple-element.7), channel_id=1, source_target_pairs={{0,1},{1,2},{2,3},{3,4},{4,5},{5,6},{6,7},{7,8},{8,9},{9,10},{10,1... | collective-permute-start | bytes 442376 | tf_op jit(solution)/shard_map/ppermute | solution.py:143
  17.1 0.2 copy.11
  17.2 1.5 %collective-permute-done.2.below = bf16[6,96,128]{2,1,0:T(8,128)(2,1)S(1)} collective-permute-done((bf16[6,96,128]{2,1,0:T(8,128)(2,1)S(1)}, bf16[6,96,128]{2,1,0:T(8,128)(2,1)S(1)}, u32[]{:S(2)}, u32[]{:S(2)}) %collective-permute-start.2) | collective-permute-done | bytes 147488 | tf_op jit(solution)/shard_map/ppermute | solution.py:144
  18.7 0.9 collective-permute-done.1.above
  19.6 0.0 copy-done
  19.6 0.0 copy-done.1
  19.6 0.0 copy-done.2
  19.6 6.8 %compute.1 = (bf16[4,384,128]{2,1,0:T(8,128)(2,1)}, bf16[2048,128]{1,0:T(8,128)(2,1)S(1)}) custom-call(bf16[4,384,128]{2,1,0:T(8,128)(2,1)S(1)} %bitcast.17, bf16[4,384,128]{2,1,0:T(8,128)(2,1)S(1)} %bitcast.12, bf16[2,384,128]{2,1,0:T(8,128)(2,1)S(1)} %bitcast.14, bf16[6,96,128]{2,1,0:T(8,128)(2,1)S(1)} %collective-permute-done.1.above, ...), custom_call_target="tpu_custom_call" | custom-call | tf_op jit(solution)/shard_map/compute/pallas_call | solution.py:146
  26.4 31.0 %all_to_all.15 = bf16[64,32,128]{2,1,0:T(8,128)(2,1)S(1)} all-to-all(bf16[64,32,128]{2,1,0:T(8,128)(2,1)S(1)} %bitcast.16), channel_id=1, replica_groups=mesh['y_hi'=2,'x'=4,'core'=2,'y_lo'=2,'z_pair'=8,'z_in'=2] {'y_hi','x','..., dimensions={0} | all-to-all | bytes 1048576 | tf_op jit(solution)/shard_map/all_to_all | solution.py:174
  57.4 0.1 reduce_sum.24
  57.5 16.6 %all_to_all.16 = bf16[8,32,128]{2,1,0:T(8,128)(2,1)S(1)} all-to-all(bf16[8,32,128]{2,1,0:T(8,128)(2,1)S(1)} %broadcast_in_dim.6), channel_id=1, replica_groups=mesh['y_hi'=2,'x'=4,'core'=2,'y_lo'=2,'z_pair'=8,'z_in'=2] {'z_pair'}, dimensions={0} | all-to-all | bytes 131072 | tf_op jit(solution)/shard_map/all_to_all | solution.py:176
  74.1 0.1 broadcast_in_dim.7
  74.2 18.4 %all_to_all.17 = bf16[64,32,128]{2,1,0:T(8,128)(2,1)S(1)} all-to-all(bf16[64,32,128]{2,1,0:T(8,128)(2,1)S(1)} %broadcast_in_dim.7), channel_id=1, replica_groups=mesh['y_hi'=2,'x'=4,'core'=2,'y_lo'=2,'z_pair'=8,'z_in'=2] {'y_hi','x','..., dimensions={0} | all-to-all | bytes 1048576 | tf_op jit(solution)/shard_map/all_to_all | solution.py:178
  92.7 1.2 %unpack.1 = f32[27,96,96]{2,1,0:T(8,128)} custom-call(bf16[2048,128]{1,0:T(8,128)(2,1)S(1)} %bitcast.13), custom_call_target="tpu_custom_call" | custom-call | tf_op jit(solution)/shard_map/unpack/pallas_call | solution.py:180
  (5 shorter events, 0.1 us)
Async XLA Ops:
  1.6 18.0 %copy-start = (bf16[4,96,4,128]{3,2,1,0:T(4,128)(2,1)S(1)}, bf16[4,96,4,128]{3,2,1,0:T(4,128)(2,1)}, u32[]{:S(2)}) copy-start(bf16[4,96,4,128]{3,2,1,0:T(4,128)(2,1)} %param.5) | copy-start | bytes 1179652
  1.6 18.0 %copy-start.1 = (bf16[3,3,3,96,96]{4,3,2,1,0:T(8,128)(2,1)S(1)}, bf16[3,3,3,96,96]{4,3,2,1,0:T(8,128)(2,1)}, u32[]{:S(2)}) copy-start(bf16[3,3,3,96,96]{4,3,2,1,0:T(8,128)(2,1)} %param.4) | copy-start | bytes 1492996
  1.7 18.0 %copy-start.2 = (bf16[4,96,4,128]{3,2,1,0:T(4,128)(2,1)S(1)}, bf16[4,96,4,128]{3,2,1,0:T(4,128)(2,1)}, u32[]{:S(2)}) copy-start(bf16[4,96,4,128]{3,2,1,0:T(4,128)(2,1)} %param.3) | copy-start | bytes 1179652
  1.7 10.0 %collective-permute-start = (bf16[2,96,4,128]{3,1,0,2:T(8,128)(2,1)S(1)}, bf16[2,96,4,128]{3,1,0,2:T(8,128)(2,1)S(1)}, u32[]{:S(2)}, u32[]{:S(2)}) collective-permute-start(bf16[2,96,4,128]{3,1,0,2:T(8,128)(2,1)S(1)} %copy.14), channel_id=1, source_target_pairs={{32,0},{64,32},{96,64},{128,96},{160,128},{192,160},{224,192},{256... | collective-permute-start | bytes 589832 | tf_op jit(solution)/shard_map/ppermute | solution.py:141
  11.8 7.0 %collective-permute-start.2 = (bf16[6,96,128]{2,1,0:T(8,128)(2,1)S(1)}, bf16[6,96,128]{2,1,0:T(8,128)(2,1)S(1)}, u32[]{:S(2)}, u32[]{:S(2)}) collective-permute-start(bf16[6,96,128]{2,1,0:T(8,128)(2,1)S(1)} %get-tuple-element.6), channel_id=1, source_target_pairs={{1,0},{2,1},{3,2},{4,3},{5,4},{6,5},{7,6},{8,7},{9,8},{10,9},{11,1... | collective-permute-start | bytes 442376 | tf_op jit(solution)/shard_map/ppermute | solution.py:144
  13.1 6.5 %collective-permute-start.1 = (bf16[6,96,128]{2,1,0:T(8,128)(2,1)S(1)}, bf16[6,96,128]{2,1,0:T(8,128)(2,1)S(1)}, u32[]{:S(2)}, u32[]{:S(2)}) collective-permute-start(bf16[6,96,128]{2,1,0:T(8,128)(2,1)S(1)} %get-tuple-element.7), channel_id=1, source_target_pairs={{0,1},{1,2},{2,3},{3,4},{4,5},{5,6},{6,7},{7,8},{8,9},{9,10},{10,1... | collective-permute-start | bytes 442376 | tf_op jit(solution)/shard_map/ppermute | solution.py:143

commit v3 on v2

v3 whole, which is shorter than its diff:
```python
import jax
import jax.numpy as jnp
from jax import lax
from jax.experimental import pallas as pl
from jax.experimental.pallas import tpu as pltpu
from jax.sharding import Mesh, PartitionSpec as P

TM = ("y_hi", "x", "core")
ROWS = ("y_lo", "z_pair", "z_in")
PLANE = ("y_hi", "x", "core", "y_lo", "z_in")
CH = 96
W = 128
F = 4
H = 4
FW = F * W
NEXT = 2 * W
TAP = 3 * CH
PACKED = 2048
F32 = jnp.float32
BF16 = jnp.bfloat16


def dot(a, b, contract):
    return lax.dot_general(a, b, (contract, ((), ())), preferred_element_type=F32)


def row_major():
    parts = []
    for h in range(H):
        pair = lax.broadcasted_iota(jnp.int32, (CH, H * CH), 1)
        channel = lax.broadcasted_iota(jnp.int32, (CH, H * CH), 0)
        parts.append(jnp.where(pair == channel * H + h, 1.0, 0.0).astype(BF16))
    return jnp.concatenate(parts, axis=0)


def frames(ref, count):
    return jnp.concatenate([ref[f] for f in range(count)], axis=1)


def shifted(value, step):
    lane = lax.broadcasted_iota(jnp.int32, (CH, W), 1)
    parts = []
    for f in range(value.shape[1] // W):
        part = pltpu.roll(value[:, f * W : (f + 1) * W], (-step) % W, 1)
        parts.append(jnp.where(lane == (W - 1 if step > 0 else 0), 0.0, part))
    return jnp.concatenate(parts, axis=1)


def own_kernel(feat, cot, weights, own, act, normed, slope, scale, by_out):
    order = row_major()
    own[...] = dot(order, frames(cot, F), ((1,), (0,))).astype(BF16)
    values = dot(order, frames(feat, F), ((1,), (0,)))
    for h in range(H):
        x = values[h * CH : (h + 1) * CH]
        s = lax.rsqrt(jnp.sum(x * x, axis=0, keepdims=True) * (1.0 / CH) + 1e-06)
        n = x * s
        sigma = 1.0 / (1.0 + jnp.exp(-n))
        a = (n * sigma).astype(BF16).astype(F32)
        act[h, :CH] = shifted(a, -1).astype(BF16)
        act[h, CH : 2 * CH] = a.astype(BF16)
        act[h, 2 * CH :] = shifted(a, 1).astype(BF16)
        normed[h] = n
        slope[h] = sigma * (1.0 + n * (1.0 - sigma))
        scale[h] = s
    stacked = [
        jnp.concatenate([weights[t * 9 + (2 - k) * 3 + c].astype(F32) for c in range(3)], axis=1)
        for t in range(3)
        for k in range(3)
    ]
    by_out[...] = jnp.concatenate(stacked, axis=0).T.astype(BF16)


def next_kernel(cot, own, after, bottom, top):
    after[...] = dot(row_major(), frames(cot, 2), ((1,), (0,))).astype(BF16)
    for h, out in ((H - 1, bottom), (0, top)):
        out[:, :FW] = own[h * CH : (h + 1) * CH, :]
        out[:, FW:] = after[h * CH : (h + 1) * CH, :]


def row_gradients(h, mine, later, act, normed, slope, scale, by_out):
    windows = [
        jnp.concatenate([mine[:, (2 - t) * W :], later[:, : (2 - t) * W]], axis=1) if t < 2 else mine for t in range(3)
    ]
    terms = [dot(windows[t], act[h], ((1,), (1,))) for t in range(3)]
    products = dot(by_out[...], jnp.concatenate(windows, axis=0), ((1,), (0,)))
    grad = products[CH : 2 * CH] + shifted(products[:CH], 1) + shifted(products[2 * CH :], -1)
    n = normed[h]
    grad = grad * slope[h]
    inner = jnp.sum(grad * n, axis=0, keepdims=True) * (1.0 / CH)
    result = scale[h] * (grad - n * inner) + mine[CH : 2 * CH].astype(F32)
    return terms, result.astype(BF16)


def inner_kernel(own, after, act, normed, slope, scale, by_out, wsum, result):
    total = None
    for h in (1, 2):
        rows = slice((h - 1) * CH, (h + 2) * CH)
        terms, result[h - 1] = row_gradients(h, own[rows], after[rows], act, normed, slope, scale, by_out)
        total = terms if total is None else [a + b for a, b in zip(total, terms)]
    for t in range(3):
        wsum[t] = total[t]


def edge_kernel(above, below, own, after, act, normed, slope, scale, by_out, wsum, result, grad_out, packed):
    args = (act, normed, slope, scale, by_out)
    mine = jnp.concatenate([above[:, :FW], own[: 2 * CH]], axis=0)
    later = jnp.concatenate([above[:, FW:], after[: 2 * CH]], axis=0)
    first, first_row = row_gradients(0, mine, later, *args)
    mine = jnp.concatenate([own[2 * CH :], below[:, :FW]], axis=0)
    later = jnp.concatenate([after[2 * CH :], below[:, FW:]], axis=0)
    last, last_row = row_gradients(H - 1, mine, later, *args)

    rests = []
    for t in range(3):
        total = wsum[t] + first[t] + last[t]
        for j in range(2):
            packed[(2 * t + j) * TAP : (2 * t + j + 1) * TAP, :] = total[:, j * W : (j + 1) * W].astype(BF16)
        rests.append(total[:, 2 * W :])
    rests.append(jnp.zeros((TAP, W - CH), F32))
    packed[6 * TAP : 7 * TAP, :] = jnp.concatenate(rests, axis=1).astype(BF16)
    packed[7 * TAP :, :] = jnp.zeros((PACKED - 7 * TAP, W), BF16)

    rows = jnp.concatenate([first_row, result[0], result[1], last_row], axis=0)
    placed = dot(row_major().astype(F32).T.astype(BF16), rows, ((1,), (0,)))
    for f in range(F):
        grad_out[f] = placed[:, f * W : (f + 1) * W].astype(BF16)


def unpack_kernel(norm_factor, packed, out):
    rests = packed[6 * TAP : 7 * TAP, :].astype(F32)
    width = TAP - 2 * W
    for t in range(3):
        tiles = [packed[(2 * t + j) * TAP : (2 * t + j + 1) * TAP, :].astype(F32) for j in range(2)]
        block = jnp.concatenate(tiles + [rests[:, t * width : (t + 1) * width]], axis=1) * norm_factor
        for c in range(3):
            column = block[:, c * CH : (c + 1) * CH]
            for k in range(3):
                out[t * 9 + (2 - k) * 3 + c] = column[k * CH : (k + 1) * CH]


def call(kernel, name, outs, args, flops=0):
    place = pl.BlockSpec(memory_space=pltpu.VMEM)
    return pl.pallas_call(
        kernel,
        out_shape=tuple(jax.ShapeDtypeStruct(shape, dtype) for shape, dtype in outs),
        in_specs=[place] * len(args),
        out_specs=(place,) * len(outs),
        compiler_params=pltpu.CompilerParams(vmem_limit_bytes=32 << 20),
        cost_estimate=pl.CostEstimate(flops=flops, bytes_accessed=4 << 20, transcendentals=0),
        name=name,
    )(*args)


def spread(value, count):
    return jnp.broadcast_to(value, (count,) + value.shape)


def local(features, weights, cotangent):
    tm, rows = lax.axis_size(TM), lax.axis_size(ROWS)
    plane, depth = lax.axis_size(PLANE), lax.axis_size("z_pair")
    cells = F * tm * H * rows * W
    features = features.reshape(F, CH * H, W)
    cotangent = cotangent.reshape(F, CH * H, W)

    next_frames = lax.ppermute(cotangent[:2], TM, [(i + 1, i) for i in range(tm - 1)])
    own, *local_values = call(
        own_kernel,
        "own",
        [
            ((H * CH, FW), BF16),
            ((H, TAP, FW), BF16),
            ((H, CH, FW), F32),
            ((H, CH, FW), F32),
            ((H, 1, FW), F32),
            ((TAP, 3 * TAP), BF16),
        ],
        (features, cotangent, weights.reshape(27, CH, CH)),
        1 << 31,
    )
    after, bottom, top = call(
        next_kernel,
        "next_frames",
        [((H * CH, NEXT), BF16), ((CH, FW + NEXT), BF16), ((CH, FW + NEXT), BF16)],
        (next_frames, own),
    )
    above = lax.ppermute(bottom, ROWS, [(i, i + 1) for i in range(rows - 1)])
    below = lax.ppermute(top, ROWS, [(i + 1, i) for i in range(rows - 1)])
    wsum, result = call(
        inner_kernel,
        "inner_rows",
        [((3, TAP, TAP), F32), ((2, CH, FW), BF16)],
        (own, after, *local_values),
        1 << 31,
    )
    input_grad, packed = call(
        edge_kernel,
        "edge_rows",
        [((F, CH * H, W), BF16), ((PACKED, W), BF16)],
        (above, below, own, after, *local_values, wsum, result),
        1 << 31,
    )

    part = PACKED // plane
    parts = lax.all_to_all(packed.reshape(plane, part, W), PLANE, 0, 0)
    mine = jnp.sum(parts.astype(F32), axis=0).astype(BF16)
    slabs = lax.all_to_all(spread(mine, depth), "z_pair", 0, 0)
    mine = jnp.sum(slabs.astype(F32), axis=0).astype(BF16)
    whole = lax.all_to_all(spread(mine, plane), PLANE, 0, 0).reshape(PACKED, W)

    (weight_grad,) = call(
        lambda *refs: unpack_kernel(1.0 / float(cells) ** 0.5, *refs),
        "unpack",
        [((27, CH, CH), F32)],
        (whole,),
    )
    return (input_grad.reshape(F, CH, H, W), weight_grad.reshape(3, 3, 3, CH, CH))


def solution(mesh):
    fine = Mesh(
        mesh.devices.reshape(2, 4, 2, 2, 8, 2), ("y_hi", "x", "core", "y_lo", "z_pair", "z_in")
    )
    return jax.shard_map(
        local,
        mesh=fine,
        in_specs=(P(TM, None, ROWS, None), P(), P(TM, None, ROWS, None)),
        out_specs=(P(TM, None, ROWS, None), P()),
        check_vma=False,
    )
```

time: 94.2 us -> 91.5 us (0.971)
  blocking collectives: 66 us -> 62.7 us
  starting transfers between devices: 14.2 us -> 11.4 us
  waiting for transfers between devices: 2.38 us -> 4.44 us
  local copies, waits for them, and re-layouts: 2.39 us -> 4.16 us
    all_to_all x1, blocking collectives: 31 us -> 23.1 us  [local(): parts = lax.all_to_all(packed.reshape(plane, part, W), PLANE, 0, 0)]
    all_to_all x1, blocking collectives: 16.6 us -> 21.1 us  [local(): slabs = lax.all_to_all(spread(mine, depth), 'z_pair', 0, 0)]
    ppermute x2, starting transfers between devices: 5.29 us -> 2.59 us  [the longest x1 1.3 us: local(): above = lax.ppermute(bottom, ROWS, [(i, i + 1) for i in range(rows - 1)])]
    ppermute x2, waiting for transfers between devices: 2.38 us -> 4.43 us  [the longest x1 4.24 us: local(): below = lax.ppermute(top, ROWS, [(i + 1, i) for i in range(rows - 1)])]
    unnamed x8 -> x6, local copies, waits for them, and re-layouts: 1.1 us -> 3.08 us
    pallas_call x2 -> x5, Pallas kernels: 8.04 us -> 7.64 us  [call(): pl.pallas_call(kernel, out_shape=tuple((jax.ShapeDtypeStruct(shape, dtype...]
  transfers between devices with their start and end apart: 3 -> 3, of which waited for: 2 -> 2; matrix products, arithmetic and copies ran while one was open for 1% -> 0% of each run, Pallas kernels for 0% -> 3%
where the time goes in v3:
time: 91.5 us; the launch traced here: 91.1 us
  blocking collectives  62.7 us (69%)
  starting transfers between devices  11.4 us (12%)
  Pallas kernels  7.64 us (8%)
  waiting for transfers between devices  4.44 us (5%)
  local copies, waits for them, and re-layouts  4.16 us (5%)
    all_to_all x1, blocking collectives, local(): parts = lax.all_to_all(packed.reshape(plane, part, W), PLANE, 0, 0)  23.1 us
    all_to_all x1, blocking collectives, local(): slabs = lax.all_to_all(spread(mine, depth), 'z_pair', 0, 0)  21.1 us
    all_to_all x1, blocking collectives, local(): whole = lax.all_to_all(spread(mine, plane), PLANE, 0, 0).reshape(PACKED, W)  18.4 us
    ppermute x1, starting transfers between devices, local(): lax.ppermute(cotangent[:2], TM, [(i + 1, i) for i in range(tm - 1)])  8.79 us
    pallas_call x5, Pallas kernels, call(): pl.pallas_call(kernel, out_shape=tuple((jax.ShapeDtypeStruct(shape, dtype...  7.64 us
    ppermute x1, waiting for transfers between devices, local(): below = lax.ppermute(top, ROWS, [(i + 1, i) for i in range(rows - 1)])  4.24 us
    unnamed x6, local copies, waits for them, and re-layouts  3.08 us
  transfers between devices with their start and end apart: 3, of which 2 were waited for; matrix products, arithmetic and copies ran while one was open for 0% of the time, Pallas kernels for 3%

profile of v3, /device:TPU:1, one launch (start us, length us, event | category | flops | bytes accessed | tf_op | source)
XLA Modules:
  0.0 91.1 jit_solution(4034695838819694935)
XLA Ops:
  0.6 1.0 %slice.6 = bf16[2,96,4,128]{3,2,1,0:T(4,128)(2,1)S(1)} slice(bf16[4,96,4,128]{3,2,1,0:T(4,128)(2,1)} %param.5), slice={[0:2], [0:96], [0:4], [0:128]} | slice | bytes 393216 | tf_op jit(solution)/shard_map/slice | solution.py:165
  1.6 8.8 %collective-permute-start = (bf16[2,384,128]{2,1,0:T(8,128)(2,1)S(1)}, bf16[2,384,128]{2,1,0:T(8,128)(2,1)S(1)}, u32[]{:S(2)}, u32[]{:S(2)}) collective-permute-start(bf16[2,384,128]{2,1,0:T(8,128)(2,1)S(1)} %bitcast.14), channel_id=1, source_target_pairs={{32,0},{64,32},{96,64},{128,96},{160,128},{192,160},{224,192},{256... | collective-permute-start | bytes 589832 | tf_op jit(solution)/shard_map/ppermute | solution.py:165
  10.4 0.0 copy-start
  10.4 1.0 %copy-done = bf16[4,96,4,128]{3,2,1,0:T(4,128)(2,1)S(1)} copy-done((bf16[4,96,4,128]{3,2,1,0:T(4,128)(2,1)S(1)}, bf16[4,96,4,128]{3,2,1,0:T(4,128)(2,1)}, u32[]{:S(2)}) %copy-start) | copy-done | bytes 393240
  11.4 0.0 copy-start.1
  11.4 1.1 %copy-done.1 = bf16[3,3,3,96,96]{4,3,2,1,0:T(8,128)(2,1)S(1)} copy-done((bf16[3,3,3,96,96]{4,3,2,1,0:T(8,128)(2,1)S(1)}, bf16[3,3,3,96,96]{4,3,2,1,0:T(8,128)(2,1)}, u32[]{:S(2)}) %copy-start.1) | copy-done | bytes 497688
  12.5 0.0 copy-start.2
  12.5 1.0 %copy-done.2 = bf16[4,96,4,128]{3,2,1,0:T(4,128)(2,1)S(1)} copy-done((bf16[4,96,4,128]{3,2,1,0:T(4,128)(2,1)S(1)}, bf16[4,96,4,128]{3,2,1,0:T(4,128)(2,1)}, u32[]{:S(2)}) %copy-start.2) | copy-done | bytes 393240
  13.5 1.2 %own.1 = (bf16[384,512]{1,0:T(8,128)(2,1)S(1)}, bf16[4,288,512]{2,1,0:T(8,128)(2,1)S(1)}, f32[4,96,512]{2,1,0:T(8,128)S(1)}, f32[4,96,512]{2,1,0:T(8,128)S(1)}, ...) custom-call(bf16[4,384,128]{2,1,0:T(8,128)(2,1)S(1)} %bitcast.12, bf16[4,384,128]{2,1,0:T(8,128)(2,1)S(1)} %bitcast.10, ...), custom_call_target="tpu_custom_call" | custom-call | flops 2147483648 | bytes 4194304 | tf_op jit(solution)/shard_map/own/pallas_call | solution.py:143
  14.7 0.0 collective-permute-done.cot
  14.7 0.3 next_frames.1
  15.0 1.3 %collective-permute-start.1 = (bf16[96,768]{1,0:T(8,128)(2,1)S(1)}, bf16[96,768]{1,0:T(8,128)(2,1)S(1)}, u32[]{:S(2)}, u32[]{:S(2)}) collective-permute-start(bf16[96,768]{1,0:T(8,128)(2,1)S(1)} %get-tuple-element.16), channel_id=1, source_target_pairs={{0,1},{1,2},{2,3},{3,4},{4,5},{5,6},{6,7},{7,8},{8,9},{9,10},{10,1... | collective-permute-start | bytes 442376 | tf_op jit(solution)/shard_map/ppermute | solution.py:186
  16.3 1.3 %collective-permute-start.2 = (bf16[96,768]{1,0:T(8,128)(2,1)S(1)}, bf16[96,768]{1,0:T(8,128)(2,1)S(1)}, u32[]{:S(2)}, u32[]{:S(2)}) collective-permute-start(bf16[96,768]{1,0:T(8,128)(2,1)S(1)} %get-tuple-element.17), channel_id=1, source_target_pairs={{1,0},{2,1},{3,2},{4,3},{5,4},{6,5},{7,6},{8,7},{9,8},{10,9},{11,1... | collective-permute-start | bytes 442376 | tf_op jit(solution)/shard_map/ppermute | solution.py:187
  17.6 1.7 %inner_rows.1 = (f32[3,288,288]{2,1,0:T(8,128)S(1)}, bf16[2,96,512]{2,1,0:T(8,128)(2,1)S(1)}) custom-call(bf16[384,512]{1,0:T(8,128)(2,1)S(1)} %get-tuple-element.15.own, bf16[384,256]{1,0:T(8,128)(2,1)S(1)} %get-tuple-element.18.after, bf16[4,288,512]{2,1,0:T(8,128)(2,1)S(1)} %get-tuple-element.19.act, f32[4,96,512]{2,1,0:T(8,128)S(1)} %get-tuple-element.20.normed, ...), custom_call_target="tpu_custom_call" | custom-call | flops 2147483648 | bytes 4194304 | tf_op jit(solution)/shard_map/inner_rows/pallas_call | solution.py:143
  19.3 0.2 collective-permute-done.1.above
  19.5 4.2 %collective-permute-done.2.below = bf16[96,768]{1,0:T(8,128)(2,1)S(1)} collective-permute-done((bf16[96,768]{1,0:T(8,128)(2,1)S(1)}, bf16[96,768]{1,0:T(8,128)(2,1)S(1)}, u32[]{:S(2)}, u32[]{:S(2)}) %collective-permute-start.2) | collective-permute-done | bytes 147488 | tf_op jit(solution)/shard_map/ppermute | solution.py:187
  23.7 2.9 %edge_rows.1 = (bf16[4,384,128]{2,1,0:T(8,128)(2,1)}, bf16[2048,128]{1,0:T(8,128)(2,1)S(1)}) custom-call(bf16[96,768]{1,0:T(8,128)(2,1)S(1)} %collective-permute-done.1.above, bf16[96,768]{1,0:T(8,128)(2,1)S(1)} %collective-permute-done.2.below, bf16[384,512]{1,0:T(8,128)(2,1)S(1)} %get-tuple-element.15.own, bf16[384,256]{1,0:T(8,128)(2,1)S(1)} %get-tuple-element.18.after, ...), custom_call_target="tpu_custom_call" | custom-call | flops 2147483648 | bytes 4194304 | tf_op jit(solution)/shard_map/edge_rows/pallas_call | solution.py:143
  26.6 23.1 %all_to_all.15 = bf16[64,32,128]{2,1,0:T(8,128)(2,1)S(1)} all-to-all(bf16[64,32,128]{2,1,0:T(8,128)(2,1)S(1)} %bitcast.9), channel_id=1, replica_groups=mesh['y_hi'=2,'x'=4,'core'=2,'y_lo'=2,'z_pair'=8,'z_in'=2] {'y_hi','x','..., dimensions={0} | all-to-all | bytes 1048576 | tf_op jit(solution)/shard_map/all_to_all | solution.py:204
  49.7 0.1 reduce_sum.24
  49.8 21.1 %all_to_all.16 = bf16[8,32,128]{2,1,0:T(8,128)(2,1)S(1)} all-to-all(bf16[8,32,128]{2,1,0:T(8,128)(2,1)S(1)} %broadcast_in_dim.6), channel_id=1, replica_groups=mesh['y_hi'=2,'x'=4,'core'=2,'y_lo'=2,'z_pair'=8,'z_in'=2] {'z_pair'}, dimensions={0} | all-to-all | bytes 131072 | tf_op jit(solution)/shard_map/all_to_all | solution.py:206
  70.9 0.1 broadcast_in_dim.7
  71.0 18.4 %all_to_all.17 = bf16[64,32,128]{2,1,0:T(8,128)(2,1)S(1)} all-to-all(bf16[64,32,128]{2,1,0:T(8,128)(2,1)S(1)} %broadcast_in_dim.7), channel_id=1, replica_groups=mesh['y_hi'=2,'x'=4,'core'=2,'y_lo'=2,'z_pair'=8,'z_in'=2] {'y_hi','x','..., dimensions={0} | all-to-all | bytes 1048576 | tf_op jit(solution)/shard_map/all_to_all | solution.py:208
  89.4 1.6 %unpack.1 = f32[27,96,96]{2,1,0:T(8,128)} custom-call(bf16[2048,128]{1,0:T(8,128)(2,1)S(1)} %bitcast.8), custom_call_target="tpu_custom_call" | custom-call | bytes 4194304 | tf_op jit(solution)/shard_map/unpack/pallas_call | solution.py:143
  (2 shorter events, 0.0 us)
Async XLA Ops:
  1.6 13.1 %collective-permute-start = (bf16[2,384,128]{2,1,0:T(8,128)(2,1)S(1)}, bf16[2,384,128]{2,1,0:T(8,128)(2,1)S(1)}, u32[]{:S(2)}, u32[]{:S(2)}) collective-permute-start(bf16[2,384,128]{2,1,0:T(8,128)(2,1)S(1)} %bitcast.14), channel_id=1, source_target_pairs={{32,0},{64,32},{96,64},{128,96},{160,128},{192,160},{224,192},{256... | collective-permute-start | bytes 589832 | tf_op jit(solution)/shard_map/ppermute | solution.py:165
  10.4 1.0 %copy-start = (bf16[4,96,4,128]{3,2,1,0:T(4,128)(2,1)S(1)}, bf16[4,96,4,128]{3,2,1,0:T(4,128)(2,1)}, u32[]{:S(2)}) copy-start(bf16[4,96,4,128]{3,2,1,0:T(4,128)(2,1)} %param.5) | copy-start | bytes 1179652
  11.4 1.1 %copy-start.1 = (bf16[3,3,3,96,96]{4,3,2,1,0:T(8,128)(2,1)S(1)}, bf16[3,3,3,96,96]{4,3,2,1,0:T(8,128)(2,1)}, u32[]{:S(2)}) copy-start(bf16[3,3,3,96,96]{4,3,2,1,0:T(8,128)(2,1)} %param.4) | copy-start | bytes 1492996
  12.5 1.0 %copy-start.2 = (bf16[4,96,4,128]{3,2,1,0:T(4,128)(2,1)S(1)}, bf16[4,96,4,128]{3,2,1,0:T(4,128)(2,1)}, u32[]{:S(2)}) copy-start(bf16[4,96,4,128]{3,2,1,0:T(4,128)(2,1)} %param.3) | copy-start | bytes 1179652
  15.0 4.5 %collective-permute-start.1 = (bf16[96,768]{1,0:T(8,128)(2,1)S(1)}, bf16[96,768]{1,0:T(8,128)(2,1)S(1)}, u32[]{:S(2)}, u32[]{:S(2)}) collective-permute-start(bf16[96,768]{1,0:T(8,128)(2,1)S(1)} %get-tuple-element.16), channel_id=1, source_target_pairs={{0,1},{1,2},{2,3},{3,4},{4,5},{5,6},{6,7},{7,8},{8,9},{9,10},{10,1... | collective-permute-start | bytes 442376 | tf_op jit(solution)/shard_map/ppermute | solution.py:186
  16.3 7.4 %collective-permute-start.2 = (bf16[96,768]{1,0:T(8,128)(2,1)S(1)}, bf16[96,768]{1,0:T(8,128)(2,1)S(1)}, u32[]{:S(2)}, u32[]{:S(2)}) collective-permute-start(bf16[96,768]{1,0:T(8,128)(2,1)S(1)} %get-tuple-element.17), channel_id=1, source_target_pairs={{1,0},{2,1},{3,2},{4,3},{5,4},{6,5},{7,6},{8,7},{9,8},{10,9},{11,1... | collective-permute-start | bytes 442376 | tf_op jit(solution)/shard_map/ppermute | solution.py:187

commit v4 on v3

v4 whole, which is shorter than its diff:
```python
import jax
import jax.numpy as jnp
from jax import lax
from jax.experimental import pallas as pl
from jax.experimental.pallas import tpu as pltpu
from jax.sharding import Mesh, PartitionSpec as P

TM = ("y_hi", "x", "core")
ROWS = ("y_lo", "z_pair", "z_in")
PLANE = ("y_hi", "x", "core", "y_lo", "z_in")
CH = 96
W = 128
F = 4
H = 4
FW = F * W
NEXT = 2 * W
TAP = 3 * CH
PACKED = 2048
F32 = jnp.float32
BF16 = jnp.bfloat16


def dot(a, b, contract):
    return lax.dot_general(a, b, (contract, ((), ())), preferred_element_type=F32)


def row_major():
    parts = []
    for h in range(H):
        pair = lax.broadcasted_iota(jnp.int32, (CH, H * CH), 1)
        channel = lax.broadcasted_iota(jnp.int32, (CH, H * CH), 0)
        parts.append(jnp.where(pair == channel * H + h, 1.0, 0.0).astype(BF16))
    return jnp.concatenate(parts, axis=0)


def frames(ref, count):
    return jnp.concatenate([ref[f] for f in range(count)], axis=1)


def shifted(value, step):
    lane = lax.broadcasted_iota(jnp.int32, (CH, W), 1)
    parts = []
    for f in range(value.shape[1] // W):
        part = pltpu.roll(value[:, f * W : (f + 1) * W], (-step) % W, 1)
        parts.append(jnp.where(lane == (W - 1 if step > 0 else 0), 0.0, part))
    return jnp.concatenate(parts, axis=1)


def column_taps(active):
    wide = active.astype(F32)
    return jnp.concatenate([shifted(wide, -1).astype(BF16), active, shifted(wide, 1).astype(BF16)], axis=0)


def rows_of(ref, first, count):
    return ref[first * CH : (first + count) * CH, :]


def normalize(x):
    scale = lax.rsqrt(jnp.sum(x * x, axis=0, keepdims=True) * (1.0 / CH) + 1e-06)
    return x * scale, scale


def sigmoid(x):
    return 1.0 / (1.0 + jnp.exp(-x))


def load_kernel(feat_in, cot_in, feat, cot, sems):
    copies = [
        pltpu.make_async_copy(cot_in, cot, sems.at[0]),
        pltpu.make_async_copy(feat_in, feat, sems.at[1]),
    ]
    for copy in copies:
        copy.start()
    for copy in copies:
        copy.wait()


def cot_kernel(cot, own, bottom, top):
    rows = dot(row_major(), frames(cot, F), ((1,), (0,))).astype(BF16)
    own[...] = rows
    top[...] = rows[:CH]
    bottom[...] = rows[(H - 1) * CH :]


def active_kernel(feat, act, normed, scale):
    values = dot(row_major(), frames(feat, F), ((1,), (0,)))
    for h in range(H):
        n, scale[h] = normalize(values[h * CH : (h + 1) * CH])
        normed[h] = n
        act[h] = column_taps((n * sigmoid(n)).astype(BF16))


def inner_kernel(own, act, wsum):
    def terms(first, count, h):
        rows = rows_of(own, first, count)
        return [dot(rows[:, (2 - t) * W :], act[h, :, : (t + 2) * W], ((1,), (1,))) for t in range(3)]

    second, third = terms(0, 3, 1), terms(1, 3, 2)
    first, last = terms(0, 2, 0), terms(2, 2, 3)
    for t in range(3):
        both = second[t] + third[t]
        wsum[t, :CH] = both[:CH] + last[t][:CH]
        wsum[t, CH : 2 * CH] = both[CH : 2 * CH] + first[t][:CH] + last[t][CH:]
        wsum[t, 2 * CH :] = both[2 * CH :] + first[t][CH:]


def past_kernel(before, own, inner_sum, wsum, past_act):
    values = dot(row_major(), frames(before, 2), ((1,), (0,)))
    sums = [inner_sum[t] for t in range(2)]
    zeros = jnp.zeros((CH, TAP), F32)
    for h in range(H):
        n, _ = normalize(values[h * CH : (h + 1) * CH])
        past = column_taps((n * sigmoid(n)).astype(BF16))
        if h in (0, H - 1):
            past_act[h // (H - 1)] = past
        rows = rows_of(own, max(h - 1, 0), 3 - (h in (0, H - 1)))
        for t in range(2):
            term = dot(rows[:, : (2 - t) * W], past[:, t * W :], ((1,), (1,)))
            term = jnp.concatenate([zeros] * (h == 0) + [term] + [zeros] * (h == H - 1), axis=0)
            sums[t] = sums[t] + term
    for t in range(2):
        wsum[t] = sums[t]
    wsum[2] = inner_sum[2]


def edge_kernel(above, below, own, act, past_act, wsum, packed, first_frames):
    upper, lower = above[...], below[...]
    first = jnp.concatenate([past_act[0], act[0]], axis=1)
    last = jnp.concatenate([past_act[1], act[H - 1]], axis=1)
    sums = []
    for t in range(3):
        from_above = dot(upper, first[:, t * W : t * W + FW], ((1,), (1,)))
        from_below = dot(lower, last[:, t * W : t * W + FW], ((1,), (1,)))
        sums.append(
            jnp.concatenate([wsum[t, :CH] + from_above, wsum[t, CH : 2 * CH], wsum[t, 2 * CH :] + from_below], axis=0)
        )
    first_frames[:CH, :] = upper[:, :NEXT]
    first_frames[CH : 5 * CH, :] = own[:, :NEXT]
    first_frames[5 * CH :, :] = lower[:, :NEXT]
    for t in range(3):
        for j in range(2):
            packed[(2 * t + j) * TAP : (2 * t + j + 1) * TAP, :] = sums[t][:, j * W : (j + 1) * W].astype(BF16)
    rests = [total[:, 2 * W :] for total in sums] + [jnp.zeros((TAP, W - CH), F32)]
    packed[6 * TAP : 7 * TAP, :] = jnp.concatenate(rests, axis=1).astype(BF16)
    packed[7 * TAP :, :] = jnp.zeros((PACKED - 7 * TAP, W), BF16)


def input_kernel(above, below, own, later, normed, scale, weights, grad_out, done):
    stacked = [
        jnp.concatenate([weights[t * 9 + (2 - k) * 3 + c].astype(F32) for c in range(3)], axis=1)
        for t in range(3)
        for k in range(3)
    ]
    by_out = jnp.concatenate(stacked, axis=0).T.astype(BF16)
    rows = jnp.concatenate([above[...], own[...], below[...]], axis=0)
    results = []
    for h in range(H):
        mine, ahead = rows[h * CH : (h + 3) * CH], rows_of(later, h, 3)
        windows = [
            jnp.concatenate([mine[:, (2 - t) * W :], ahead[:, : (2 - t) * W]], axis=1) if t < 2 else mine
            for t in range(3)
        ]
        products = dot(by_out, jnp.concatenate(windows, axis=0), ((1,), (0,)))
        grad = products[CH : 2 * CH] + shifted(products[:CH], 1) + shifted(products[2 * CH :], -1)
        n = normed[h]
        sigma = sigmoid(n)
        grad = grad * sigma * (1.0 + n * (1.0 - sigma))
        inner = jnp.sum(grad * n, axis=0, keepdims=True) * (1.0 / CH)
        result = scale[h] * (grad - n * inner) + mine[CH : 2 * CH].astype(F32)
        results.append(result.astype(BF16))
    placed = dot(row_major().astype(F32).T.astype(BF16), jnp.concatenate(results, axis=0), ((1,), (0,)))
    for f in range(F):
        grad_out[f] = placed[:, f * W : (f + 1) * W].astype(BF16)
    done[...] = jnp.zeros(done.shape, F32)


def sum_kernel(parts, *refs):
    out = refs[-1]
    total = parts[0].astype(F32)
    for i in range(1, parts.shape[0]):
        total = total + parts[i].astype(F32)
    total = total.astype(BF16)
    for i in range(out.shape[0]):
        out[i] = total


def unpack_kernel(norm_factor, packed, out, held, sems):
    rests = packed[6 * TAP : 7 * TAP, :].astype(F32)
    width = TAP - 2 * W
    copies = []
    for t in range(3):
        tiles = [packed[(2 * t + j) * TAP : (2 * t + j + 1) * TAP, :].astype(F32) for j in range(2)]
        block = jnp.concatenate(tiles + [rests[:, t * width : (t + 1) * width]], axis=1) * norm_factor
        for c in range(3):
            column = block[:, c * CH : (c + 1) * CH]
            for k in range(3):
                held[t, (2 - k) * 3 + c] = column[k * CH : (k + 1) * CH]
        copies.append(pltpu.make_async_copy(held.at[t], out.at[pl.ds(t * 9, 9)], sems.at[t]))
        copies[-1].start()
    for copy in copies:
        copy.wait()


def call(kernel, name, outs, args, flops=0, after=(), out_hbm=False, scratch=()):
    vmem, anywhere = pl.BlockSpec(memory_space=pltpu.VMEM), pl.BlockSpec(memory_space=pl.ANY)
    return pl.pallas_call(
        kernel,
        out_shape=tuple(jax.ShapeDtypeStruct(shape, dtype) for shape, dtype in outs),
        in_specs=[vmem] * len(args) + [anywhere] * len(after),
        out_specs=(anywhere if out_hbm else vmem,) * len(outs),
        scratch_shapes=scratch,
        compiler_params=pltpu.CompilerParams(vmem_limit_bytes=16 << 20),
        cost_estimate=pl.CostEstimate(flops=flops, bytes_accessed=4 << 20, transcendentals=0),
        name=name,
    )(*args, *after)


def sum_to_slots(parts, count, name, after=()):
    return call(sum_kernel, name, [((count,) + parts.shape[1:], BF16)], (parts,), after=after)[0]


def local(features, weights, cotangent):
    tm, rows = lax.axis_size(TM), lax.axis_size(ROWS)
    plane, depth = lax.axis_size(PLANE), lax.axis_size("z_pair")
    cells = F * tm * H * rows * W
    features = features.reshape(F, CH * H, W)
    cotangent = cotangent.reshape(F, CH * H, W)

    forward, back = [(i, i + 1) for i in range(tm - 1)], [(i + 1, i) for i in range(tm - 1)]
    before = lax.ppermute(features[F - 2 :], TM, forward)
    features, cotangent = call(
        load_kernel,
        "load",
        [((F, CH * H, W), BF16), ((F, CH * H, W), BF16)],
        (),
        after=[pltpu.with_memory_space_constraint(value, pltpu.HBM) for value in (features, cotangent)],
        scratch=[pltpu.SemaphoreType.DMA((2,))],
    )
    own, bottom, top = call(
        cot_kernel,
        "cot_rows",
        [((H * CH, FW), BF16), ((CH, FW), BF16), ((CH, FW), BF16)],
        (cotangent,),
        1 << 30,
    )
    above = lax.ppermute(bottom, ROWS, [(i, i + 1) for i in range(rows - 1)])
    below = lax.ppermute(top, ROWS, [(i + 1, i) for i in range(rows - 1)])
    act, normed, scale = call(
        active_kernel,
        "active",
        [((H, TAP, FW), BF16), ((H, CH, FW), F32), ((H, 1, FW), F32)],
        (features,),
        1 << 31,
    )
    (wsum,) = call(inner_kernel, "own_cells", [((3, TAP, TAP), F32)], (own, act), 1 << 31)
    wsum, past_act = call(
        past_kernel,
        "frames_before",
        [((3, TAP, TAP), F32), ((2, TAP, NEXT), BF16)],
        (before, own, wsum),
        1 << 30,
    )
    packed, first_frames = call(
        edge_kernel,
        "edge_rows",
        [((PACKED, W), BF16), (((H + 2) * CH, NEXT), BF16)],
        (above, below, own, act, past_act, wsum),
        1 << 30,
    )
    later = lax.ppermute(first_frames, TM, back)
    input_grad, done = call(
        input_kernel,
        "input_grad",
        [((F, CH * H, W), BF16), ((8, W), F32)],
        (above, below, own, later, normed, scale, weights.reshape(27, CH, CH)),
        1 << 31,
    )

    part = PACKED // plane
    parts = lax.all_to_all(packed.reshape(plane, part, W), PLANE, 0, 0)
    slabs = sum_to_slots(parts, depth, "plane_sum", after=())
    slabs = lax.all_to_all(slabs, "z_pair", 0, 0)
    whole = sum_to_slots(slabs, plane, "depth_sum", after=(done,))
    whole = lax.all_to_all(whole, PLANE, 0, 0).reshape(PACKED, W)

    (weight_grad,) = call(
        lambda *refs: unpack_kernel(1.0 / float(cells) ** 0.5, *refs),
        "unpack",
        [((27, CH, CH), F32)],
        (whole,),
        out_hbm=True,
        scratch=[pltpu.VMEM((3, 9, CH, CH), F32), pltpu.SemaphoreType.DMA((3,))],
    )
    return (input_grad.reshape(F, CH, H, W), weight_grad.reshape(3, 3, 3, CH, CH))


def solution(mesh):
    fine = Mesh(
        mesh.devices.reshape(2, 4, 2, 2, 8, 2), ("y_hi", "x", "core", "y_lo", "z_pair", "z_in")
    )
    return jax.shard_map(
        local,
        mesh=fine,
        in_specs=(P(TM, None, ROWS, None), P(), P(TM, None, ROWS, None)),
        out_specs=(P(TM, None, ROWS, None), P()),
        check_vma=False,
    )
```

time: 91.5 us -> 87.8 us (0.960)
  blocking collectives: 62.7 us -> 18.7 us
  starting transfers between devices: 11.4 us -> 35.2 us
  waiting for transfers between devices: 4.44 us -> 20.2 us
  Pallas kernels: 7.64 us -> 11.6 us
  local copies, waits for them, and re-layouts: 4.16 us -> 1 us
    all_to_all x3 -> x1, blocking collectives: 62.7 us -> 18.7 us  [local(): whole = lax.all_to_all(whole, PLANE, 0, 0).reshape(PACKED, W)]
    all_to_all x0 -> x2, starting transfers between devices: none -> 23.5 us  [the longest x1 14.7 us: local(): parts = lax.all_to_all(packed.reshape(plane, part, W), PLANE, 0, 0)]
    all_to_all x0 -> x2, waiting for transfers between devices: none -> 19.3 us  [the longest x1 10.4 us: local(): parts = lax.all_to_all(packed.reshape(plane, part, W), PLANE, 0, 0)]
    pallas_call x5 -> x10, Pallas kernels: 7.64 us -> 11.6 us  [call(): pl.pallas_call(kernel, out_shape=tuple((jax.ShapeDtypeStruct(shape, dtype...]
    ppermute x1, waiting for transfers between devices: 4.24 us -> 0.91 us  [local(): below = lax.ppermute(top, ROWS, [(i + 1, i) for i in range(rows - 1)])]
    unnamed x6 -> x2, local copies, waits for them, and re-layouts: 3.08 us -> 0.01 us
    ppermute x1, starting transfers between devices: 1.3 us -> 3.55 us  [local(): above = lax.ppermute(bottom, ROWS, [(i, i + 1) for i in range(rows - 1)])]
    ppermute x1 -> x2, starting transfers between devices: 8.79 us -> 6.87 us  [the longest x1 4.51 us: local(): before = lax.ppermute(features[F - 2:], TM, forward)]
  transfers between devices with their start and end apart: 3 -> 6, of which waited for: 2 -> 3; matrix products, arithmetic and copies ran while one was open for 0% -> 0% of each run, Pallas kernels for 3% -> 10%
where the time goes in v4:
time: 87.8 us; the launch traced here: 87.4 us
  starting transfers between devices  35.2 us (40%)
  waiting for transfers between devices  20.2 us (23%)
  blocking collectives  18.7 us (21%)
  Pallas kernels  11.6 us (13%)
  local copies, waits for them, and re-layouts  1 us (1%)
    all_to_all x1, blocking collectives, local(): whole = lax.all_to_all(whole, PLANE, 0, 0).reshape(PACKED, W)  18.7 us
    all_to_all x1, starting transfers between devices, local(): parts = lax.all_to_all(packed.reshape(plane, part, W), PLANE, 0, 0)  14.7 us
    pallas_call x10, Pallas kernels, call(): pl.pallas_call(kernel, out_shape=tuple((jax.ShapeDtypeStruct(shape, dtype...  11.6 us
    all_to_all x1, waiting for transfers between devices, local(): parts = lax.all_to_all(packed.reshape(plane, part, W), PLANE, 0, 0)  10.4 us
    all_to_all x1, waiting for transfers between devices, local(): slabs = lax.all_to_all(slabs, 'z_pair', 0, 0)  8.91 us
    all_to_all x1, starting transfers between devices, local(): slabs = lax.all_to_all(slabs, 'z_pair', 0, 0)  8.72 us
    ppermute x1, starting transfers between devices, local(): before = lax.ppermute(features[F - 2:], TM, forward)  4.51 us
    ppermute x1, starting transfers between devices, local(): above = lax.ppermute(bottom, ROWS, [(i, i + 1) for i in range(rows - 1)])  3.55 us
  transfers between devices with their start and end apart: 6, of which 3 were waited for; matrix products, arithmetic and copies ran while one was open for 0% of the time, Pallas kernels for 10%

profile of v4, /device:TPU:1, one launch (start us, length us, event | category | flops | bytes accessed | tf_op | source)
XLA Modules:
  0.0 87.4 jit_solution(12558672983787173621)
XLA Ops:
  0.6 1.0 %slice.6 = bf16[2,96,4,128]{3,2,1,0:T(4,128)(2,1)S(1)} slice(bf16[4,96,4,128]{3,2,1,0:T(4,128)(2,1)} %param.3), slice={[2:4], [0:96], [0:4], [0:128]} | slice | bytes 393216 | tf_op jit(solution)/shard_map/slice | solution.py:230
  1.6 4.5 %collective-permute-start.2 = (bf16[2,384,128]{2,1,0:T(8,128)(2,1)S(1)}, bf16[2,384,128]{2,1,0:T(8,128)(2,1)S(1)}, u32[]{:S(2)}, u32[]{:S(2)}) collective-permute-start(bf16[2,384,128]{2,1,0:T(8,128)(2,1)S(1)} %bitcast.13), channel_id=1, source_target_pairs={{0,32},{32,64},{64,96},{96,128},{128,160},{160,192},{192,224},{224... | collective-permute-start | bytes 589832 | tf_op jit(solution)/shard_map/ppermute | solution.py:230
  6.1 1.1 %load.1 = (bf16[4,384,128]{2,1,0:T(8,128)(2,1)S(1)}, bf16[4,384,128]{2,1,0:T(8,128)(2,1)S(1)}) custom-call(bf16[4,384,128]{2,1,0:T(8,128)(2,1)} %bitcast.11, bf16[4,384,128]{2,1,0:T(8,128)(2,1)} %bitcast.12), custom_call_target="tpu_custom_call" | custom-call | bytes 4194304 | tf_op jit(solution)/shard_map/load/pallas_call | solution.py:206
  7.3 0.4 cot_rows.1
  7.7 3.5 %collective-permute-start = (bf16[96,512]{1,0:T(8,128)(2,1)S(1)}, bf16[96,512]{1,0:T(8,128)(2,1)S(1)}, u32[]{:S(2)}, u32[]{:S(2)}) collective-permute-start(bf16[96,512]{1,0:T(8,128)(2,1)S(1)} %get-tuple-element.17), channel_id=1, source_target_pairs={{0,1},{1,2},{2,3},{3,4},{4,5},{5,6},{6,7},{7,8},{8,9},{9,10},{10,1... | collective-permute-start | bytes 294920 | tf_op jit(solution)/shard_map/ppermute | solution.py:246
  11.2 1.3 %collective-permute-start.1 = (bf16[96,512]{1,0:T(8,128)(2,1)S(1)}, bf16[96,512]{1,0:T(8,128)(2,1)S(1)}, u32[]{:S(2)}, u32[]{:S(2)}) collective-permute-start(bf16[96,512]{1,0:T(8,128)(2,1)S(1)} %get-tuple-element.18), channel_id=1, source_target_pairs={{1,0},{2,1},{3,2},{4,3},{5,4},{6,5},{7,6},{8,7},{9,8},{10,9},{11,1... | collective-permute-start | bytes 294920 | tf_op jit(solution)/shard_map/ppermute | solution.py:247
  12.5 0.8 active.1
  13.3 1.4 %own_cells.1.inner_sum = f32[3,288,288]{2,1,0:T(8,128)S(1)} custom-call(bf16[384,512]{1,0:T(8,128)(2,1)S(1)} %get-tuple-element.19.own, bf16[4,288,512]{2,1,0:T(8,128)(2,1)S(1)} %get-tuple-element.21.act), custom_call_target="tpu_custom_call" | custom-call | flops 2147483648 | bytes 4194304 | tf_op jit(solution)/shard_map/own_cells/pallas_call | solution.py:206
  14.7 0.0 collective-permute-done.2.before
  14.7 1.1 %frames_before.1 = (f32[3,288,288]{2,1,0:T(8,128)S(1)}, bf16[2,288,256]{2,1,0:T(8,128)(2,1)S(1)}) custom-call(bf16[2,384,128]{2,1,0:T(8,128)(2,1)S(1)} %collective-permute-done.2.before, bf16[384,512]{1,0:T(8,128)(2,1)S(1)} %get-tuple-element.19.own, f32[3,288,288]{2,1,0:T(8,128)S(1)} %own_cells.1.inner_sum), custom_call_target="tpu_custom_call" | custom-call | flops 1073741824 | bytes 4194304 | tf_op jit(solution)/shard_map/frames_before/pallas_call | solution.py:206
  15.8 0.0 collective-permute-done.above
  15.9 0.9 %collective-permute-done.1.below = bf16[96,512]{1,0:T(8,128)(2,1)S(1)} collective-permute-done((bf16[96,512]{1,0:T(8,128)(2,1)S(1)}, bf16[96,512]{1,0:T(8,128)(2,1)S(1)}, u32[]{:S(2)}, u32[]{:S(2)}) %collective-permute-start.1) | collective-permute-done | bytes 98336 | tf_op jit(solution)/shard_map/ppermute | solution.py:247
  16.8 1.6 %edge_rows.1 = (bf16[2048,128]{1,0:T(8,128)(2,1)}, bf16[576,256]{1,0:T(8,128)(2,1)S(1)}) custom-call(bf16[96,512]{1,0:T(8,128)(2,1)S(1)} %collective-permute-done.above, bf16[96,512]{1,0:T(8,128)(2,1)S(1)} %collective-permute-done.1.below, bf16[384,512]{1,0:T(8,128)(2,1)S(1)} %get-tuple-element.19.own, bf16[4,288,512]{2,1,0:T(8,128)(2,1)S(1)} %get-tuple-element.21.act, ...), custom_call_target="tpu_custom_call" | custom-call | flops 1073741824 | bytes 4194304 | tf_op jit(solution)/shard_map/edge_rows/pallas_call | solution.py:206
  18.4 14.7 %all-to-all-start = ((bf16[64,32,128]{2,1,0:T(8,128)(2,1)}), bf16[64,32,128]{2,1,0:T(8,128)(2,1)S(1)}, u32[]{:S(2)}, u32[]{:S(2)}) async-start(bf16[64,32,128]{2,1,0:T(8,128)(2,1)} %bitcast.5), calls=%async_computation | async-start | bytes 1048576 | tf_op jit(solution)/shard_map/all_to_all | solution.py:280
  33.1 2.4 %collective-permute-start.3 = (bf16[576,256]{1,0:T(8,128)(2,1)S(1)}, bf16[576,256]{1,0:T(8,128)(2,1)S(1)}, u32[]{:S(2)}, u32[]{:S(2)}) collective-permute-start(bf16[576,256]{1,0:T(8,128)(2,1)S(1)} %get-tuple-element.24), channel_id=1, source_target_pairs={{32,0},{64,32},{96,64},{128,96},{160,128},{192,160},{224,192},{256... | collective-permute-start | bytes 884744 | tf_op jit(solution)/shard_map/ppermute | solution.py:270
  35.5 10.4 %all-to-all-done.parts = bf16[64,32,128]{2,1,0:T(8,128)(2,1)S(1)} async-done(((bf16[64,32,128]{2,1,0:T(8,128)(2,1)}), bf16[64,32,128]{2,1,0:T(8,128)(2,1)S(1)}, u32[]{:S(2)}, u32[]{:S(2)}) %all-to-all-start) | async-done | bytes 524320 | tf_op jit(solution)/shard_map/all_to_all | solution.py:280
  45.8 0.7 plane_sum.1
  46.6 8.7 %all-to-all-start.1 = ((bf16[8,32,128]{2,1,0:T(8,128)(2,1)}), bf16[8,32,128]{2,1,0:T(8,128)(2,1)S(1)}, u32[]{:S(2)}, u32[]{:S(2)}) async-start(bf16[8,32,128]{2,1,0:T(8,128)(2,1)} %plane_sum.1), calls=%async_computation.1 | async-start | bytes 131072 | tf_op jit(solution)/shard_map/all_to_all | solution.py:282
  55.3 0.0 collective-permute-done.3.later
  55.3 0.0 copy-done
  55.3 3.1 %input_grad.1 = (bf16[4,384,128]{2,1,0:T(8,128)(2,1)}, f32[8,128]{1,0:T(8,128)S(1)}) custom-call(bf16[96,512]{1,0:T(8,128)(2,1)S(1)} %collective-permute-done.above, bf16[96,512]{1,0:T(8,128)(2,1)S(1)} %collective-permute-done.1.below, bf16[384,512]{1,0:T(8,128)(2,1)S(1)} %get-tuple-element.19.own, bf16[576,256]{1,0:T(8,128)(2,1)S(1)} %collective-permute-done.3.later, ...), custom_call_target="tpu_custom_call" | custom-call | flops 2147483648 | bytes 4194304 | tf_op jit(solution)/shard_map/input_grad/pallas_call | solution.py:206
  58.4 8.9 %all-to-all-done.1.parts = bf16[8,32,128]{2,1,0:T(8,128)(2,1)S(1)} async-done(((bf16[8,32,128]{2,1,0:T(8,128)(2,1)}), bf16[8,32,128]{2,1,0:T(8,128)(2,1)S(1)}, u32[]{:S(2)}, u32[]{:S(2)}) %all-to-all-start.1) | async-done | bytes 65568 | tf_op jit(solution)/shard_map/all_to_all | solution.py:282
  67.3 18.7 %all_to_all.15 = bf16[64,32,128]{2,1,0:T(8,128)(2,1)S(1)} all-to-all(bf16[64,32,128]{2,1,0:T(8,128)(2,1)S(1)} %depth_sum.1), channel_id=1, replica_groups=mesh['y_hi'=2,'x'=4,'core'=2,'y_lo'=2,'z_pair'=8,'z_in'=2] {'y_hi','x','..., dimensions={0} | all-to-all | bytes 1048576 | tf_op jit(solution)/shard_map/all_to_all | solution.py:284
  86.0 1.4 %unpack.1 = f32[27,96,96]{2,1,0:T(8,128)} custom-call(bf16[2048,128]{1,0:T(8,128)(2,1)S(1)} %bitcast.8), custom_call_target="tpu_custom_call" | custom-call | bytes 4194304 | tf_op jit(solution)/shard_map/unpack/pallas_call | solution.py:206
  (2 shorter events, 0.0 us)
Async XLA Ops:
  1.6 13.1 %collective-permute-start.2 = (bf16[2,384,128]{2,1,0:T(8,128)(2,1)S(1)}, bf16[2,384,128]{2,1,0:T(8,128)(2,1)S(1)}, u32[]{:S(2)}, u32[]{:S(2)}) collective-permute-start(bf16[2,384,128]{2,1,0:T(8,128)(2,1)S(1)} %bitcast.13), channel_id=1, source_target_pairs={{0,32},{32,64},{64,96},{96,128},{128,160},{160,192},{192,224},{224... | collective-permute-start | bytes 589832 | tf_op jit(solution)/shard_map/ppermute | solution.py:230
  7.7 8.2 %collective-permute-start = (bf16[96,512]{1,0:T(8,128)(2,1)S(1)}, bf16[96,512]{1,0:T(8,128)(2,1)S(1)}, u32[]{:S(2)}, u32[]{:S(2)}) collective-permute-start(bf16[96,512]{1,0:T(8,128)(2,1)S(1)} %get-tuple-element.17), channel_id=1, source_target_pairs={{0,1},{1,2},{2,3},{3,4},{4,5},{5,6},{6,7},{7,8},{8,9},{9,10},{10,1... | collective-permute-start | bytes 294920 | tf_op jit(solution)/shard_map/ppermute | solution.py:246
  11.2 5.5 %collective-permute-start.1 = (bf16[96,512]{1,0:T(8,128)(2,1)S(1)}, bf16[96,512]{1,0:T(8,128)(2,1)S(1)}, u32[]{:S(2)}, u32[]{:S(2)}) collective-permute-start(bf16[96,512]{1,0:T(8,128)(2,1)S(1)} %get-tuple-element.18), channel_id=1, source_target_pairs={{1,0},{2,1},{3,2},{4,3},{5,4},{6,5},{7,6},{8,7},{9,8},{10,9},{11,1... | collective-permute-start | bytes 294920 | tf_op jit(solution)/shard_map/ppermute | solution.py:247
  18.4 36.9 %copy-start = (bf16[3,3,3,96,96]{4,3,2,1,0:T(8,128)(2,1)S(1)}, bf16[3,3,3,96,96]{4,3,2,1,0:T(8,128)(2,1)}, u32[]{:S(2)}) copy-start(bf16[3,3,3,96,96]{4,3,2,1,0:T(8,128)(2,1)} %param.4) | copy-start | bytes 1492996
  18.4 27.5 %all-to-all-start = ((bf16[64,32,128]{2,1,0:T(8,128)(2,1)}), bf16[64,32,128]{2,1,0:T(8,128)(2,1)S(1)}, u32[]{:S(2)}, u32[]{:S(2)}) async-start(bf16[64,32,128]{2,1,0:T(8,128)(2,1)} %bitcast.5), calls=%async_computation | async-start | bytes 1048576 | tf_op jit(solution)/shard_map/all_to_all | solution.py:280
  33.1 22.2 %collective-permute-start.3 = (bf16[576,256]{1,0:T(8,128)(2,1)S(1)}, bf16[576,256]{1,0:T(8,128)(2,1)S(1)}, u32[]{:S(2)}, u32[]{:S(2)}) collective-permute-start(bf16[576,256]{1,0:T(8,128)(2,1)S(1)} %get-tuple-element.24), channel_id=1, source_target_pairs={{32,0},{64,32},{96,64},{128,96},{160,128},{192,160},{224,192},{256... | collective-permute-start | bytes 884744 | tf_op jit(solution)/shard_map/ppermute | solution.py:270
  46.6 20.7 %all-to-all-start.1 = ((bf16[8,32,128]{2,1,0:T(8,128)(2,1)}), bf16[8,32,128]{2,1,0:T(8,128)(2,1)S(1)}, u32[]{:S(2)}, u32[]{:S(2)}) async-start(bf16[8,32,128]{2,1,0:T(8,128)(2,1)} %plane_sum.1), calls=%async_computation.1 | async-start | bytes 131072 | tf_op jit(solution)/shard_map/all_to_all | solution.py:282

commit v5 on v4

--- a/solution.py
+++ b/solution.py
@@ -7,7 +7,8 @@
 
 TM = ("y_hi", "x", "core")
 ROWS = ("y_lo", "z_pair", "z_in")
-PLANE = ("y_hi", "x", "core", "y_lo", "z_in")
+NEAR = ("y_hi", "x", "y_lo", "z_in")
+PLANE = ("core",) + NEAR
 CH = 96
 W = 128
 F = 4
@@ -15,7 +16,9 @@
 FW = F * W
 NEXT = 2 * W
 TAP = 3 * CH
-PACKED = 2048
+HALF = CH // 2
+TILE = 3 * HALF
+PACKED = 1024
 F32 = jnp.float32
 BF16 = jnp.bfloat16
 
@@ -64,10 +67,11 @@
     return 1.0 / (1.0 + jnp.exp(-x))
 
 
-def load_kernel(feat_in, cot_in, feat, cot, sems):
+def load_kernel(feat_in, cot_in, last_frames, feat, cot, sems):
     copies = [
-        pltpu.make_async_copy(cot_in, cot, sems.at[0]),
-        pltpu.make_async_copy(feat_in, feat, sems.at[1]),
+        pltpu.make_async_copy(feat_in.at[pl.ds(F - 2, 2)], last_frames, sems.at[0]),
+        pltpu.make_async_copy(cot_in, cot, sems.at[1]),
+        pltpu.make_async_copy(feat_in, feat, sems.at[2]),
     ]
     for copy in copies:
         copy.start()
@@ -137,12 +141,17 @@
     first_frames[:CH, :] = upper[:, :NEXT]
     first_frames[CH : 5 * CH, :] = own[:, :NEXT]
     first_frames[5 * CH :, :] = lower[:, :NEXT]
-    for t in range(3):
-        for j in range(2):
-            packed[(2 * t + j) * TAP : (2 * t + j + 1) * TAP, :] = sums[t][:, j * W : (j + 1) * W].astype(BF16)
-    rests = [total[:, 2 * W :] for total in sums] + [jnp.zeros((TAP, W - CH), F32)]
-    packed[6 * TAP : 7 * TAP, :] = jnp.concatenate(rests, axis=1).astype(BF16)
-    packed[7 * TAP :, :] = jnp.zeros((PACKED - 7 * TAP, W), BF16)
+    for half in range(2):
+        picked = [
+            jnp.concatenate([total[k * CH + half * HALF : k * CH + (half + 1) * HALF] for k in range(3)], axis=0)
+            for total in sums
+        ]
+        for t in range(3):
+            for j in range(2):
+                packed[half, (2 * t + j) * TILE : (2 * t + j + 1) * TILE, :] = picked[t][:, j * W : (j + 1) * W].astype(BF16)
+        rests = [total[:, 2 * W :] for total in picked] + [jnp.zeros((TILE, W - CH), F32)]
+        packed[half, 6 * TILE : 7 * TILE, :] = jnp.concatenate(rests, axis=1).astype(BF16)
+        packed[half, 7 * TILE :, :] = jnp.zeros((PACKED - 7 * TILE, W), BF16)
 
 
 def input_kernel(above, below, own, later, normed, scale, weights, grad_out, done):
@@ -184,35 +193,38 @@
         out[i] = total
 
 
-def unpack_kernel(norm_factor, packed, out, held, sems):
-    rests = packed[6 * TAP : 7 * TAP, :].astype(F32)
+def unpack_kernel(norm_factor, half, packed, *refs):
+    out, held, sems = refs[-3:]
+    rests = packed[6 * TILE : 7 * TILE, :].astype(F32)
     width = TAP - 2 * W
+    place = pl.multiple_of(half[0] * HALF, HALF)
     copies = []
     for t in range(3):
-        tiles = [packed[(2 * t + j) * TAP : (2 * t + j + 1) * TAP, :].astype(F32) for j in range(2)]
+        tiles = [packed[(2 * t + j) * TILE : (2 * t + j + 1) * TILE, :].astype(F32) for j in range(2)]
         block = jnp.concatenate(tiles + [rests[:, t * width : (t + 1) * width]], axis=1) * norm_factor
         for c in range(3):
             column = block[:, c * CH : (c + 1) * CH]
             for k in range(3):
-                held[t, (2 - k) * 3 + c] = column[k * CH : (k + 1) * CH]
-        copies.append(pltpu.make_async_copy(held.at[t], out.at[pl.ds(t * 9, 9)], sems.at[t]))
+                held[t, (2 - k) * 3 + c] = column[k * HALF : (k + 1) * HALF]
+        copies.append(pltpu.make_async_copy(held.at[t], out.at[pl.ds(t * 9, 9), pl.ds(place, HALF)], sems.at[t]))
         copies[-1].start()
     for copy in copies:
         copy.wait()
 
 
-def call(kernel, name, outs, args, flops=0, after=(), out_hbm=False, scratch=()):
+def call(kernel, name, outs, args, flops=0, smem=(), after=(), out_hbm=False, scratch=(), aliases={}):
     vmem, anywhere = pl.BlockSpec(memory_space=pltpu.VMEM), pl.BlockSpec(memory_space=pl.ANY)
     return pl.pallas_call(
         kernel,
         out_shape=tuple(jax.ShapeDtypeStruct(shape, dtype) for shape, dtype in outs),
-        in_specs=[vmem] * len(args) + [anywhere] * len(after),
+        in_specs=[pl.BlockSpec(memory_space=pltpu.SMEM)] * len(smem) + [vmem] * len(args) + [anywhere] * len(after),
         out_specs=(anywhere if out_hbm else vmem,) * len(outs),
         scratch_shapes=scratch,
+        input_output_aliases=aliases,
         compiler_params=pltpu.CompilerParams(vmem_limit_bytes=16 << 20),
-        cost_estimate=pl.CostEstimate(flops=flops, bytes_accessed=4 << 20, transcendentals=0),
+        cost_estimate=pl.CostEstimate(flops=flops, bytes_accessed=0, transcendentals=0),
         name=name,
-    )(*args, *after)
+    )(*smem, *args, *after)
 
 
 def sum_to_slots(parts, count, name, after=()):
@@ -227,21 +239,21 @@
     cotangent = cotangent.reshape(F, CH * H, W)
 
     forward, back = [(i, i + 1) for i in range(tm - 1)], [(i + 1, i) for i in range(tm - 1)]
-    before = lax.ppermute(features[F - 2 :], TM, forward)
-    features, cotangent = call(
+    last_frames, features, cotangent = call(
         load_kernel,
         "load",
-        [((F, CH * H, W), BF16), ((F, CH * H, W), BF16)],
+        [((2, CH * H, W), BF16), ((F, CH * H, W), BF16), ((F, CH * H, W), BF16)],
         (),
         after=[pltpu.with_memory_space_constraint(value, pltpu.HBM) for value in (features, cotangent)],
-        scratch=[pltpu.SemaphoreType.DMA((2,))],
-    )
+        scratch=[pltpu.SemaphoreType.DMA((3,))],
+    )
+    before = lax.ppermute(last_frames, TM, forward)
     own, bottom, top = call(
         cot_kernel,
         "cot_rows",
         [((H * CH, FW), BF16), ((CH, FW), BF16), ((CH, FW), BF16)],
         (cotangent,),
-        1 << 30,
+        1 << 33,
     )
     above = lax.ppermute(bottom, ROWS, [(i, i + 1) for i in range(rows - 1)])
     below = lax.ppermute(top, ROWS, [(i + 1, i) for i in range(rows - 1)])
@@ -250,20 +262,18 @@
         "active",
         [((H, TAP, FW), BF16), ((H, CH, FW), F32), ((H, 1, FW), F32)],
         (features,),
-        1 << 31,
-    )
-    (wsum,) = call(inner_kernel, "own_cells", [((3, TAP, TAP), F32)], (own, act), 1 << 31)
+    )
+    (wsum,) = call(inner_kernel, "own_cells", [((3, TAP, TAP), F32)], (own, act))
     wsum, past_act = call(
         past_kernel,
         "frames_before",
         [((3, TAP, TAP), F32), ((2, TAP, NEXT), BF16)],
         (before, own, wsum),
-        1 << 30,
     )
     packed, first_frames = call(
         edge_kernel,
         "edge_rows",
-        [((PACKED, W), BF16), (((H + 2) * CH, NEXT), BF16)],
+        [((2, PACKED, W), BF16), (((H + 2) * CH, NEXT), BF16)],
         (above, below, own, act, past_act, wsum),
         1 << 30,
     )
@@ -276,22 +286,29 @@
         1 << 31,
     )
 
-    part = PACKED // plane
+    part = 2 * PACKED // plane
     parts = lax.all_to_all(packed.reshape(plane, part, W), PLANE, 0, 0)
-    slabs = sum_to_slots(parts, depth, "plane_sum", after=())
+    slabs = sum_to_slots(parts, depth, "plane_sum")
     slabs = lax.all_to_all(slabs, "z_pair", 0, 0)
-    whole = sum_to_slots(slabs, plane, "depth_sum", after=(done,))
-    whole = lax.all_to_all(whole, PLANE, 0, 0).reshape(PACKED, W)
-
-    (weight_grad,) = call(
-        lambda *refs: unpack_kernel(1.0 / float(cells) ** 0.5, *refs),
-        "unpack",
-        [((27, CH, CH), F32)],
-        (whole,),
-        out_hbm=True,
-        scratch=[pltpu.VMEM((3, 9, CH, CH), F32), pltpu.SemaphoreType.DMA((3,))],
-    )
-    return (input_grad.reshape(F, CH, H, W), weight_grad.reshape(3, 3, 3, CH, CH))
+    slots = sum_to_slots(slabs, plane // 2, "depth_sum", after=(done,))
+    own_half = lax.all_to_all(slots, NEAR, 0, 0).reshape(PACKED, W)
+    other_half = lax.ppermute(own_half, "core", [(0, 1), (1, 0)])
+
+    core = lax.axis_index("core").astype(jnp.int32).reshape(1)
+    weight_grad = ()
+    for half, values in ((core, own_half), (1 - core, other_half)):
+        weight_grad = call(
+            lambda *refs: unpack_kernel(1.0 / float(cells) ** 0.5, *refs),
+            "unpack",
+            [((27, CH, CH), F32)],
+            (values,),
+            smem=(half,),
+            after=weight_grad,
+            out_hbm=True,
+            scratch=[pltpu.VMEM((3, 9, HALF, CH), F32), pltpu.SemaphoreType.DMA((3,))],
+            aliases={2: 0} if weight_grad else {},
+        )
+    return (input_grad.reshape(F, CH, H, W), weight_grad[0].reshape(3, 3, 3, CH, CH))
 
 
 def solution(mesh):

time: 87.8 us -> 86.4 us (0.984)
  blocking collectives: 18.7 us -> 12.6 us
  starting transfers between devices: 35.2 us -> 40.5 us
  local copies, waits for them, and re-layouts: 1 us -> 0.01 us
    all_to_all x1, blocking collectives: 18.7 us -> 12.6 us  [local(): own_half = lax.all_to_all(slots, NEAR, 0, 0).reshape(PACKED, W)]
    ppermute x1 -> x2, starting transfers between devices: 4.51 us -> 9.88 us  [the longest x1 5.37 us: local(): other_half = lax.ppermute(own_half, 'core', [(0, 1), (1, 0)])]
    slice x1 -> x0, local copies, waits for them, and re-layouts: 1 us -> none  [local(): before = lax.ppermute(features[F - 2:], TM, forward)]
    pallas_call x10 -> x11, Pallas kernels: 11.6 us -> 12.4 us  [call(): pl.pallas_call(kernel, out_shape=tuple((jax.ShapeDtypeStruct(shape, dtype...]
  transfers between devices with their start and end apart: 6 -> 7, of which waited for: 3 -> 4; matrix products, arithmetic and copies ran while one was open for 0% -> 0% of each run, Pallas kernels for 10% -> 10%
where the time goes in v5:
time: 86.4 us; the launch traced here: 85.9 us
  starting transfers between devices  40.5 us (47%)
  waiting for transfers between devices  19.6 us (23%)
  blocking collectives  12.6 us (15%)
  Pallas kernels  12.4 us (14%)
    all_to_all x1, starting transfers between devices, local(): parts = lax.all_to_all(packed.reshape(plane, part, W), PLANE, 0, 0)  14.8 us
    all_to_all x1, blocking collectives, local(): own_half = lax.all_to_all(slots, NEAR, 0, 0).reshape(PACKED, W)  12.6 us
    pallas_call x11, Pallas kernels, call(): pl.pallas_call(kernel, out_shape=tuple((jax.ShapeDtypeStruct(shape, dtype...  12.4 us
    all_to_all x1, waiting for transfers between devices, local(): parts = lax.all_to_all(packed.reshape(plane, part, W), PLANE, 0, 0)  9.74 us
    all_to_all x1, waiting for transfers between devices, local(): slabs = lax.all_to_all(slabs, 'z_pair', 0, 0)  8.9 us
    all_to_all x1, starting transfers between devices, local(): slabs = lax.all_to_all(slabs, 'z_pair', 0, 0)  8.72 us
    ppermute x1, starting transfers between devices, local(): other_half = lax.ppermute(own_half, 'core', [(0, 1), (1, 0)])  5.37 us
    ppermute x1, starting transfers between devices, local(): before = lax.ppermute(last_frames, TM, forward)  4.51 us
  transfers between devices with their start and end apart: 7, of which 4 were waited for; matrix products, arithmetic and copies ran while one was open for 0% of the time, Pallas kernels for 10%

profile of v5, /device:TPU:1, one launch (start us, length us, event | category | flops | bytes accessed | tf_op | source)
XLA Modules:
  0.0 85.9 jit_solution(12564939674534918358)
XLA Ops:
  0.6 1.2 %load.1 = (bf16[2,384,128]{2,1,0:T(8,128)(2,1)S(1)}, bf16[4,384,128]{2,1,0:T(8,128)(2,1)S(1)}, bf16[4,384,128]{2,1,0:T(8,128)(2,1)S(1)}) custom-call(bf16[4,384,128]{2,1,0:T(8,128)(2,1)} %bitcast.12, bf16[4,384,128]{2,1,0:T(8,128)(2,1)} %bitcast.13), custom_call_target="tpu_custom_call" | custom-call | tf_op jit(solution)/shard_map/load/pallas_call | solution.py:217
  1.9 4.5 %collective-permute-start.2 = (bf16[2,384,128]{2,1,0:T(8,128)(2,1)S(1)}, bf16[2,384,128]{2,1,0:T(8,128)(2,1)S(1)}, u32[]{:S(2)}, u32[]{:S(2)}) collective-permute-start(bf16[2,384,128]{2,1,0:T(8,128)(2,1)S(1)} %get-tuple-element.23), channel_id=1, source_target_pairs={{0,32},{32,64},{64,96},{96,128},{128,160},{160,192},{192,224},{224... | collective-permute-start | bytes 589832 | tf_op jit(solution)/shard_map/ppermute | solution.py:250
  6.4 0.4 cot_rows.1
  6.8 3.5 %collective-permute-start = (bf16[96,512]{1,0:T(8,128)(2,1)S(1)}, bf16[96,512]{1,0:T(8,128)(2,1)S(1)}, u32[]{:S(2)}, u32[]{:S(2)}) collective-permute-start(bf16[96,512]{1,0:T(8,128)(2,1)S(1)} %get-tuple-element.18), channel_id=1, source_target_pairs={{0,1},{1,2},{2,3},{3,4},{4,5},{5,6},{6,7},{7,8},{8,9},{9,10},{10,1... | collective-permute-start | bytes 294920 | tf_op jit(solution)/shard_map/ppermute | solution.py:258
  10.3 1.3 %collective-permute-start.1 = (bf16[96,512]{1,0:T(8,128)(2,1)S(1)}, bf16[96,512]{1,0:T(8,128)(2,1)S(1)}, u32[]{:S(2)}, u32[]{:S(2)}) collective-permute-start(bf16[96,512]{1,0:T(8,128)(2,1)S(1)} %get-tuple-element.19), channel_id=1, source_target_pairs={{1,0},{2,1},{3,2},{4,3},{5,4},{6,5},{7,6},{8,7},{9,8},{10,9},{11,1... | collective-permute-start | bytes 294920 | tf_op jit(solution)/shard_map/ppermute | solution.py:259
  11.6 0.8 active.1
  12.4 1.4 %own_cells.1.inner_sum = f32[3,288,288]{2,1,0:T(8,128)S(1)} custom-call(bf16[384,512]{1,0:T(8,128)(2,1)S(1)} %get-tuple-element.20.own, bf16[4,288,512]{2,1,0:T(8,128)(2,1)S(1)} %get-tuple-element.22.act), custom_call_target="tpu_custom_call" | custom-call | tf_op jit(solution)/shard_map/own_cells/pallas_call | solution.py:217
  13.9 1.1 %frames_before.1 = (f32[3,288,288]{2,1,0:T(8,128)S(1)}, bf16[2,288,256]{2,1,0:T(8,128)(2,1)S(1)}) custom-call(bf16[2,384,128]{2,1,0:T(8,128)(2,1)S(1)} %collective-permute-done.2.before, bf16[384,512]{1,0:T(8,128)(2,1)S(1)} %get-tuple-element.20.own, f32[3,288,288]{2,1,0:T(8,128)S(1)} %own_cells.1.inner_sum), custom_call_target="tpu_custom_call" | custom-call | tf_op jit(solution)/shard_map/frames_before/pallas_call | solution.py:217
  15.0 0.0 collective-permute-done.above
  15.0 0.9 %collective-permute-done.1.below = bf16[96,512]{1,0:T(8,128)(2,1)S(1)} collective-permute-done((bf16[96,512]{1,0:T(8,128)(2,1)S(1)}, bf16[96,512]{1,0:T(8,128)(2,1)S(1)}, u32[]{:S(2)}, u32[]{:S(2)}) %collective-permute-start.1) | collective-permute-done | bytes 98336 | tf_op jit(solution)/shard_map/ppermute | solution.py:259
  15.9 1.6 %edge_rows.1 = (bf16[2,1024,128]{2,1,0:T(8,128)(2,1)}, bf16[576,256]{1,0:T(8,128)(2,1)S(1)}) custom-call(bf16[96,512]{1,0:T(8,128)(2,1)S(1)} %collective-permute-done.above, bf16[96,512]{1,0:T(8,128)(2,1)S(1)} %collective-permute-done.1.below, bf16[384,512]{1,0:T(8,128)(2,1)S(1)} %get-tuple-element.20.own, bf16[4,288,512]{2,1,0:T(8,128)(2,1)S(1)} %get-tuple-element.22.act, ...), custom_call_target="tpu_custom_call" | custom-call | flops 1073741824 | tf_op jit(solution)/shard_map/edge_rows/pallas_call | solution.py:217
  17.5 14.8 %all-to-all-start = ((bf16[64,32,128]{2,1,0:T(8,128)(2,1)}), bf16[64,32,128]{2,1,0:T(8,128)(2,1)S(1)}, u32[]{:S(2)}, u32[]{:S(2)}) async-start(bf16[64,32,128]{2,1,0:T(8,128)(2,1)} %bitcast.5), calls=%async_computation | async-start | bytes 1048576 | tf_op jit(solution)/shard_map/all_to_all | solution.py:290
  32.3 2.3 %collective-permute-start.3 = (bf16[576,256]{1,0:T(8,128)(2,1)S(1)}, bf16[576,256]{1,0:T(8,128)(2,1)S(1)}, u32[]{:S(2)}, u32[]{:S(2)}) collective-permute-start(bf16[576,256]{1,0:T(8,128)(2,1)S(1)} %get-tuple-element.26), channel_id=1, source_target_pairs={{32,0},{64,32},{96,64},{128,96},{160,128},{192,160},{224,192},{256... | collective-permute-start | bytes 884744 | tf_op jit(solution)/shard_map/ppermute | solution.py:280
  34.6 9.7 %all-to-all-done.parts = bf16[64,32,128]{2,1,0:T(8,128)(2,1)S(1)} async-done(((bf16[64,32,128]{2,1,0:T(8,128)(2,1)}), bf16[64,32,128]{2,1,0:T(8,128)(2,1)S(1)}, u32[]{:S(2)}, u32[]{:S(2)}) %all-to-all-start) | async-done | bytes 524320 | tf_op jit(solution)/shard_map/all_to_all | solution.py:290
  44.3 0.7 plane_sum.1
  45.0 8.7 %all-to-all-start.1 = ((bf16[8,32,128]{2,1,0:T(8,128)(2,1)}), bf16[8,32,128]{2,1,0:T(8,128)(2,1)S(1)}, u32[]{:S(2)}, u32[]{:S(2)}) async-start(bf16[8,32,128]{2,1,0:T(8,128)(2,1)} %plane_sum.1), calls=%async_computation.1 | async-start | bytes 131072 | tf_op jit(solution)/shard_map/all_to_all | solution.py:292
  53.8 0.0 collective-permute-done.3.later
  53.8 3.0 %input_grad.1 = (bf16[4,384,128]{2,1,0:T(8,128)(2,1)}, f32[8,128]{1,0:T(8,128)S(1)}) custom-call(bf16[96,512]{1,0:T(8,128)(2,1)S(1)} %collective-permute-done.above, bf16[96,512]{1,0:T(8,128)(2,1)S(1)} %collective-permute-done.1.below, bf16[384,512]{1,0:T(8,128)(2,1)S(1)} %get-tuple-element.20.own, bf16[576,256]{1,0:T(8,128)(2,1)S(1)} %collective-permute-done.3.later, ...), custom_call_target="tpu_custom_call" | custom-call | flops 2147483648 | tf_op jit(solution)/shard_map/input_grad/pallas_call | solution.py:217
  56.8 8.9 %all-to-all-done.1.parts = bf16[8,32,128]{2,1,0:T(8,128)(2,1)S(1)} async-done(((bf16[8,32,128]{2,1,0:T(8,128)(2,1)}), bf16[8,32,128]{2,1,0:T(8,128)(2,1)S(1)}, u32[]{:S(2)}, u32[]{:S(2)}) %all-to-all-start.1) | async-done | bytes 65568 | tf_op jit(solution)/shard_map/all_to_all | solution.py:292
  65.8 12.6 %all_to_all.15 = bf16[32,32,128]{2,1,0:T(8,128)(2,1)S(1)} all-to-all(bf16[32,32,128]{2,1,0:T(8,128)(2,1)S(1)} %depth_sum.1), channel_id=1, replica_groups=mesh['y_hi'=2,'x'=4,'core'=2,'y_lo'=2,'z_pair'=8,'z_in'=2] {'y_hi','x','..., dimensions={0} | all-to-all | bytes 524288 | tf_op jit(solution)/shard_map/all_to_all | solution.py:294
  78.3 5.4 %collective-permute-start.4 = (bf16[1024,128]{1,0:T(8,128)(2,1)S(1)}, bf16[1024,128]{1,0:T(8,128)(2,1)S(1)}, u32[]{:S(2)}, u32[]{:S(2)}) collective-permute-start(bf16[1024,128]{1,0:T(8,128)(2,1)S(1)} %bitcast.8), channel_id=1, source_target_pairs={{0,32},{32,0},{1,33},{33,1},{2,34},{34,2},{3,35},{35,3},{4,36},{36... | collective-permute-start | bytes 786440 | tf_op jit(solution)/shard_map/ppermute | solution.py:295
  83.7 1.1 %unpack.2.refs_2_ = f32[27,96,96]{2,1,0:T(8,128)} custom-call(s32[1]{0:T(128)} %bitcast.4.refs_0_, bf16[1024,128]{1,0:T(8,128)(2,1)S(1)} %bitcast.9), custom_call_target="tpu_custom_call" | custom-call | tf_op jit(solution)/shard_map/unpack/pallas_call | solution.py:217
  84.8 0.1 collective-permute-done.4.refs_1_
  84.8 1.1 %unpack.3 = f32[27,96,96]{2,1,0:T(8,128)} custom-call(s32[1]{0:T(128)S(6)} %sub.3.refs_0_, bf16[1024,128]{1,0:T(8,128)(2,1)S(1)} %collective-permute-done.4.refs_1_, f32[27,96,96]{2,1,0:T(8,128)} %unpack.2.refs_2_), custom_call_target="tpu_custom_call", output_to_operand_aliasing={{}: (2, {})} | custom-call | tf_op jit(solution)/shard_map/unpack/pallas_call | solution.py:217
  (4 shorter events, 0.0 us)
Async XLA Ops:
  1.9 12.0 %collective-permute-start.2 = (bf16[2,384,128]{2,1,0:T(8,128)(2,1)S(1)}, bf16[2,384,128]{2,1,0:T(8,128)(2,1)S(1)}, u32[]{:S(2)}, u32[]{:S(2)}) collective-permute-start(bf16[2,384,128]{2,1,0:T(8,128)(2,1)S(1)} %get-tuple-element.23), channel_id=1, source_target_pairs={{0,32},{32,64},{64,96},{96,128},{128,160},{160,192},{192,224},{224... | collective-permute-start | bytes 589832 | tf_op jit(solution)/shard_map/ppermute | solution.py:250
  6.8 8.2 %collective-permute-start = (bf16[96,512]{1,0:T(8,128)(2,1)S(1)}, bf16[96,512]{1,0:T(8,128)(2,1)S(1)}, u32[]{:S(2)}, u32[]{:S(2)}) collective-permute-start(bf16[96,512]{1,0:T(8,128)(2,1)S(1)} %get-tuple-element.18), channel_id=1, source_target_pairs={{0,1},{1,2},{2,3},{3,4},{4,5},{5,6},{6,7},{7,8},{8,9},{9,10},{10,1... | collective-permute-start | bytes 294920 | tf_op jit(solution)/shard_map/ppermute | solution.py:258
  10.3 5.5 %collective-permute-start.1 = (bf16[96,512]{1,0:T(8,128)(2,1)S(1)}, bf16[96,512]{1,0:T(8,128)(2,1)S(1)}, u32[]{:S(2)}, u32[]{:S(2)}) collective-permute-start(bf16[96,512]{1,0:T(8,128)(2,1)S(1)} %get-tuple-element.19), channel_id=1, source_target_pairs={{1,0},{2,1},{3,2},{4,3},{5,4},{6,5},{7,6},{8,7},{9,8},{10,9},{11,1... | collective-permute-start | bytes 294920 | tf_op jit(solution)/shard_map/ppermute | solution.py:259
  17.5 36.3 %copy-start = (bf16[3,3,3,96,96]{4,3,2,1,0:T(8,128)(2,1)S(1)}, bf16[3,3,3,96,96]{4,3,2,1,0:T(8,128)(2,1)}, u32[]{:S(2)}) copy-start(bf16[3,3,3,96,96]{4,3,2,1,0:T(8,128)(2,1)} %param.4) | copy-start | bytes 1492996
  17.5 26.9 %all-to-all-start = ((bf16[64,32,128]{2,1,0:T(8,128)(2,1)}), bf16[64,32,128]{2,1,0:T(8,128)(2,1)S(1)}, u32[]{:S(2)}, u32[]{:S(2)}) async-start(bf16[64,32,128]{2,1,0:T(8,128)(2,1)} %bitcast.5), calls=%async_computation | async-start | bytes 1048576 | tf_op jit(solution)/shard_map/all_to_all | solution.py:290
  32.3 21.5 %collective-permute-start.3 = (bf16[576,256]{1,0:T(8,128)(2,1)S(1)}, bf16[576,256]{1,0:T(8,128)(2,1)S(1)}, u32[]{:S(2)}, u32[]{:S(2)}) collective-permute-start(bf16[576,256]{1,0:T(8,128)(2,1)S(1)} %get-tuple-element.26), channel_id=1, source_target_pairs={{32,0},{64,32},{96,64},{128,96},{160,128},{192,160},{224,192},{256... | collective-permute-start | bytes 884744 | tf_op jit(solution)/shard_map/ppermute | solution.py:280
  45.0 20.7 %all-to-all-start.1 = ((bf16[8,32,128]{2,1,0:T(8,128)(2,1)}), bf16[8,32,128]{2,1,0:T(8,128)(2,1)S(1)}, u32[]{:S(2)}, u32[]{:S(2)}) async-start(bf16[8,32,128]{2,1,0:T(8,128)(2,1)} %plane_sum.1), calls=%async_computation.1 | async-start | bytes 131072 | tf_op jit(solution)/shard_map/all_to_all | solution.py:292
  78.3 6.5 %collective-permute-start.4 = (bf16[1024,128]{1,0:T(8,128)(2,1)S(1)}, bf16[1024,128]{1,0:T(8,128)(2,1)S(1)}, u32[]{:S(2)}, u32[]{:S(2)}) collective-permute-start(bf16[1024,128]{1,0:T(8,128)(2,1)S(1)} %bitcast.8), channel_id=1, source_target_pairs={{0,32},{32,0},{1,33},{33,1},{2,34},{34,2},{3,35},{35,3},{4,36},{36... | collective-permute-start | bytes 786440 | tf_op jit(solution)/shard_map/ppermute | solution.py:295

commit v6 on v5

--- a/solution.py
+++ b/solution.py
@@ -8,7 +8,6 @@
 TM = ("y_hi", "x", "core")
 ROWS = ("y_lo", "z_pair", "z_in")
 NEAR = ("y_hi", "x", "y_lo", "z_in")
-PLANE = ("core",) + NEAR
 CH = 96
 W = 128
 F = 4
@@ -18,6 +17,7 @@
 TAP = 3 * CH
 HALF = CH // 2
 TILE = 3 * HALF
+TILES = 7
 PACKED = 1024
 F32 = jnp.float32
 BF16 = jnp.bfloat16
@@ -52,6 +52,17 @@
 def column_taps(active):
     wide = active.astype(F32)
     return jnp.concatenate([shifted(wide, -1).astype(BF16), active, shifted(wide, 1).astype(BF16)], axis=0)
+
+
+def time_taps(past, active):
+    return jnp.concatenate(
+        [
+            jnp.concatenate([past, active[:, : FW - NEXT]], axis=1),
+            jnp.concatenate([past[:, W:], active[:, : FW - W]], axis=1),
+            active,
+        ],
+        axis=0,
+    )
 
 
 def rows_of(ref, first, count):
@@ -79,15 +90,16 @@
         copy.wait()
 
 
-def cot_kernel(cot, own, bottom, top):
-    rows = dot(row_major(), frames(cot, F), ((1,), (0,))).astype(BF16)
+def cot_kernel(cot, own, bottom, top, order):
+    order[...] = row_major()
+    rows = dot(order[...], frames(cot, F), ((1,), (0,))).astype(BF16)
     own[...] = rows
     top[...] = rows[:CH]
     bottom[...] = rows[(H - 1) * CH :]
 
 
-def active_kernel(feat, act, normed, scale):
-    values = dot(row_major(), frames(feat, F), ((1,), (0,)))
+def active_kernel(feat, order, act, normed, scale):
+    values = dot(order[...], frames(feat, F), ((1,), (0,)))
     for h in range(H):
         n, scale[h] = normalize(values[h * CH : (h + 1) * CH])
         normed[h] = n
@@ -95,63 +107,55 @@
 
 
 def inner_kernel(own, act, wsum):
-    def terms(first, count, h):
-        rows = rows_of(own, first, count)
-        return [dot(rows[:, (2 - t) * W :], act[h, :, : (t + 2) * W], ((1,), (1,))) for t in range(3)]
-
-    second, third = terms(0, 3, 1), terms(1, 3, 2)
-    first, last = terms(0, 2, 0), terms(2, 2, 3)
-    for t in range(3):
-        both = second[t] + third[t]
-        wsum[t, :CH] = both[:CH] + last[t][:CH]
-        wsum[t, CH : 2 * CH] = both[CH : 2 * CH] + first[t][:CH] + last[t][CH:]
-        wsum[t, 2 * CH :] = both[2 * CH :] + first[t][CH:]
-
-
-def past_kernel(before, own, inner_sum, wsum, past_act):
-    values = dot(row_major(), frames(before, 2), ((1,), (0,)))
-    sums = [inner_sum[t] for t in range(2)]
-    zeros = jnp.zeros((CH, TAP), F32)
+    def term(first, count, h):
+        past = jnp.zeros((TAP, NEXT), BF16)
+        return dot(rows_of(own, first, count), time_taps(past, act[h]), ((1,), (1,)))
+
+    both = term(0, 3, 1) + term(1, 3, 2)
+    first, last = term(0, 2, 0), term(2, 2, 3)
+    wsum[:CH, :] = both[:CH] + last[:CH]
+    wsum[CH : 2 * CH, :] = both[CH : 2 * CH] + first[:CH] + last[CH:]
+    wsum[2 * CH :, :] = both[2 * CH :] + first[CH:]
+
+
+def past_kernel(before, own, order, inner_sum, wsum, past_act):
+    values = dot(order[...], frames(before, 2), ((1,), (0,)))
+    zeros = jnp.zeros((CH, 2 * TAP), F32)
+    early = jnp.zeros((TAP, 2 * TAP), F32)
     for h in range(H):
         n, _ = normalize(values[h * CH : (h + 1) * CH])
         past = column_taps((n * sigmoid(n)).astype(BF16))
         if h in (0, H - 1):
             past_act[h // (H - 1)] = past
+        late = jnp.concatenate([past[:, W:], jnp.zeros((TAP, W), BF16)], axis=1)
         rows = rows_of(own, max(h - 1, 0), 3 - (h in (0, H - 1)))
-        for t in range(2):
-            term = dot(rows[:, : (2 - t) * W], past[:, t * W :], ((1,), (1,)))
-            term = jnp.concatenate([zeros] * (h == 0) + [term] + [zeros] * (h == H - 1), axis=0)
-            sums[t] = sums[t] + term
-    for t in range(2):
-        wsum[t] = sums[t]
-    wsum[2] = inner_sum[2]
-
-
-def edge_kernel(above, below, own, act, past_act, wsum, packed, first_frames):
+        term = dot(rows[:, :NEXT], jnp.concatenate([past, late], axis=0), ((1,), (1,)))
+        early = early + jnp.concatenate([zeros] * (h == 0) + [term] + [zeros] * (h == H - 1), axis=0)
+    wsum[...] = inner_sum[...] + jnp.concatenate([early, jnp.zeros((TAP, TAP), F32)], axis=1)
+
+
+def edge_kernel(core, above, below, own, act, past_act, wsum, kept, given, first_frames, total):
     upper, lower = above[...], below[...]
-    first = jnp.concatenate([past_act[0], act[0]], axis=1)
-    last = jnp.concatenate([past_act[1], act[H - 1]], axis=1)
-    sums = []
-    for t in range(3):
-        from_above = dot(upper, first[:, t * W : t * W + FW], ((1,), (1,)))
-        from_below = dot(lower, last[:, t * W : t * W + FW], ((1,), (1,)))
-        sums.append(
-            jnp.concatenate([wsum[t, :CH] + from_above, wsum[t, CH : 2 * CH], wsum[t, 2 * CH :] + from_below], axis=0)
-        )
+    from_above = dot(upper, time_taps(past_act[0], act[0]), ((1,), (1,)))
+    from_below = dot(lower, time_taps(past_act[1], act[H - 1]), ((1,), (1,)))
     first_frames[:CH, :] = upper[:, :NEXT]
     first_frames[CH : 5 * CH, :] = own[:, :NEXT]
     first_frames[5 * CH :, :] = lower[:, :NEXT]
-    for half in range(2):
-        picked = [
-            jnp.concatenate([total[k * CH + half * HALF : k * CH + (half + 1) * HALF] for k in range(3)], axis=0)
-            for total in sums
-        ]
-        for t in range(3):
-            for j in range(2):
-                packed[half, (2 * t + j) * TILE : (2 * t + j + 1) * TILE, :] = picked[t][:, j * W : (j + 1) * W].astype(BF16)
-        rests = [total[:, 2 * W :] for total in picked] + [jnp.zeros((TILE, W - CH), F32)]
-        packed[half, 6 * TILE : 7 * TILE, :] = jnp.concatenate(rests, axis=1).astype(BF16)
-        packed[half, 7 * TILE :, :] = jnp.zeros((PACKED - 7 * TILE, W), BF16)
+    total[:CH, : 3 * TAP] = wsum[:CH] + from_above
+    total[CH : 2 * CH, : 3 * TAP] = wsum[CH : 2 * CH]
+    total[2 * CH :, : 3 * TAP] = wsum[2 * CH :] + from_below
+    total[:, 3 * TAP :] = jnp.zeros((TAP, TILES * W - 3 * TAP), F32)
+    for out, half in ((given, 1 - core[0]), (kept, core[0])):
+        for k in range(3):
+            rows = pl.ds(pl.multiple_of(k * CH + half * HALF, HALF), HALF)
+            for j in range(TILES):
+                tile = total[rows, j * W : (j + 1) * W]
+                out[j * TILE + k * HALF : j * TILE + (k + 1) * HALF, :] = tile.astype(out.dtype)
+        out[TILES * TILE :, :] = jnp.zeros((PACKED - TILES * TILE, W), out.dtype)
+
+
+def add_kernel(kept, received, out):
+    out[...] = (kept[...] + received[...].astype(F32)).astype(BF16)
 
 
 def input_kernel(above, below, own, later, normed, scale, weights, grad_out, done):
@@ -195,15 +199,12 @@
 
 def unpack_kernel(norm_factor, half, packed, *refs):
     out, held, sems = refs[-3:]
-    rests = packed[6 * TILE : 7 * TILE, :].astype(F32)
-    width = TAP - 2 * W
     place = pl.multiple_of(half[0] * HALF, HALF)
+    block = jnp.concatenate([packed[j * TILE : (j + 1) * TILE, :].astype(F32) for j in range(TILES)], axis=1) * norm_factor
     copies = []
     for t in range(3):
-        tiles = [packed[(2 * t + j) * TILE : (2 * t + j + 1) * TILE, :].astype(F32) for j in range(2)]
-        block = jnp.concatenate(tiles + [rests[:, t * width : (t + 1) * width]], axis=1) * norm_factor
         for c in range(3):
-            column = block[:, c * CH : (c + 1) * CH]
+            column = block[:, (t * 3 + c) * CH : (t * 3 + c + 1) * CH]
             for k in range(3):
                 held[t, (2 - k) * 3 + c] = column[k * HALF : (k + 1) * HALF]
         copies.append(pltpu.make_async_copy(held.at[t], out.at[pl.ds(t * 9, 9), pl.ds(place, HALF)], sems.at[t]))
@@ -212,13 +213,13 @@
         copy.wait()
 
 
-def call(kernel, name, outs, args, flops=0, smem=(), after=(), out_hbm=False, scratch=(), aliases={}):
+def call(kernel, name, outs, args, flops=0, smem=(), after=(), out_hbm=(), scratch=(), aliases={}):
     vmem, anywhere = pl.BlockSpec(memory_space=pltpu.VMEM), pl.BlockSpec(memory_space=pl.ANY)
     return pl.pallas_call(
         kernel,
         out_shape=tuple(jax.ShapeDtypeStruct(shape, dtype) for shape, dtype in outs),
         in_specs=[pl.BlockSpec(memory_space=pltpu.SMEM)] * len(smem) + [vmem] * len(args) + [anywhere] * len(after),
-        out_specs=(anywhere if out_hbm else vmem,) * len(outs),
+        out_specs=tuple(anywhere if i in out_hbm else vmem for i in range(len(outs))),
         scratch_shapes=scratch,
         input_output_aliases=aliases,
         compiler_params=pltpu.CompilerParams(vmem_limit_bytes=16 << 20),
@@ -233,7 +234,7 @@
 
 def local(features, weights, cotangent):
     tm, rows = lax.axis_size(TM), lax.axis_size(ROWS)
-    plane, depth = lax.axis_size(PLANE), lax.axis_size("z_pair")
+    near, depth = lax.axis_size(NEAR), lax.axis_size("z_pair")
     cells = F * tm * H * rows * W
     features = features.reshape(F, CH * H, W)
     cotangent = cotangent.reshape(F, CH * H, W)
@@ -248,10 +249,10 @@
         scratch=[pltpu.SemaphoreType.DMA((3,))],
     )
     before = lax.ppermute(last_frames, TM, forward)
-    own, bottom, top = call(
+    own, bottom, top, order = call(
         cot_kernel,
         "cot_rows",
-        [((H * CH, FW), BF16), ((CH, FW), BF16), ((CH, FW), BF16)],
+        [((H * CH, FW), BF16), ((CH, FW), BF16), ((CH, FW), BF16), ((H * CH, H * CH), BF16)],
         (cotangent,),
         1 << 33,
     )
@@ -261,22 +262,25 @@
         active_kernel,
         "active",
         [((H, TAP, FW), BF16), ((H, CH, FW), F32), ((H, 1, FW), F32)],
-        (features,),
-    )
-    (wsum,) = call(inner_kernel, "own_cells", [((3, TAP, TAP), F32)], (own, act))
+        (features, order),
+    )
+    (wsum,) = call(inner_kernel, "own_cells", [((TAP, 3 * TAP), F32)], (own, act))
     wsum, past_act = call(
         past_kernel,
         "frames_before",
-        [((3, TAP, TAP), F32), ((2, TAP, NEXT), BF16)],
-        (before, own, wsum),
-    )
-    packed, first_frames = call(
+        [((TAP, 3 * TAP), F32), ((2, TAP, NEXT), BF16)],
+        (before, own, order, wsum),
+    )
+    core = lax.axis_index("core").astype(jnp.int32).reshape(1)
+    kept, given, first_frames = call(
         edge_kernel,
         "edge_rows",
-        [((2, PACKED, W), BF16), (((H + 2) * CH, NEXT), BF16)],
+        [((PACKED, W), F32), ((PACKED, W), BF16), (((H + 2) * CH, NEXT), BF16)],
         (above, below, own, act, past_act, wsum),
-        1 << 30,
-    )
+        smem=(core,),
+        scratch=[pltpu.VMEM((TAP, TILES * W), F32)],
+    )
+    received = lax.ppermute(given, "core", [(0, 1), (1, 0)])
     later = lax.ppermute(first_frames, TM, back)
     input_grad, done = call(
         input_kernel,
@@ -286,15 +290,14 @@
         1 << 31,
     )
 
-    part = 2 * PACKED // plane
-    parts = lax.all_to_all(packed.reshape(plane, part, W), PLANE, 0, 0)
+    (packed,) = call(add_kernel, "core_sum", [((PACKED, W), BF16)], (kept, received))
+    parts = lax.all_to_all(packed.reshape(near, PACKED // near, W), NEAR, 0, 0)
     slabs = sum_to_slots(parts, depth, "plane_sum")
     slabs = lax.all_to_all(slabs, "z_pair", 0, 0)
-    slots = sum_to_slots(slabs, plane // 2, "depth_sum", after=(done,))
+    slots = sum_to_slots(slabs, near, "depth_sum", after=(done,))
     own_half = lax.all_to_all(slots, NEAR, 0, 0).reshape(PACKED, W)
     other_half = lax.ppermute(own_half, "core", [(0, 1), (1, 0)])
 
-    core = lax.axis_index("core").astype(jnp.int32).reshape(1)
     weight_grad = ()
     for half, values in ((core, own_half), (1 - core, other_half)):
         weight_grad = call(
@@ -304,7 +307,7 @@
             (values,),
             smem=(half,),
             after=weight_grad,
-            out_hbm=True,
+            out_hbm=(0,),
             scratch=[pltpu.VMEM((3, 9, HALF, CH), F32), pltpu.SemaphoreType.DMA((3,))],
             aliases={2: 0} if weight_grad else {},
         )

time: 86.4 us -> 85.6 us (level)
  starting transfers between devices: 40.5 us -> 43 us
  waiting for transfers between devices: 19.6 us -> 18.1 us
  blocking collectives: 12.6 us -> 11.4 us
    ppermute x0 -> x1, starting transfers between devices: none -> 4.43 us  [local(): received = lax.ppermute(given, 'core', [(0, 1), (1, 0)])]
    all_to_all x1, waiting for transfers between devices: 9.74 us -> 6.45 us  [local(): parts = lax.all_to_all(packed.reshape(near, PACKED // near, W), NEAR, 0, 0)]
    all_to_all x1, starting transfers between devices: 14.8 us -> 11.9 us  [local(): parts = lax.all_to_all(packed.reshape(near, PACKED // near, W), NEAR, 0, 0)]
    all_to_all x1, blocking collectives: 12.6 us -> 11.4 us  [local(): own_half = lax.all_to_all(slots, NEAR, 0, 0).reshape(PACKED, W)]
    ppermute x0 -> x1, waiting for transfers between devices: none -> 1.14 us  [local(): received = lax.ppermute(given, 'core', [(0, 1), (1, 0)])]
    ppermute x1, starting transfers between devices: 5.37 us -> 6.32 us  [local(): other_half = lax.ppermute(own_half, 'core', [(0, 1), (1, 0)])]
    pallas_call x11 -> x12, Pallas kernels: 12.4 us -> 11.9 us  [call(): pl.pallas_call(kernel, out_shape=tuple((jax.ShapeDtypeStruct(shape, dtype...]
  transfers between devices with their start and end apart: 7 -> 8, of which waited for: 4 -> 5; matrix products, arithmetic and copies ran while one was open for 0% -> 0% of each run, Pallas kernels for 10% -> 10%
where the time goes in v6:
time: 85.6 us; the launch traced here: 85.1 us
  starting transfers between devices  43 us (50%)
  waiting for transfers between devices  18.1 us (21%)
  Pallas kernels  11.9 us (14%)
  blocking collectives  11.4 us (13%)
    pallas_call x12, Pallas kernels, call(): pl.pallas_call(kernel, out_shape=tuple((jax.ShapeDtypeStruct(shape, dtype...  11.9 us
    all_to_all x1, starting transfers between devices, local(): parts = lax.all_to_all(packed.reshape(near, PACKED // near, W), NEAR, 0, 0)  11.9 us
    all_to_all x1, blocking collectives, local(): own_half = lax.all_to_all(slots, NEAR, 0, 0).reshape(PACKED, W)  11.4 us
    all_to_all x1, waiting for transfers between devices, local(): slabs = lax.all_to_all(slabs, 'z_pair', 0, 0)  9.26 us
    all_to_all x1, starting transfers between devices, local(): slabs = lax.all_to_all(slabs, 'z_pair', 0, 0)  8.67 us
    all_to_all x1, waiting for transfers between devices, local(): parts = lax.all_to_all(packed.reshape(near, PACKED // near, W), NEAR, 0, 0)  6.45 us
    ppermute x1, starting transfers between devices, local(): other_half = lax.ppermute(own_half, 'core', [(0, 1), (1, 0)])  6.32 us
    ppermute x1, starting transfers between devices, local(): before = lax.ppermute(last_frames, TM, forward)  4.51 us
  transfers between devices with their start and end apart: 8, of which 5 were waited for; matrix products, arithmetic and copies ran while one was open for 0% of the time, Pallas kernels for 10%

profile of v6, /device:TPU:1, one launch (start us, length us, event | category | flops | bytes accessed | tf_op | source)
XLA Modules:
  0.0 85.1 jit_solution(14199913430089631944)
XLA Ops:
  0.6 1.2 %load.1 = (bf16[2,384,128]{2,1,0:T(8,128)(2,1)S(1)}, bf16[4,384,128]{2,1,0:T(8,128)(2,1)S(1)}, bf16[4,384,128]{2,1,0:T(8,128)(2,1)S(1)}) custom-call(bf16[4,384,128]{2,1,0:T(8,128)(2,1)} %bitcast.12, bf16[4,384,128]{2,1,0:T(8,128)(2,1)} %bitcast.13), custom_call_target="tpu_custom_call" | custom-call | tf_op jit(solution)/shard_map/load/pallas_call | solution.py:218
  1.9 4.5 %collective-permute-start.2 = (bf16[2,384,128]{2,1,0:T(8,128)(2,1)S(1)}, bf16[2,384,128]{2,1,0:T(8,128)(2,1)S(1)}, u32[]{:S(2)}, u32[]{:S(2)}) collective-permute-start(bf16[2,384,128]{2,1,0:T(8,128)(2,1)S(1)} %get-tuple-element.26), channel_id=1, source_target_pairs={{0,32},{32,64},{64,96},{96,128},{128,160},{160,192},{192,224},{224... | collective-permute-start | bytes 589832 | tf_op jit(solution)/shard_map/ppermute | solution.py:251
  6.4 0.4 cot_rows.1
  6.8 3.5 %collective-permute-start = (bf16[96,512]{1,0:T(8,128)(2,1)S(1)}, bf16[96,512]{1,0:T(8,128)(2,1)S(1)}, u32[]{:S(2)}, u32[]{:S(2)}) collective-permute-start(bf16[96,512]{1,0:T(8,128)(2,1)S(1)} %get-tuple-element.20), channel_id=1, source_target_pairs={{0,1},{1,2},{2,3},{3,4},{4,5},{5,6},{6,7},{7,8},{8,9},{9,10},{10,1... | collective-permute-start | bytes 294920 | tf_op jit(solution)/shard_map/ppermute | solution.py:259
  10.4 1.3 %collective-permute-start.1 = (bf16[96,512]{1,0:T(8,128)(2,1)S(1)}, bf16[96,512]{1,0:T(8,128)(2,1)S(1)}, u32[]{:S(2)}, u32[]{:S(2)}) collective-permute-start(bf16[96,512]{1,0:T(8,128)(2,1)S(1)} %get-tuple-element.21), channel_id=1, source_target_pairs={{1,0},{2,1},{3,2},{4,3},{5,4},{6,5},{7,6},{8,7},{9,8},{10,9},{11,1... | collective-permute-start | bytes 294920 | tf_op jit(solution)/shard_map/ppermute | solution.py:260
  11.7 0.8 active.1
  12.4 1.3 %own_cells.1.inner_sum = f32[288,864]{1,0:T(8,128)S(1)} custom-call(bf16[384,512]{1,0:T(8,128)(2,1)S(1)} %get-tuple-element.22.own, bf16[4,288,512]{2,1,0:T(8,128)(2,1)S(1)} %get-tuple-element.25.act), custom_call_target="tpu_custom_call" | custom-call | tf_op jit(solution)/shard_map/own_cells/pallas_call | solution.py:218
  13.7 1.1 %frames_before.1 = (f32[288,864]{1,0:T(8,128)S(1)}, bf16[2,288,256]{2,1,0:T(8,128)(2,1)S(1)}) custom-call(bf16[2,384,128]{2,1,0:T(8,128)(2,1)S(1)} %collective-permute-done.2.before, bf16[384,512]{1,0:T(8,128)(2,1)S(1)} %get-tuple-element.22.own, bf16[384,384]{1,0:T(8,128)(2,1)S(1)} %get-tuple-element.24.order, f32[288,864]{1,0:T(8,128)S(1)} %own_cells.1.inner_sum), custom_call_target="tpu_custom_call" | custom-call | tf_op jit(solution)/shard_map/frames_before/pallas_call | solution.py:218
  14.8 1.1 %collective-permute-done.1.below = bf16[96,512]{1,0:T(8,128)(2,1)S(1)} collective-permute-done((bf16[96,512]{1,0:T(8,128)(2,1)S(1)}, bf16[96,512]{1,0:T(8,128)(2,1)S(1)}, u32[]{:S(2)}, u32[]{:S(2)}) %collective-permute-start.1) | collective-permute-done | bytes 98336 | tf_op jit(solution)/shard_map/ppermute | solution.py:260
  15.9 0.7 edge_rows.1
  16.6 4.4 %collective-permute-start.4 = (bf16[1024,128]{1,0:T(8,128)(2,1)S(1)}, bf16[1024,128]{1,0:T(8,128)(2,1)S(1)}, u32[]{:S(2)}, u32[]{:S(2)}) collective-permute-start(bf16[1024,128]{1,0:T(8,128)(2,1)S(1)} %get-tuple-element.34), channel_id=1, source_target_pairs={{0,32},{32,0},{1,33},{33,1},{2,34},{34,2},{3,35},{35,3},{4,36},{36... | collective-permute-start | bytes 786440 | tf_op jit(solution)/shard_map/ppermute | solution.py:283
  21.1 1.1 %collective-permute-done.4.received = bf16[1024,128]{1,0:T(8,128)(2,1)S(1)} collective-permute-done((bf16[1024,128]{1,0:T(8,128)(2,1)S(1)}, bf16[1024,128]{1,0:T(8,128)(2,1)S(1)}, u32[]{:S(2)}, u32[]{:S(2)}) %collective-permute-start.4) | collective-permute-done | bytes 262176 | tf_op jit(solution)/shard_map/ppermute | solution.py:283
  22.2 0.7 core_sum.1
  22.9 11.9 %all-to-all-start = ((bf16[32,32,128]{2,1,0:T(8,128)(2,1)}), bf16[32,32,128]{2,1,0:T(8,128)(2,1)S(1)}, u32[]{:S(2)}, u32[]{:S(2)}) async-start(bf16[32,32,128]{2,1,0:T(8,128)(2,1)} %bitcast.5), calls=%async_computation | async-start | bytes 524288 | tf_op jit(solution)/shard_map/all_to_all | solution.py:294
  34.8 2.3 %collective-permute-start.3 = (bf16[576,256]{1,0:T(8,128)(2,1)S(1)}, bf16[576,256]{1,0:T(8,128)(2,1)S(1)}, u32[]{:S(2)}, u32[]{:S(2)}) collective-permute-start(bf16[576,256]{1,0:T(8,128)(2,1)S(1)} %get-tuple-element.29), channel_id=1, source_target_pairs={{32,0},{64,32},{96,64},{128,96},{160,128},{192,160},{224,192},{256... | collective-permute-start | bytes 884744 | tf_op jit(solution)/shard_map/ppermute | solution.py:284
  37.2 6.5 %all-to-all-done.parts = bf16[32,32,128]{2,1,0:T(8,128)(2,1)S(1)} async-done(((bf16[32,32,128]{2,1,0:T(8,128)(2,1)}), bf16[32,32,128]{2,1,0:T(8,128)(2,1)S(1)}, u32[]{:S(2)}, u32[]{:S(2)}) %all-to-all-start) | async-done | bytes 262176 | tf_op jit(solution)/shard_map/all_to_all | solution.py:294
  43.6 0.7 plane_sum.1
  44.3 8.7 %all-to-all-start.1 = ((bf16[8,32,128]{2,1,0:T(8,128)(2,1)}), bf16[8,32,128]{2,1,0:T(8,128)(2,1)S(1)}, u32[]{:S(2)}, u32[]{:S(2)}) async-start(bf16[8,32,128]{2,1,0:T(8,128)(2,1)} %plane_sum.1), calls=%async_computation.1 | async-start | bytes 131072 | tf_op jit(solution)/shard_map/all_to_all | solution.py:296
  53.0 3.0 %input_grad.1 = (bf16[4,384,128]{2,1,0:T(8,128)(2,1)}, f32[8,128]{1,0:T(8,128)S(1)}) custom-call(bf16[96,512]{1,0:T(8,128)(2,1)S(1)} %collective-permute-done.above, bf16[96,512]{1,0:T(8,128)(2,1)S(1)} %collective-permute-done.1.below, bf16[384,512]{1,0:T(8,128)(2,1)S(1)} %get-tuple-element.22.own, bf16[576,256]{1,0:T(8,128)(2,1)S(1)} %collective-permute-done.3.later, ...), custom_call_target="tpu_custom_call" | custom-call | flops 2147483648 | tf_op jit(solution)/shard_map/input_grad/pallas_call | solution.py:218
  56.0 9.3 %all-to-all-done.1.parts = bf16[8,32,128]{2,1,0:T(8,128)(2,1)S(1)} async-done(((bf16[8,32,128]{2,1,0:T(8,128)(2,1)}), bf16[8,32,128]{2,1,0:T(8,128)(2,1)S(1)}, u32[]{:S(2)}, u32[]{:S(2)}) %all-to-all-start.1) | async-done | bytes 65568 | tf_op jit(solution)/shard_map/all_to_all | solution.py:296
  65.3 11.4 %all_to_all.15 = bf16[32,32,128]{2,1,0:T(8,128)(2,1)S(1)} all-to-all(bf16[32,32,128]{2,1,0:T(8,128)(2,1)S(1)} %depth_sum.1), channel_id=1, replica_groups=mesh['y_hi'=2,'x'=4,'core'=2,'y_lo'=2,'z_pair'=8,'z_in'=2] {'y_hi','x','..., dimensions={0} | all-to-all | bytes 524288 | tf_op jit(solution)/shard_map/all_to_all | solution.py:298
  76.7 6.3 %collective-permute-start.5 = (bf16[1024,128]{1,0:T(8,128)(2,1)S(1)}, bf16[1024,128]{1,0:T(8,128)(2,1)S(1)}, u32[]{:S(2)}, u32[]{:S(2)}) collective-permute-start(bf16[1024,128]{1,0:T(8,128)(2,1)S(1)} %bitcast.8), channel_id=1, source_target_pairs={{0,32},{32,0},{1,33},{33,1},{2,34},{34,2},{3,35},{35,3},{4,36},{36... | collective-permute-start | bytes 786440 | tf_op jit(solution)/shard_map/ppermute | solution.py:299
  83.0 1.0 %unpack.2.refs_2_ = f32[27,96,96]{2,1,0:T(8,128)} custom-call(s32[1]{0:T(128)} %bitcast.2.core.refs_0_, bf16[1024,128]{1,0:T(8,128)(2,1)S(1)} %bitcast.9), custom_call_target="tpu_custom_call" | custom-call | tf_op jit(solution)/shard_map/unpack/pallas_call | solution.py:218
  84.1 1.0 %unpack.3 = f32[27,96,96]{2,1,0:T(8,128)} custom-call(s32[1]{0:T(128)S(6)} %sub.3.refs_0_, bf16[1024,128]{1,0:T(8,128)(2,1)S(1)} %collective-permute-done.5.refs_1_, f32[27,96,96]{2,1,0:T(8,128)} %unpack.2.refs_2_), custom_call_target="tpu_custom_call", output_to_operand_aliasing={{}: (2, {})} | custom-call | tf_op jit(solution)/shard_map/unpack/pallas_call | solution.py:218
  (7 shorter events, 0.2 us)
Async XLA Ops:
  1.9 11.8 %collective-permute-start.2 = (bf16[2,384,128]{2,1,0:T(8,128)(2,1)S(1)}, bf16[2,384,128]{2,1,0:T(8,128)(2,1)S(1)}, u32[]{:S(2)}, u32[]{:S(2)}) collective-permute-start(bf16[2,384,128]{2,1,0:T(8,128)(2,1)S(1)} %get-tuple-element.26), channel_id=1, source_target_pairs={{0,32},{32,64},{64,96},{96,128},{128,160},{160,192},{192,224},{224... | collective-permute-start | bytes 589832 | tf_op jit(solution)/shard_map/ppermute | solution.py:251
  6.8 8.0 %collective-permute-start = (bf16[96,512]{1,0:T(8,128)(2,1)S(1)}, bf16[96,512]{1,0:T(8,128)(2,1)S(1)}, u32[]{:S(2)}, u32[]{:S(2)}) collective-permute-start(bf16[96,512]{1,0:T(8,128)(2,1)S(1)} %get-tuple-element.20), channel_id=1, source_target_pairs={{0,1},{1,2},{2,3},{3,4},{4,5},{5,6},{6,7},{7,8},{8,9},{9,10},{10,1... | collective-permute-start | bytes 294920 | tf_op jit(solution)/shard_map/ppermute | solution.py:259
  10.4 5.5 %collective-permute-start.1 = (bf16[96,512]{1,0:T(8,128)(2,1)S(1)}, bf16[96,512]{1,0:T(8,128)(2,1)S(1)}, u32[]{:S(2)}, u32[]{:S(2)}) collective-permute-start(bf16[96,512]{1,0:T(8,128)(2,1)S(1)} %get-tuple-element.21), channel_id=1, source_target_pairs={{1,0},{2,1},{3,2},{4,3},{5,4},{6,5},{7,6},{8,7},{9,8},{10,9},{11,1... | collective-permute-start | bytes 294920 | tf_op jit(solution)/shard_map/ppermute | solution.py:260
  16.6 36.4 %copy-start = (bf16[3,3,3,96,96]{4,3,2,1,0:T(8,128)(2,1)S(1)}, bf16[3,3,3,96,96]{4,3,2,1,0:T(8,128)(2,1)}, u32[]{:S(2)}) copy-start(bf16[3,3,3,96,96]{4,3,2,1,0:T(8,128)(2,1)} %param.4) | copy-start | bytes 1492996
  16.6 5.6 %collective-permute-start.4 = (bf16[1024,128]{1,0:T(8,128)(2,1)S(1)}, bf16[1024,128]{1,0:T(8,128)(2,1)S(1)}, u32[]{:S(2)}, u32[]{:S(2)}) collective-permute-start(bf16[1024,128]{1,0:T(8,128)(2,1)S(1)} %get-tuple-element.34), channel_id=1, source_target_pairs={{0,32},{32,0},{1,33},{33,1},{2,34},{34,2},{3,35},{35,3},{4,36},{36... | collective-permute-start | bytes 786440 | tf_op jit(solution)/shard_map/ppermute | solution.py:283
  22.9 20.7 %all-to-all-start = ((bf16[32,32,128]{2,1,0:T(8,128)(2,1)}), bf16[32,32,128]{2,1,0:T(8,128)(2,1)S(1)}, u32[]{:S(2)}, u32[]{:S(2)}) async-start(bf16[32,32,128]{2,1,0:T(8,128)(2,1)} %bitcast.5), calls=%async_computation | async-start | bytes 524288 | tf_op jit(solution)/shard_map/all_to_all | solution.py:294
  34.8 18.2 %collective-permute-start.3 = (bf16[576,256]{1,0:T(8,128)(2,1)S(1)}, bf16[576,256]{1,0:T(8,128)(2,1)S(1)}, u32[]{:S(2)}, u32[]{:S(2)}) collective-permute-start(bf16[576,256]{1,0:T(8,128)(2,1)S(1)} %get-tuple-element.29), channel_id=1, source_target_pairs={{32,0},{64,32},{96,64},{128,96},{160,128},{192,160},{224,192},{256... | collective-permute-start | bytes 884744 | tf_op jit(solution)/shard_map/ppermute | solution.py:284
  44.3 21.0 %all-to-all-start.1 = ((bf16[8,32,128]{2,1,0:T(8,128)(2,1)}), bf16[8,32,128]{2,1,0:T(8,128)(2,1)S(1)}, u32[]{:S(2)}, u32[]{:S(2)}) async-start(bf16[8,32,128]{2,1,0:T(8,128)(2,1)} %plane_sum.1), calls=%async_computation.1 | async-start | bytes 131072 | tf_op jit(solution)/shard_map/all_to_all | solution.py:296
  76.7 7.5 %collective-permute-start.5 = (bf16[1024,128]{1,0:T(8,128)(2,1)S(1)}, bf16[1024,128]{1,0:T(8,128)(2,1)S(1)}, u32[]{:S(2)}, u32[]{:S(2)}) collective-permute-start(bf16[1024,128]{1,0:T(8,128)(2,1)S(1)} %bitcast.8), channel_id=1, source_target_pairs={{0,32},{32,0},{1,33},{33,1},{2,34},{34,2},{3,35},{35,3},{4,36},{36... | collective-permute-start | bytes 786440 | tf_op jit(solution)/shard_map/ppermute | solution.py:299

commit v7 on v6

--- a/solution.py
+++ b/solution.py
@@ -154,8 +154,8 @@
         out[TILES * TILE :, :] = jnp.zeros((PACKED - TILES * TILE, W), out.dtype)
 
 
-def add_kernel(kept, received, out):
-    out[...] = (kept[...] + received[...].astype(F32)).astype(BF16)
+def add_kernel(core, kept, exchanged, out):
+    out[...] = (kept[...] + exchanged[1 - core[0]].astype(F32)).astype(BF16)
 
 
 def input_kernel(above, below, own, later, normed, scale, weights, grad_out, done):
@@ -197,17 +197,20 @@
         out[i] = total
 
 
-def unpack_kernel(norm_factor, half, packed, *refs):
-    out, held, sems = refs[-3:]
-    place = pl.multiple_of(half[0] * HALF, HALF)
-    block = jnp.concatenate([packed[j * TILE : (j + 1) * TILE, :].astype(F32) for j in range(TILES)], axis=1) * norm_factor
+def unpack_kernel(norm_factor, packed, out, held, sems):
     copies = []
+    blocks = [
+        jnp.concatenate([packed[half, j * TILE : (j + 1) * TILE, :].astype(F32) for j in range(TILES)], axis=1)
+        * norm_factor
+        for half in range(2)
+    ]
     for t in range(3):
         for c in range(3):
-            column = block[:, (t * 3 + c) * CH : (t * 3 + c + 1) * CH]
-            for k in range(3):
-                held[t, (2 - k) * 3 + c] = column[k * HALF : (k + 1) * HALF]
-        copies.append(pltpu.make_async_copy(held.at[t], out.at[pl.ds(t * 9, 9), pl.ds(place, HALF)], sems.at[t]))
+            for half in range(2):
+                column = blocks[half][:, (t * 3 + c) * CH : (t * 3 + c + 1) * CH]
+                for k in range(3):
+                    held[t * 9 + (2 - k) * 3 + c, half * HALF : (half + 1) * HALF] = column[k * HALF : (k + 1) * HALF]
+        copies.append(pltpu.make_async_copy(held.at[pl.ds(t * 9, 9)], out.at[pl.ds(t * 9, 9)], sems.at[t]))
         copies[-1].start()
     for copy in copies:
         copy.wait()
@@ -280,7 +283,7 @@
         smem=(core,),
         scratch=[pltpu.VMEM((TAP, TILES * W), F32)],
     )
-    received = lax.ppermute(given, "core", [(0, 1), (1, 0)])
+    exchanged = lax.all_gather(given, "core")
     later = lax.ppermute(first_frames, TM, back)
     input_grad, done = call(
         input_kernel,
@@ -290,28 +293,22 @@
         1 << 31,
     )
 
-    (packed,) = call(add_kernel, "core_sum", [((PACKED, W), BF16)], (kept, received))
+    (packed,) = call(add_kernel, "core_sum", [((PACKED, W), BF16)], (kept, exchanged), smem=(core,))
     parts = lax.all_to_all(packed.reshape(near, PACKED // near, W), NEAR, 0, 0)
     slabs = sum_to_slots(parts, depth, "plane_sum")
     slabs = lax.all_to_all(slabs, "z_pair", 0, 0)
     slots = sum_to_slots(slabs, near, "depth_sum", after=(done,))
     own_half = lax.all_to_all(slots, NEAR, 0, 0).reshape(PACKED, W)
-    other_half = lax.ppermute(own_half, "core", [(0, 1), (1, 0)])
-
-    weight_grad = ()
-    for half, values in ((core, own_half), (1 - core, other_half)):
-        weight_grad = call(
-            lambda *refs: unpack_kernel(1.0 / float(cells) ** 0.5, *refs),
-            "unpack",
-            [((27, CH, CH), F32)],
-            (values,),
-            smem=(half,),
-            after=weight_grad,
-            out_hbm=(0,),
-            scratch=[pltpu.VMEM((3, 9, HALF, CH), F32), pltpu.SemaphoreType.DMA((3,))],
-            aliases={2: 0} if weight_grad else {},
-        )
-    return (input_grad.reshape(F, CH, H, W), weight_grad[0].reshape(3, 3, 3, CH, CH))
+    whole = lax.all_gather(own_half, "core")
+    (weight_grad,) = call(
+        lambda *refs: unpack_kernel(1.0 / float(cells) ** 0.5, *refs),
+        "unpack",
+        [((27, CH, CH), F32)],
+        (whole,),
+        out_hbm=(0,),
+        scratch=[pltpu.VMEM((27, CH, CH), F32), pltpu.SemaphoreType.DMA((3,))],
+    )
+    return (input_grad.reshape(F, CH, H, W), weight_grad.reshape(3, 3, 3, CH, CH))
 
 
 def solution(mesh):

time: 85.6 us -> 83.2 us (0.972)
  starting transfers between devices: 43 us -> 32.2 us
  blocking collectives: 11.4 us -> 21.8 us
  waiting for transfers between devices: 18.1 us -> 16.8 us
    ppermute x2 -> x0, starting transfers between devices: 10.8 us -> none  [the longest x1 6.32 us: local(): other_half = lax.ppermute(own_half, 'core', [(0, 1), (1, 0)])]
    all_gather x0 -> x2, blocking collectives: none -> 10.4 us  [the longest x1 6.22 us: local(): whole = lax.all_gather(own_half, 'core')]
    ppermute x2 -> x0, waiting for transfers between devices: 1.27 us -> none  [the longest x1 1.14 us: local(): received = lax.ppermute(given, 'core', [(0, 1), (1, 0)])]
    pallas_call x12 -> x11, Pallas kernels: 11.9 us -> 11.2 us  [call(): pl.pallas_call(kernel, out_shape=tuple((jax.ShapeDtypeStruct(shape, dtype...]
  transfers between devices with their start and end apart: 8 -> 6, of which waited for: 5 -> 3; matrix products, arithmetic and copies ran while one was open for 0% -> 0% of each run, Pallas kernels for 10% -> 9%
where the time goes in v7:
time: 83.2 us; the launch traced here: 82.8 us
  starting transfers between devices  32.2 us (39%)
  blocking collectives  21.8 us (26%)
  waiting for transfers between devices  16.8 us (20%)
  Pallas kernels  11.2 us (13%)
    all_to_all x1, starting transfers between devices, local(): parts = lax.all_to_all(packed.reshape(near, PACKED // near, W), NEAR, 0, 0)  11.9 us
    all_to_all x1, blocking collectives, local(): own_half = lax.all_to_all(slots, NEAR, 0, 0).reshape(PACKED, W)  11.4 us
    pallas_call x11, Pallas kernels, call(): pl.pallas_call(kernel, out_shape=tuple((jax.ShapeDtypeStruct(shape, dtype...  11.2 us
    all_to_all x1, waiting for transfers between devices, local(): slabs = lax.all_to_all(slabs, 'z_pair', 0, 0)  9.27 us
    all_to_all x1, starting transfers between devices, local(): slabs = lax.all_to_all(slabs, 'z_pair', 0, 0)  8.67 us
    all_to_all x1, waiting for transfers between devices, local(): parts = lax.all_to_all(packed.reshape(near, PACKED // near, W), NEAR, 0, 0)  6.45 us
    all_gather x1, blocking collectives, local(): whole = lax.all_gather(own_half, 'core')  6.22 us
    ppermute x1, starting transfers between devices, local(): before = lax.ppermute(last_frames, TM, forward)  4.51 us
  transfers between devices with their start and end apart: 6, of which 3 were waited for; matrix products, arithmetic and copies ran while one was open for 0% of the time, Pallas kernels for 9%

profile of v7, /device:TPU:1, one launch (start us, length us, event | category | flops | bytes accessed | tf_op | source)
XLA Modules:
  0.0 82.8 jit_solution(78107235027222000)
XLA Ops:
  0.6 1.2 %load.1 = (bf16[2,384,128]{2,1,0:T(8,128)(2,1)S(1)}, bf16[4,384,128]{2,1,0:T(8,128)(2,1)S(1)}, bf16[4,384,128]{2,1,0:T(8,128)(2,1)S(1)}) custom-call(bf16[4,384,128]{2,1,0:T(8,128)(2,1)} %bitcast.13, bf16[4,384,128]{2,1,0:T(8,128)(2,1)} %bitcast.14), custom_call_target="tpu_custom_call" | custom-call | tf_op jit(solution)/shard_map/load/pallas_call | solution.py:221
  1.9 4.5 %collective-permute-start.2 = (bf16[2,384,128]{2,1,0:T(8,128)(2,1)S(1)}, bf16[2,384,128]{2,1,0:T(8,128)(2,1)S(1)}, u32[]{:S(2)}, u32[]{:S(2)}) collective-permute-start(bf16[2,384,128]{2,1,0:T(8,128)(2,1)S(1)} %get-tuple-element.26), channel_id=1, source_target_pairs={{0,32},{32,64},{64,96},{96,128},{128,160},{160,192},{192,224},{224... | collective-permute-start | bytes 589832 | tf_op jit(solution)/shard_map/ppermute | solution.py:254
  6.4 0.4 cot_rows.1
  6.8 3.5 %collective-permute-start = (bf16[96,512]{1,0:T(8,128)(2,1)S(1)}, bf16[96,512]{1,0:T(8,128)(2,1)S(1)}, u32[]{:S(2)}, u32[]{:S(2)}) collective-permute-start(bf16[96,512]{1,0:T(8,128)(2,1)S(1)} %get-tuple-element.20), channel_id=1, source_target_pairs={{0,1},{1,2},{2,3},{3,4},{4,5},{5,6},{6,7},{7,8},{8,9},{9,10},{10,1... | collective-permute-start | bytes 294920 | tf_op jit(solution)/shard_map/ppermute | solution.py:262
  10.4 1.3 %collective-permute-start.1 = (bf16[96,512]{1,0:T(8,128)(2,1)S(1)}, bf16[96,512]{1,0:T(8,128)(2,1)S(1)}, u32[]{:S(2)}, u32[]{:S(2)}) collective-permute-start(bf16[96,512]{1,0:T(8,128)(2,1)S(1)} %get-tuple-element.21), channel_id=1, source_target_pairs={{1,0},{2,1},{3,2},{4,3},{5,4},{6,5},{7,6},{8,7},{9,8},{10,9},{11,1... | collective-permute-start | bytes 294920 | tf_op jit(solution)/shard_map/ppermute | solution.py:263
  11.7 0.8 active.1
  12.4 1.3 %own_cells.1.inner_sum = f32[288,864]{1,0:T(8,128)S(1)} custom-call(bf16[384,512]{1,0:T(8,128)(2,1)S(1)} %get-tuple-element.22.own, bf16[4,288,512]{2,1,0:T(8,128)(2,1)S(1)} %get-tuple-element.25.act), custom_call_target="tpu_custom_call" | custom-call | tf_op jit(solution)/shard_map/own_cells/pallas_call | solution.py:221
  13.7 0.0 collective-permute-done.2.before
  13.7 1.1 %frames_before.1 = (f32[288,864]{1,0:T(8,128)S(1)}, bf16[2,288,256]{2,1,0:T(8,128)(2,1)S(1)}) custom-call(bf16[2,384,128]{2,1,0:T(8,128)(2,1)S(1)} %collective-permute-done.2.before, bf16[384,512]{1,0:T(8,128)(2,1)S(1)} %get-tuple-element.22.own, bf16[384,384]{1,0:T(8,128)(2,1)S(1)} %get-tuple-element.24.order, f32[288,864]{1,0:T(8,128)S(1)} %own_cells.1.inner_sum), custom_call_target="tpu_custom_call" | custom-call | tf_op jit(solution)/shard_map/frames_before/pallas_call | solution.py:221
  14.8 0.0 collective-permute-done.above
  14.8 1.1 %collective-permute-done.1.below = bf16[96,512]{1,0:T(8,128)(2,1)S(1)} collective-permute-done((bf16[96,512]{1,0:T(8,128)(2,1)S(1)}, bf16[96,512]{1,0:T(8,128)(2,1)S(1)}, u32[]{:S(2)}, u32[]{:S(2)}) %collective-permute-start.1) | collective-permute-done | bytes 98336 | tf_op jit(solution)/shard_map/ppermute | solution.py:263
  15.9 0.7 edge_rows.1
  16.6 4.2 %all-gather = bf16[2048,128]{1,0:T(8,128)(2,1)S(1)} all-gather(bf16[1024,128]{1,0:T(8,128)(2,1)S(1)} %get-tuple-element.34), channel_id=2, replica_groups=mesh['y_hi'=2,'x'=4,'core'=2,'y_lo'=2,'z_pair'=8,'z_in'=2] {'core'}, dimensions={0}, use_global_device_ids=true | all-gather | bytes 786432 | tf_op jit(solution)/shard_map/all_gather | solution.py:286
  20.8 0.7 core_sum.1
  21.6 11.9 %all-to-all-start = ((bf16[32,32,128]{2,1,0:T(8,128)(2,1)}), bf16[32,32,128]{2,1,0:T(8,128)(2,1)S(1)}, u32[]{:S(2)}, u32[]{:S(2)}) async-start(bf16[32,32,128]{2,1,0:T(8,128)(2,1)} %bitcast.6), calls=%async_computation | async-start | bytes 524288 | tf_op jit(solution)/shard_map/all_to_all | solution.py:297
  33.4 2.3 %collective-permute-start.3 = (bf16[576,256]{1,0:T(8,128)(2,1)S(1)}, bf16[576,256]{1,0:T(8,128)(2,1)S(1)}, u32[]{:S(2)}, u32[]{:S(2)}) collective-permute-start(bf16[576,256]{1,0:T(8,128)(2,1)S(1)} %get-tuple-element.29), channel_id=1, source_target_pairs={{32,0},{64,32},{96,64},{128,96},{160,128},{192,160},{224,192},{256... | collective-permute-start | bytes 884744 | tf_op jit(solution)/shard_map/ppermute | solution.py:287
  35.8 6.5 %all-to-all-done.parts = bf16[32,32,128]{2,1,0:T(8,128)(2,1)S(1)} async-done(((bf16[32,32,128]{2,1,0:T(8,128)(2,1)}), bf16[32,32,128]{2,1,0:T(8,128)(2,1)S(1)}, u32[]{:S(2)}, u32[]{:S(2)}) %all-to-all-start) | async-done | bytes 262176 | tf_op jit(solution)/shard_map/all_to_all | solution.py:297
  42.2 0.7 plane_sum.1
  42.9 8.7 %all-to-all-start.1 = ((bf16[8,32,128]{2,1,0:T(8,128)(2,1)}), bf16[8,32,128]{2,1,0:T(8,128)(2,1)S(1)}, u32[]{:S(2)}, u32[]{:S(2)}) async-start(bf16[8,32,128]{2,1,0:T(8,128)(2,1)} %plane_sum.1), calls=%async_computation.1 | async-start | bytes 131072 | tf_op jit(solution)/shard_map/all_to_all | solution.py:299
  51.6 3.0 %input_grad.1 = (bf16[4,384,128]{2,1,0:T(8,128)(2,1)}, f32[8,128]{1,0:T(8,128)S(1)}) custom-call(bf16[96,512]{1,0:T(8,128)(2,1)S(1)} %collective-permute-done.above, bf16[96,512]{1,0:T(8,128)(2,1)S(1)} %collective-permute-done.1.below, bf16[384,512]{1,0:T(8,128)(2,1)S(1)} %get-tuple-element.22.own, bf16[576,256]{1,0:T(8,128)(2,1)S(1)} %collective-permute-done.3.later, ...), custom_call_target="tpu_custom_call" | custom-call | flops 2147483648 | tf_op jit(solution)/shard_map/input_grad/pallas_call | solution.py:221
  54.6 9.3 %all-to-all-done.1.parts = bf16[8,32,128]{2,1,0:T(8,128)(2,1)S(1)} async-done(((bf16[8,32,128]{2,1,0:T(8,128)(2,1)}), bf16[8,32,128]{2,1,0:T(8,128)(2,1)S(1)}, u32[]{:S(2)}, u32[]{:S(2)}) %all-to-all-start.1) | async-done | bytes 65568 | tf_op jit(solution)/shard_map/all_to_all | solution.py:299
  63.9 11.4 %all_to_all.15 = bf16[32,32,128]{2,1,0:T(8,128)(2,1)S(1)} all-to-all(bf16[32,32,128]{2,1,0:T(8,128)(2,1)S(1)} %depth_sum.1), channel_id=1, replica_groups=mesh['y_hi'=2,'x'=4,'core'=2,'y_lo'=2,'z_pair'=8,'z_in'=2] {'y_hi','x','..., dimensions={0} | all-to-all | bytes 524288 | tf_op jit(solution)/shard_map/all_to_all | solution.py:301
  75.3 6.2 %all_gather.11.refs_0_ = bf16[2,1024,128]{2,1,0:T(8,128)(2,1)S(1)} all-gather(bf16[1,1024,128]{2,1,0:T(8,128)(2,1)S(1)} %bitcast.12), channel_id=1, replica_groups=mesh['y_hi'=2,'x'=4,'core'=2,'y_lo'=2,'z_pair'=8,'z_in'=2] {'core'}, dimensions={0}, use_global_device_ids=true | all-gather | bytes 786432 | tf_op jit(solution)/shard_map/all_gather | solution.py:302
  81.5 1.3 %unpack.1 = f32[27,96,96]{2,1,0:T(8,128)} custom-call(bf16[2,1024,128]{2,1,0:T(8,128)(2,1)S(1)} %all_gather.11.refs_0_), custom_call_target="tpu_custom_call" | custom-call | tf_op jit(solution)/shard_map/unpack/pallas_call | solution.py:221
  (4 shorter events, 0.0 us)
Async XLA Ops:
  1.9 11.8 %collective-permute-start.2 = (bf16[2,384,128]{2,1,0:T(8,128)(2,1)S(1)}, bf16[2,384,128]{2,1,0:T(8,128)(2,1)S(1)}, u32[]{:S(2)}, u32[]{:S(2)}) collective-permute-start(bf16[2,384,128]{2,1,0:T(8,128)(2,1)S(1)} %get-tuple-element.26), channel_id=1, source_target_pairs={{0,32},{32,64},{64,96},{96,128},{128,160},{160,192},{192,224},{224... | collective-permute-start | bytes 589832 | tf_op jit(solution)/shard_map/ppermute | solution.py:254
  6.8 8.0 %collective-permute-start = (bf16[96,512]{1,0:T(8,128)(2,1)S(1)}, bf16[96,512]{1,0:T(8,128)(2,1)S(1)}, u32[]{:S(2)}, u32[]{:S(2)}) collective-permute-start(bf16[96,512]{1,0:T(8,128)(2,1)S(1)} %get-tuple-element.20), channel_id=1, source_target_pairs={{0,1},{1,2},{2,3},{3,4},{4,5},{5,6},{6,7},{7,8},{8,9},{9,10},{10,1... | collective-permute-start | bytes 294920 | tf_op jit(solution)/shard_map/ppermute | solution.py:262
  10.4 5.5 %collective-permute-start.1 = (bf16[96,512]{1,0:T(8,128)(2,1)S(1)}, bf16[96,512]{1,0:T(8,128)(2,1)S(1)}, u32[]{:S(2)}, u32[]{:S(2)}) collective-permute-start(bf16[96,512]{1,0:T(8,128)(2,1)S(1)} %get-tuple-element.21), channel_id=1, source_target_pairs={{1,0},{2,1},{3,2},{4,3},{5,4},{6,5},{7,6},{8,7},{9,8},{10,9},{11,1... | collective-permute-start | bytes 294920 | tf_op jit(solution)/shard_map/ppermute | solution.py:263
  20.8 30.8 %copy-start = (bf16[3,3,3,96,96]{4,3,2,1,0:T(8,128)(2,1)S(1)}, bf16[3,3,3,96,96]{4,3,2,1,0:T(8,128)(2,1)}, u32[]{:S(2)}) copy-start(bf16[3,3,3,96,96]{4,3,2,1,0:T(8,128)(2,1)} %param.4) | copy-start | bytes 1492996
  21.6 20.7 %all-to-all-start = ((bf16[32,32,128]{2,1,0:T(8,128)(2,1)}), bf16[32,32,128]{2,1,0:T(8,128)(2,1)S(1)}, u32[]{:S(2)}, u32[]{:S(2)}) async-start(bf16[32,32,128]{2,1,0:T(8,128)(2,1)} %bitcast.6), calls=%async_computation | async-start | bytes 524288 | tf_op jit(solution)/shard_map/all_to_all | solution.py:297
  33.4 18.1 %collective-permute-start.3 = (bf16[576,256]{1,0:T(8,128)(2,1)S(1)}, bf16[576,256]{1,0:T(8,128)(2,1)S(1)}, u32[]{:S(2)}, u32[]{:S(2)}) collective-permute-start(bf16[576,256]{1,0:T(8,128)(2,1)S(1)} %get-tuple-element.29), channel_id=1, source_target_pairs={{32,0},{64,32},{96,64},{128,96},{160,128},{192,160},{224,192},{256... | collective-permute-start | bytes 884744 | tf_op jit(solution)/shard_map/ppermute | solution.py:287
  42.9 21.0 %all-to-all-start.1 = ((bf16[8,32,128]{2,1,0:T(8,128)(2,1)}), bf16[8,32,128]{2,1,0:T(8,128)(2,1)S(1)}, u32[]{:S(2)}, u32[]{:S(2)}) async-start(bf16[8,32,128]{2,1,0:T(8,128)(2,1)} %plane_sum.1), calls=%async_computation.1 | async-start | bytes 131072 | tf_op jit(solution)/shard_map/all_to_all | solution.py:299

commit v8 on v7

--- a/solution.py
+++ b/solution.py
@@ -235,6 +235,10 @@
     return call(sum_kernel, name, [((count,) + parts.shape[1:], BF16)], (parts,), after=after)[0]
 
 
+def turned(count, first):
+    return [[(i + first) % count for i in range(count)]]
+
+
 def local(features, weights, cotangent):
     tm, rows = lax.axis_size(TM), lax.axis_size(ROWS)
     near, depth = lax.axis_size(NEAR), lax.axis_size("z_pair")
@@ -294,11 +298,11 @@
     )
 
     (packed,) = call(add_kernel, "core_sum", [((PACKED, W), BF16)], (kept, exchanged), smem=(core,))
-    parts = lax.all_to_all(packed.reshape(near, PACKED // near, W), NEAR, 0, 0)
+    parts = lax.all_to_all(packed.reshape(near, PACKED // near, W), NEAR, 0, 0, axis_index_groups=turned(near, 24))
     slabs = sum_to_slots(parts, depth, "plane_sum")
-    slabs = lax.all_to_all(slabs, "z_pair", 0, 0)
+    slabs = lax.all_to_all(slabs, "z_pair", 0, 0, axis_index_groups=turned(depth, 4))
     slots = sum_to_slots(slabs, near, "depth_sum", after=(done,))
-    own_half = lax.all_to_all(slots, NEAR, 0, 0).reshape(PACKED, W)
+    own_half = lax.all_to_all(slots, NEAR, 0, 0, axis_index_groups=turned(near, 24)).reshape(PACKED, W)
     whole = lax.all_gather(own_half, "core")
     (weight_grad,) = call(
         lambda *refs: unpack_kernel(1.0 / float(cells) ** 0.5, *refs),

time: 83.2 us -> 73.9 us (0.89)
  waiting for transfers between devices: 16.8 us -> 2.92 us
  starting transfers between devices: 32.2 us -> 37.7 us
  blocking collectives: 21.8 us -> 20.9 us
    all_to_all x2, waiting for transfers between devices: 15.7 us -> 1.83 us  [the longest x1 1.82 us: local(): lax.all_to_all(packed.reshape(near, PACKED // near, W), NEAR, 0, 0, axis_...]
    all_to_all x2, starting transfers between devices: 20.5 us -> 25.7 us  [the longest x1 14.2 us: local(): lax.all_to_all(packed.reshape(near, PACKED // near, W), NEAR, 0, 0, axis_...]
  transfers between devices with their start and end apart: 6 -> 6, of which waited for: 3 -> 2; matrix products, arithmetic and copies ran while one was open for 0% -> 0% of each run, Pallas kernels for 9% -> 10%
where the time goes in v8:
time: 73.9 us; the launch traced here: 73.5 us
  starting transfers between devices  37.7 us (51%)
  blocking collectives  20.9 us (28%)
  Pallas kernels  11.2 us (15%)
  waiting for transfers between devices  2.92 us (4%)
  between operations  0.74 us (1%)
    all_to_all x1, starting transfers between devices, local(): lax.all_to_all(packed.reshape(near, PACKED // near, W), NEAR, 0, 0, axis_...  14.2 us
    all_to_all x1, starting transfers between devices, local(): lax.all_to_all(slabs, 'z_pair', 0, 0, axis_index_groups=turned(depth, 4))  11.5 us
    all_to_all x1, blocking collectives, local(): lax.all_to_all(slots, NEAR, 0, 0, axis_index_groups=turned(near, 24))  11.3 us
    pallas_call x11, Pallas kernels, call(): pl.pallas_call(kernel, out_shape=tuple((jax.ShapeDtypeStruct(shape, dtype...  11.2 us
    all_gather x1, blocking collectives, local(): whole = lax.all_gather(own_half, 'core')  5.44 us
    ppermute x1, starting transfers between devices, local(): before = lax.ppermute(last_frames, TM, forward)  4.51 us
    all_gather x1, blocking collectives, local(): exchanged = lax.all_gather(given, 'core')  4.19 us
    ppermute x1, starting transfers between devices, local(): above = lax.ppermute(bottom, ROWS, [(i, i + 1) for i in range(rows - 1)])  3.54 us
  transfers between devices with their start and end apart: 6, of which 2 were waited for; matrix products, arithmetic and copies ran while one was open for 0% of the time, Pallas kernels for 10%

profile of v8, /device:TPU:1, one launch (start us, length us, event | category | flops | bytes accessed | tf_op | source)
XLA Modules:
  0.0 73.5 jit_solution(1430730149426627861)
XLA Ops:
  0.6 1.2 %load.1 = (bf16[2,384,128]{2,1,0:T(8,128)(2,1)S(1)}, bf16[4,384,128]{2,1,0:T(8,128)(2,1)S(1)}, bf16[4,384,128]{2,1,0:T(8,128)(2,1)S(1)}) custom-call(bf16[4,384,128]{2,1,0:T(8,128)(2,1)} %bitcast.13, bf16[4,384,128]{2,1,0:T(8,128)(2,1)} %bitcast.14), custom_call_target="tpu_custom_call" | custom-call | tf_op jit(solution)/shard_map/load/pallas_call | solution.py:221
  1.9 4.5 %collective-permute-start.2 = (bf16[2,384,128]{2,1,0:T(8,128)(2,1)S(1)}, bf16[2,384,128]{2,1,0:T(8,128)(2,1)S(1)}, u32[]{:S(2)}, u32[]{:S(2)}) collective-permute-start(bf16[2,384,128]{2,1,0:T(8,128)(2,1)S(1)} %get-tuple-element.26), channel_id=1, source_target_pairs={{0,32},{32,64},{64,96},{96,128},{128,160},{160,192},{192,224},{224... | collective-permute-start | bytes 589832 | tf_op jit(solution)/shard_map/ppermute | solution.py:258
  6.4 0.4 cot_rows.1
  6.8 3.5 %collective-permute-start = (bf16[96,512]{1,0:T(8,128)(2,1)S(1)}, bf16[96,512]{1,0:T(8,128)(2,1)S(1)}, u32[]{:S(2)}, u32[]{:S(2)}) collective-permute-start(bf16[96,512]{1,0:T(8,128)(2,1)S(1)} %get-tuple-element.20), channel_id=1, source_target_pairs={{0,1},{1,2},{2,3},{3,4},{4,5},{5,6},{6,7},{7,8},{8,9},{9,10},{10,1... | collective-permute-start | bytes 294920 | tf_op jit(solution)/shard_map/ppermute | solution.py:266
  10.4 1.3 %collective-permute-start.1 = (bf16[96,512]{1,0:T(8,128)(2,1)S(1)}, bf16[96,512]{1,0:T(8,128)(2,1)S(1)}, u32[]{:S(2)}, u32[]{:S(2)}) collective-permute-start(bf16[96,512]{1,0:T(8,128)(2,1)S(1)} %get-tuple-element.21), channel_id=1, source_target_pairs={{1,0},{2,1},{3,2},{4,3},{5,4},{6,5},{7,6},{8,7},{9,8},{10,9},{11,1... | collective-permute-start | bytes 294920 | tf_op jit(solution)/shard_map/ppermute | solution.py:267
  11.7 0.8 %active.1 = (bf16[4,288,512]{2,1,0:T(8,128)(2,1)S(1)}, f32[4,96,512]{2,1,0:T(8,128)S(1)}, f32[4,1,512]{2,1,0:T(1,128)S(1)}) custom-call(bf16[4,384,128]{2,1,0:T(8,128)(2,1)S(1)} %get-tuple-element.23.feat, bf16[384,384]{1,0:T(8,128)(2,1)S(1)} %get-tuple-element.24.order), custom_call_target="tpu_custom_call" | custom-call | tf_op jit(solution)/shard_map/active/pallas_call | solution.py:221
  12.4 1.3 %own_cells.1.inner_sum = f32[288,864]{1,0:T(8,128)S(1)} custom-call(bf16[384,512]{1,0:T(8,128)(2,1)S(1)} %get-tuple-element.22.own, bf16[4,288,512]{2,1,0:T(8,128)(2,1)S(1)} %get-tuple-element.25.act), custom_call_target="tpu_custom_call" | custom-call | tf_op jit(solution)/shard_map/own_cells/pallas_call | solution.py:221
  13.7 0.0 collective-permute-done.2.before
  13.7 1.1 %frames_before.1 = (f32[288,864]{1,0:T(8,128)S(1)}, bf16[2,288,256]{2,1,0:T(8,128)(2,1)S(1)}) custom-call(bf16[2,384,128]{2,1,0:T(8,128)(2,1)S(1)} %collective-permute-done.2.before, bf16[384,512]{1,0:T(8,128)(2,1)S(1)} %get-tuple-element.22.own, bf16[384,384]{1,0:T(8,128)(2,1)S(1)} %get-tuple-element.24.order, f32[288,864]{1,0:T(8,128)S(1)} %own_cells.1.inner_sum), custom_call_target="tpu_custom_call" | custom-call | tf_op jit(solution)/shard_map/frames_before/pallas_call | solution.py:221
  14.8 0.0 collective-permute-done.above
  14.8 1.1 %collective-permute-done.1.below = bf16[96,512]{1,0:T(8,128)(2,1)S(1)} collective-permute-done((bf16[96,512]{1,0:T(8,128)(2,1)S(1)}, bf16[96,512]{1,0:T(8,128)(2,1)S(1)}, u32[]{:S(2)}, u32[]{:S(2)}) %collective-permute-start.1) | collective-permute-done | bytes 98336 | tf_op jit(solution)/shard_map/ppermute | solution.py:267
  15.9 0.7 edge_rows.1
  16.6 4.2 %all-gather = bf16[2048,128]{1,0:T(8,128)(2,1)S(1)} all-gather(bf16[1024,128]{1,0:T(8,128)(2,1)S(1)} %get-tuple-element.34), channel_id=2, replica_groups=mesh['y_hi'=2,'x'=4,'core'=2,'y_lo'=2,'z_pair'=8,'z_in'=2] {'core'}, dimensions={0}, use_global_device_ids=true | all-gather | bytes 786432 | tf_op jit(solution)/shard_map/all_gather | solution.py:290
  20.8 0.7 %core_sum.1 = bf16[1024,128]{1,0:T(8,128)(2,1)} custom-call(s32[1]{0:T(128)} %bitcast.2.core, f32[1024,128]{1,0:T(8,128)S(1)} %get-tuple-element.33.kept, bf16[2,1024,128]{2,1,0:T(8,128)(2,1)S(1)} %bitcast.9), custom_call_target="tpu_custom_call" | custom-call | tf_op jit(solution)/shard_map/core_sum/pallas_call | solution.py:221
  21.6 14.2 %all-to-all-start = ((bf16[32,32,128]{2,1,0:T(8,128)(2,1)}), bf16[32,32,128]{2,1,0:T(8,128)(2,1)S(1)}, u32[]{:S(2)}, u32[]{:S(2)}) async-start(bf16[32,32,128]{2,1,0:T(8,128)(2,1)} %bitcast.6), calls=%async_computation | async-start | bytes 524288 | tf_op jit(solution)/shard_map/all_to_all | solution.py:301
  35.8 2.6 %collective-permute-start.3 = (bf16[576,256]{1,0:T(8,128)(2,1)S(1)}, bf16[576,256]{1,0:T(8,128)(2,1)S(1)}, u32[]{:S(2)}, u32[]{:S(2)}) collective-permute-start(bf16[576,256]{1,0:T(8,128)(2,1)S(1)} %get-tuple-element.29), channel_id=1, source_target_pairs={{32,0},{64,32},{96,64},{128,96},{160,128},{192,160},{224,192},{256... | collective-permute-start | bytes 884744 | tf_op jit(solution)/shard_map/ppermute | solution.py:291
  38.4 1.8 %all-to-all-done.parts = bf16[32,32,128]{2,1,0:T(8,128)(2,1)S(1)} async-done(((bf16[32,32,128]{2,1,0:T(8,128)(2,1)}), bf16[32,32,128]{2,1,0:T(8,128)(2,1)S(1)}, u32[]{:S(2)}, u32[]{:S(2)}) %all-to-all-start) | async-done | bytes 262176 | tf_op jit(solution)/shard_map/all_to_all | solution.py:301
  40.3 0.7 plane_sum.1
  40.9 11.5 %all-to-all-start.1 = ((bf16[8,32,128]{2,1,0:T(8,128)(2,1)}), bf16[8,32,128]{2,1,0:T(8,128)(2,1)S(1)}, u32[]{:S(2)}, u32[]{:S(2)}) async-start(bf16[8,32,128]{2,1,0:T(8,128)(2,1)} %plane_sum.1), calls=%async_computation.1 | async-start | bytes 131072 | tf_op jit(solution)/shard_map/all_to_all | solution.py:303
  52.4 3.0 %input_grad.1 = (bf16[4,384,128]{2,1,0:T(8,128)(2,1)}, f32[8,128]{1,0:T(8,128)S(1)}) custom-call(bf16[96,512]{1,0:T(8,128)(2,1)S(1)} %collective-permute-done.above, bf16[96,512]{1,0:T(8,128)(2,1)S(1)} %collective-permute-done.1.below, bf16[384,512]{1,0:T(8,128)(2,1)S(1)} %get-tuple-element.22.own, bf16[576,256]{1,0:T(8,128)(2,1)S(1)} %collective-permute-done.3.later, ...), custom_call_target="tpu_custom_call" | custom-call | flops 2147483648 | tf_op jit(solution)/shard_map/input_grad/pallas_call | solution.py:221
  55.4 0.0 all-to-all-done.1.parts
  55.4 11.3 %all_to_all.15 = bf16[32,32,128]{2,1,0:T(8,128)(2,1)S(1)} all-to-all(bf16[32,32,128]{2,1,0:T(8,128)(2,1)S(1)} %depth_sum.1), channel_id=1, replica_groups={{384,385,400,401,448,449,464,465,0,1,16,17,64,65,80,81,128,129,144,145,..., dimensions={0} | all-to-all | bytes 524288 | tf_op jit(solution)/shard_map/all_to_all | solution.py:305
  66.7 5.4 %all_gather.11.refs_0_ = bf16[2,1024,128]{2,1,0:T(8,128)(2,1)S(1)} all-gather(bf16[1,1024,128]{2,1,0:T(8,128)(2,1)S(1)} %bitcast.12), channel_id=1, replica_groups=mesh['y_hi'=2,'x'=4,'core'=2,'y_lo'=2,'z_pair'=8,'z_in'=2] {'core'}, dimensions={0}, use_global_device_ids=true | all-gather | bytes 786432 | tf_op jit(solution)/shard_map/all_gather | solution.py:306
  72.2 1.3 %unpack.1 = f32[27,96,96]{2,1,0:T(8,128)} custom-call(bf16[2,1024,128]{2,1,0:T(8,128)(2,1)S(1)} %all_gather.11.refs_0_), custom_call_target="tpu_custom_call" | custom-call | tf_op jit(solution)/shard_map/unpack/pallas_call | solution.py:221
  (4 shorter events, 0.0 us)
Async XLA Ops:
  1.9 11.8 %collective-permute-start.2 = (bf16[2,384,128]{2,1,0:T(8,128)(2,1)S(1)}, bf16[2,384,128]{2,1,0:T(8,128)(2,1)S(1)}, u32[]{:S(2)}, u32[]{:S(2)}) collective-permute-start(bf16[2,384,128]{2,1,0:T(8,128)(2,1)S(1)} %get-tuple-element.26), channel_id=1, source_target_pairs={{0,32},{32,64},{64,96},{96,128},{128,160},{160,192},{192,224},{224... | collective-permute-start | bytes 589832 | tf_op jit(solution)/shard_map/ppermute | solution.py:258
  6.8 8.0 %collective-permute-start = (bf16[96,512]{1,0:T(8,128)(2,1)S(1)}, bf16[96,512]{1,0:T(8,128)(2,1)S(1)}, u32[]{:S(2)}, u32[]{:S(2)}) collective-permute-start(bf16[96,512]{1,0:T(8,128)(2,1)S(1)} %get-tuple-element.20), channel_id=1, source_target_pairs={{0,1},{1,2},{2,3},{3,4},{4,5},{5,6},{6,7},{7,8},{8,9},{9,10},{10,1... | collective-permute-start | bytes 294920 | tf_op jit(solution)/shard_map/ppermute | solution.py:266
  10.4 5.5 %collective-permute-start.1 = (bf16[96,512]{1,0:T(8,128)(2,1)S(1)}, bf16[96,512]{1,0:T(8,128)(2,1)S(1)}, u32[]{:S(2)}, u32[]{:S(2)}) collective-permute-start(bf16[96,512]{1,0:T(8,128)(2,1)S(1)} %get-tuple-element.21), channel_id=1, source_target_pairs={{1,0},{2,1},{3,2},{4,3},{5,4},{6,5},{7,6},{8,7},{9,8},{10,9},{11,1... | collective-permute-start | bytes 294920 | tf_op jit(solution)/shard_map/ppermute | solution.py:267
  20.8 31.6 %copy-start = (bf16[3,3,3,96,96]{4,3,2,1,0:T(8,128)(2,1)S(1)}, bf16[3,3,3,96,96]{4,3,2,1,0:T(8,128)(2,1)}, u32[]{:S(2)}) copy-start(bf16[3,3,3,96,96]{4,3,2,1,0:T(8,128)(2,1)} %param.4) | copy-start | bytes 1492996
  21.6 18.7 %all-to-all-start = ((bf16[32,32,128]{2,1,0:T(8,128)(2,1)}), bf16[32,32,128]{2,1,0:T(8,128)(2,1)S(1)}, u32[]{:S(2)}, u32[]{:S(2)}) async-start(bf16[32,32,128]{2,1,0:T(8,128)(2,1)} %bitcast.6), calls=%async_computation | async-start | bytes 524288 | tf_op jit(solution)/shard_map/all_to_all | solution.py:301
  35.8 16.6 %collective-permute-start.3 = (bf16[576,256]{1,0:T(8,128)(2,1)S(1)}, bf16[576,256]{1,0:T(8,128)(2,1)S(1)}, u32[]{:S(2)}, u32[]{:S(2)}) collective-permute-start(bf16[576,256]{1,0:T(8,128)(2,1)S(1)} %get-tuple-element.29), channel_id=1, source_target_pairs={{32,0},{64,32},{96,64},{128,96},{160,128},{192,160},{224,192},{256... | collective-permute-start | bytes 884744 | tf_op jit(solution)/shard_map/ppermute | solution.py:291
  40.9 14.5 %all-to-all-start.1 = ((bf16[8,32,128]{2,1,0:T(8,128)(2,1)}), bf16[8,32,128]{2,1,0:T(8,128)(2,1)S(1)}, u32[]{:S(2)}, u32[]{:S(2)}) async-start(bf16[8,32,128]{2,1,0:T(8,128)(2,1)} %plane_sum.1), calls=%async_computation.1 | async-start | bytes 131072 | tf_op jit(solution)/shard_map/all_to_all | solution.py:303

commit v9 on v8

--- a/solution.py
+++ b/solution.py
@@ -78,7 +78,7 @@
     return 1.0 / (1.0 + jnp.exp(-x))
 
 
-def load_kernel(feat_in, cot_in, last_frames, feat, cot, sems):
+def load_kernel(feat_in, cot_in, last_frames, feat, cot, order, sems):
     copies = [
         pltpu.make_async_copy(feat_in.at[pl.ds(F - 2, 2)], last_frames, sems.at[0]),
         pltpu.make_async_copy(cot_in, cot, sems.at[1]),
@@ -86,12 +86,12 @@
     ]
     for copy in copies:
         copy.start()
+    order[...] = row_major()
     for copy in copies:
         copy.wait()
 
 
-def cot_kernel(cot, own, bottom, top, order):
-    order[...] = row_major()
+def cot_kernel(cot, order, own, bottom, top):
     rows = dot(order[...], frames(cot, F), ((1,), (0,))).astype(BF16)
     own[...] = rows
     top[...] = rows[:CH]
@@ -118,10 +118,9 @@
     wsum[2 * CH :, :] = both[2 * CH :] + first[CH:]
 
 
-def past_kernel(before, own, order, inner_sum, wsum, past_act):
+def past_kernel(before, own, order, early, past_act):
     values = dot(order[...], frames(before, 2), ((1,), (0,)))
-    zeros = jnp.zeros((CH, 2 * TAP), F32)
-    early = jnp.zeros((TAP, 2 * TAP), F32)
+    terms = []
     for h in range(H):
         n, _ = normalize(values[h * CH : (h + 1) * CH])
         past = column_taps((n * sigmoid(n)).astype(BF16))
@@ -129,27 +128,39 @@
             past_act[h // (H - 1)] = past
         late = jnp.concatenate([past[:, W:], jnp.zeros((TAP, W), BF16)], axis=1)
         rows = rows_of(own, max(h - 1, 0), 3 - (h in (0, H - 1)))
-        term = dot(rows[:, :NEXT], jnp.concatenate([past, late], axis=0), ((1,), (1,)))
-        early = early + jnp.concatenate([zeros] * (h == 0) + [term] + [zeros] * (h == H - 1), axis=0)
-    wsum[...] = inner_sum[...] + jnp.concatenate([early, jnp.zeros((TAP, TAP), F32)], axis=1)
-
-
-def edge_kernel(core, above, below, own, act, past_act, wsum, kept, given, first_frames, total):
-    upper, lower = above[...], below[...]
-    from_above = dot(upper, time_taps(past_act[0], act[0]), ((1,), (1,)))
-    from_below = dot(lower, time_taps(past_act[1], act[H - 1]), ((1,), (1,)))
-    first_frames[:CH, :] = upper[:, :NEXT]
+        terms.append(dot(rows[:, :NEXT], jnp.concatenate([past, late], axis=0), ((1,), (1,))))
+    first, second, third, last = terms
+    both = second + third
+    early[:CH, :] = both[:CH] + last[:CH]
+    early[CH : 2 * CH, :] = both[CH : 2 * CH] + first[:CH] + last[CH:]
+    early[2 * CH :, :] = both[2 * CH :] + first[CH:]
+
+
+def above_kernel(above, act, past_act, wsum, early, total):
+    term = dot(above[...], time_taps(past_act[0], act[0]), ((1,), (1,)))
+    for k in range(3):
+        rows = slice(k * CH, (k + 1) * CH)
+        soon, late = wsum[rows, : 2 * TAP] + early[rows], wsum[rows, 2 * TAP :]
+        if k == 0:
+            soon, late = soon + term[:, : 2 * TAP], late + term[:, 2 * TAP :]
+        total[rows, : 2 * TAP] = soon
+        total[rows, 2 * TAP : 3 * TAP] = late
+        total[rows, 3 * TAP :] = jnp.zeros((CH, TILES * W - 3 * TAP), F32)
+
+
+def below_kernel(core, above, below, own, act, past_act, total, kept, given, first_frames, last):
+    lower = below[...]
+    last[:, : 3 * TAP] = total[2 * CH :, : 3 * TAP] + dot(lower, time_taps(past_act[1], act[H - 1]), ((1,), (1,)))
+    last[:, 3 * TAP :] = jnp.zeros((CH, TILES * W - 3 * TAP), F32)
+    first_frames[:CH, :] = above[:, :NEXT]
     first_frames[CH : 5 * CH, :] = own[:, :NEXT]
     first_frames[5 * CH :, :] = lower[:, :NEXT]
-    total[:CH, : 3 * TAP] = wsum[:CH] + from_above
-    total[CH : 2 * CH, : 3 * TAP] = wsum[CH : 2 * CH]
-    total[2 * CH :, : 3 * TAP] = wsum[2 * CH :] + from_below
-    total[:, 3 * TAP :] = jnp.zeros((TAP, TILES * W - 3 * TAP), F32)
     for out, half in ((given, 1 - core[0]), (kept, core[0])):
         for k in range(3):
-            rows = pl.ds(pl.multiple_of(k * CH + half * HALF, HALF), HALF)
+            source, first = (last, 0) if k == 2 else (total, k * CH)
+            rows = pl.ds(pl.multiple_of(first + half * HALF, HALF), HALF)
             for j in range(TILES):
-                tile = total[rows, j * W : (j + 1) * W]
+                tile = source[rows, j * W : (j + 1) * W]
                 out[j * TILE + k * HALF : j * TILE + (k + 1) * HALF, :] = tile.astype(out.dtype)
         out[TILES * TILE :, :] = jnp.zeros((PACKED - TILES * TILE, W), out.dtype)
 
@@ -247,20 +258,20 @@
     cotangent = cotangent.reshape(F, CH * H, W)
 
     forward, back = [(i, i + 1) for i in range(tm - 1)], [(i + 1, i) for i in range(tm - 1)]
-    last_frames, features, cotangent = call(
+    last_frames, features, cotangent, order = call(
         load_kernel,
         "load",
-        [((2, CH * H, W), BF16), ((F, CH * H, W), BF16), ((F, CH * H, W), BF16)],
+        [((2, CH * H, W), BF16), ((F, CH * H, W), BF16), ((F, CH * H, W), BF16), ((H * CH, H * CH), BF16)],
         (),
         after=[pltpu.with_memory_space_constraint(value, pltpu.HBM) for value in (features, cotangent)],
         scratch=[pltpu.SemaphoreType.DMA((3,))],
     )
     before = lax.ppermute(last_frames, TM, forward)
-    own, bottom, top, order = call(
+    own, bottom, top = call(
         cot_kernel,
         "cot_rows",
-        [((H * CH, FW), BF16), ((CH, FW), BF16), ((CH, FW), BF16), ((H * CH, H * CH), BF16)],
-        (cotangent,),
+        [((H * CH, FW), BF16), ((CH, FW), BF16), ((CH, FW), BF16)],
+        (cotangent, order),
         1 << 33,
     )
     above = lax.ppermute(bottom, ROWS, [(i, i + 1) for i in range(rows - 1)])
@@ -272,20 +283,23 @@
         (features, order),
     )
     (wsum,) = call(inner_kernel, "own_cells", [((TAP, 3 * TAP), F32)], (own, act))
-    wsum, past_act = call(
+    early, past_act = call(
         past_kernel,
         "frames_before",
-        [((TAP, 3 * TAP), F32), ((2, TAP, NEXT), BF16)],
-        (before, own, order, wsum),
+        [((TAP, 2 * TAP), F32), ((2, TAP, NEXT), BF16)],
+        (before, own, order),
     )
     core = lax.axis_index("core").astype(jnp.int32).reshape(1)
+    (total,) = call(
+        above_kernel, "row_above", [((TAP, TILES * W), F32)], (above, act, past_act, wsum, early)
+    )
     kept, given, first_frames = call(
-        edge_kernel,
-        "edge_rows",
+        below_kernel,
+        "row_below",
         [((PACKED, W), F32), ((PACKED, W), BF16), (((H + 2) * CH, NEXT), BF16)],
-        (above, below, own, act, past_act, wsum),
+        (above, below, own, act, past_act, total),
         smem=(core,),
-        scratch=[pltpu.VMEM((TAP, TILES * W), F32)],
+        scratch=[pltpu.VMEM((CH, TILES * W), F32)],
     )
     exchanged = lax.all_gather(given, "core")
     later = lax.ppermute(first_frames, TM, back)

time: 73.9 us -> 74.5 us (level)
  Pallas kernels: 11.2 us -> 12.3 us
    pallas_call x11 -> x12, Pallas kernels: 11.2 us -> 12.3 us  [call(): pl.pallas_call(kernel, out_shape=tuple((jax.ShapeDtypeStruct(shape, dtype...]
  transfers between devices with their start and end apart: 6 -> 6, of which waited for: 2 -> 2; matrix products, arithmetic and copies ran while one was open for 0% -> 0% of each run, Pallas kernels for 10% -> 12%
where the time goes in v9:
time: 74.5 us; the launch traced here: 74 us
  starting transfers between devices  38.1 us (51%)
  blocking collectives  20.4 us (27%)
  Pallas kernels  12.3 us (17%)
  waiting for transfers between devices  2.52 us (3%)
  between operations  0.76 us (1%)
    all_to_all x1, starting transfers between devices, local(): lax.all_to_all(packed.reshape(near, PACKED // near, W), NEAR, 0, 0, axis_...  14.6 us
    pallas_call x12, Pallas kernels, call(): pl.pallas_call(kernel, out_shape=tuple((jax.ShapeDtypeStruct(shape, dtype...  12.3 us
    all_to_all x1, starting transfers between devices, local(): lax.all_to_all(slabs, 'z_pair', 0, 0, axis_index_groups=turned(depth, 4))  11.5 us
    all_to_all x1, blocking collectives, local(): lax.all_to_all(slots, NEAR, 0, 0, axis_index_groups=turned(near, 24))  11.3 us
    all_gather x1, blocking collectives, local(): whole = lax.all_gather(own_half, 'core')  4.94 us
    ppermute x1, starting transfers between devices, local(): before = lax.ppermute(last_frames, TM, forward)  4.51 us
    all_gather x1, blocking collectives, local(): exchanged = lax.all_gather(given, 'core')  4.19 us
    ppermute x1, starting transfers between devices, local(): above = lax.ppermute(bottom, ROWS, [(i, i + 1) for i in range(rows - 1)])  3.55 us
  transfers between devices with their start and end apart: 6, of which 2 were waited for; matrix products, arithmetic and copies ran while one was open for 0% of the time, Pallas kernels for 12%

profile of v9, /device:TPU:1, one launch (start us, length us, event | category | flops | bytes accessed | tf_op | source)
XLA Modules:
  0.0 74.0 jit_solution(2955682023264295992)
XLA Ops:
  0.6 1.2 %load.1 = (bf16[2,384,128]{2,1,0:T(8,128)(2,1)S(1)}, bf16[4,384,128]{2,1,0:T(8,128)(2,1)S(1)}, bf16[4,384,128]{2,1,0:T(8,128)(2,1)S(1)}, bf16[384,384]{1,0:T(8,128)(2,1)S(1)}) custom-call(bf16[4,384,128]{2,1,0:T(8,128)(2,1)} %bitcast.13, bf16[4,384,128]{2,1,0:T(8,128)(2,1)} %bitcast.14), custom_call_target="tpu_custom_call" | custom-call | tf_op jit(solution)/shard_map/load/pallas_call | solution.py:232
  1.9 4.5 %collective-permute-start.2 = (bf16[2,384,128]{2,1,0:T(8,128)(2,1)S(1)}, bf16[2,384,128]{2,1,0:T(8,128)(2,1)S(1)}, u32[]{:S(2)}, u32[]{:S(2)}) collective-permute-start(bf16[2,384,128]{2,1,0:T(8,128)(2,1)S(1)} %get-tuple-element.26), channel_id=1, source_target_pairs={{0,32},{32,64},{64,96},{96,128},{128,160},{160,192},{192,224},{224... | collective-permute-start | bytes 589832 | tf_op jit(solution)/shard_map/ppermute | solution.py:269
  6.4 0.4 cot_rows.1
  6.8 3.5 %collective-permute-start = (bf16[96,512]{1,0:T(8,128)(2,1)S(1)}, bf16[96,512]{1,0:T(8,128)(2,1)S(1)}, u32[]{:S(2)}, u32[]{:S(2)}) collective-permute-start(bf16[96,512]{1,0:T(8,128)(2,1)S(1)} %get-tuple-element.21), channel_id=1, source_target_pairs={{0,1},{1,2},{2,3},{3,4},{4,5},{5,6},{6,7},{7,8},{8,9},{9,10},{10,1... | collective-permute-start | bytes 294920 | tf_op jit(solution)/shard_map/ppermute | solution.py:277
  10.3 1.3 %collective-permute-start.1 = (bf16[96,512]{1,0:T(8,128)(2,1)S(1)}, bf16[96,512]{1,0:T(8,128)(2,1)S(1)}, u32[]{:S(2)}, u32[]{:S(2)}) collective-permute-start(bf16[96,512]{1,0:T(8,128)(2,1)S(1)} %get-tuple-element.22), channel_id=1, source_target_pairs={{1,0},{2,1},{3,2},{4,3},{5,4},{6,5},{7,6},{8,7},{9,8},{10,9},{11,1... | collective-permute-start | bytes 294920 | tf_op jit(solution)/shard_map/ppermute | solution.py:278
  11.6 0.8 %active.1 = (bf16[4,288,512]{2,1,0:T(8,128)(2,1)S(1)}, f32[4,96,512]{2,1,0:T(8,128)S(1)}, f32[4,1,512]{2,1,0:T(1,128)S(1)}) custom-call(bf16[4,384,128]{2,1,0:T(8,128)(2,1)S(1)} %get-tuple-element.24.feat, bf16[384,384]{1,0:T(8,128)(2,1)S(1)} %get-tuple-element.20.order), custom_call_target="tpu_custom_call" | custom-call | tf_op jit(solution)/shard_map/active/pallas_call | solution.py:232
  12.4 1.3 %own_cells.1.wsum = f32[288,864]{1,0:T(8,128)S(1)} custom-call(bf16[384,512]{1,0:T(8,128)(2,1)S(1)} %get-tuple-element.23.own, bf16[4,288,512]{2,1,0:T(8,128)(2,1)S(1)} %get-tuple-element.25.act), custom_call_target="tpu_custom_call" | custom-call | tf_op jit(solution)/shard_map/own_cells/pallas_call | solution.py:232
  13.7 1.1 %frames_before.1 = (f32[288,576]{1,0:T(8,128)S(1)}, bf16[2,288,256]{2,1,0:T(8,128)(2,1)S(1)}) custom-call(bf16[2,384,128]{2,1,0:T(8,128)(2,1)S(1)} %collective-permute-done.2.before, bf16[384,512]{1,0:T(8,128)(2,1)S(1)} %get-tuple-element.23.own, bf16[384,384]{1,0:T(8,128)(2,1)S(1)} %get-tuple-element.20.order), custom_call_target="tpu_custom_call" | custom-call | tf_op jit(solution)/shard_map/frames_before/pallas_call | solution.py:232
  14.8 0.4 row_above.1.total
  15.2 0.7 collective-permute-done.1.below
  15.9 0.4 row_below.1
  16.3 4.2 %all-gather = bf16[2048,128]{1,0:T(8,128)(2,1)S(1)} all-gather(bf16[1024,128]{1,0:T(8,128)(2,1)S(1)} %get-tuple-element.34), channel_id=2, replica_groups=mesh['y_hi'=2,'x'=4,'core'=2,'y_lo'=2,'z_pair'=8,'z_in'=2] {'core'}, dimensions={0}, use_global_device_ids=true | all-gather | bytes 786432 | tf_op jit(solution)/shard_map/all_gather | solution.py:304
  20.5 0.7 %core_sum.1 = bf16[1024,128]{1,0:T(8,128)(2,1)} custom-call(s32[1]{0:T(128)} %bitcast.2.core, f32[1024,128]{1,0:T(8,128)S(1)} %get-tuple-element.33.kept, bf16[2,1024,128]{2,1,0:T(8,128)(2,1)S(1)} %bitcast.9), custom_call_target="tpu_custom_call" | custom-call | tf_op jit(solution)/shard_map/core_sum/pallas_call | solution.py:232
  21.3 14.6 %all-to-all-start = ((bf16[32,32,128]{2,1,0:T(8,128)(2,1)}), bf16[32,32,128]{2,1,0:T(8,128)(2,1)S(1)}, u32[]{:S(2)}, u32[]{:S(2)}) async-start(bf16[32,32,128]{2,1,0:T(8,128)(2,1)} %bitcast.6), calls=%async_computation | async-start | bytes 524288 | tf_op jit(solution)/shard_map/all_to_all | solution.py:315
  35.9 2.6 %collective-permute-start.3 = (bf16[576,256]{1,0:T(8,128)(2,1)S(1)}, bf16[576,256]{1,0:T(8,128)(2,1)}, u32[]{:S(2)}, u32[]{:S(2)}) collective-permute-start(bf16[576,256]{1,0:T(8,128)(2,1)S(1)} %get-tuple-element.29), channel_id=1, source_target_pairs={{32,0},{64,32},{96,64},{128,96},{160,128},{192,160},{224,192},{256... | collective-permute-start | bytes 884744 | tf_op jit(solution)/shard_map/ppermute | solution.py:305
  38.5 1.8 %all-to-all-done.parts = bf16[32,32,128]{2,1,0:T(8,128)(2,1)S(1)} async-done(((bf16[32,32,128]{2,1,0:T(8,128)(2,1)}), bf16[32,32,128]{2,1,0:T(8,128)(2,1)S(1)}, u32[]{:S(2)}, u32[]{:S(2)}) %all-to-all-start) | async-done | bytes 262176 | tf_op jit(solution)/shard_map/all_to_all | solution.py:315
  40.3 0.7 plane_sum.1
  41.0 11.5 %all-to-all-start.1 = ((bf16[8,32,128]{2,1,0:T(8,128)(2,1)}), bf16[8,32,128]{2,1,0:T(8,128)(2,1)S(1)}, u32[]{:S(2)}, u32[]{:S(2)}) async-start(bf16[8,32,128]{2,1,0:T(8,128)(2,1)} %plane_sum.1), calls=%async_computation.1 | async-start | bytes 131072 | tf_op jit(solution)/shard_map/all_to_all | solution.py:317
  52.5 0.0 collective-permute-done.3.later
  52.5 4.0 %input_grad.1 = (bf16[4,384,128]{2,1,0:T(8,128)(2,1)}, f32[8,128]{1,0:T(8,128)S(1)}) custom-call(bf16[96,512]{1,0:T(8,128)(2,1)S(1)} %collective-permute-done.above, bf16[96,512]{1,0:T(8,128)(2,1)S(1)} %collective-permute-done.1.below, bf16[384,512]{1,0:T(8,128)(2,1)S(1)} %get-tuple-element.23.own, bf16[576,256]{1,0:T(8,128)(2,1)} %collective-permute-done.3.later, ...), custom_call_target="tpu_custom_call" | custom-call | flops 2147483648 | tf_op jit(solution)/shard_map/input_grad/pallas_call | solution.py:232
  56.5 0.0 all-to-all-done.1.parts
  56.5 11.3 %all_to_all.15 = bf16[32,32,128]{2,1,0:T(8,128)(2,1)S(1)} all-to-all(bf16[32,32,128]{2,1,0:T(8,128)(2,1)S(1)} %depth_sum.1), channel_id=1, replica_groups={{384,385,400,401,448,449,464,465,0,1,16,17,64,65,80,81,128,129,144,145,..., dimensions={0} | all-to-all | bytes 524288 | tf_op jit(solution)/shard_map/all_to_all | solution.py:319
  67.8 4.9 %all_gather.11.refs_0_ = bf16[2,1024,128]{2,1,0:T(8,128)(2,1)S(1)} all-gather(bf16[1,1024,128]{2,1,0:T(8,128)(2,1)S(1)} %bitcast.12), channel_id=1, replica_groups=mesh['y_hi'=2,'x'=4,'core'=2,'y_lo'=2,'z_pair'=8,'z_in'=2] {'core'}, dimensions={0}, use_global_device_ids=true | all-gather | bytes 786432 | tf_op jit(solution)/shard_map/all_gather | solution.py:320
  72.7 1.3 %unpack.1 = f32[27,96,96]{2,1,0:T(8,128)} custom-call(bf16[2,1024,128]{2,1,0:T(8,128)(2,1)S(1)} %all_gather.11.refs_0_), custom_call_target="tpu_custom_call" | custom-call | tf_op jit(solution)/shard_map/unpack/pallas_call | solution.py:232
  (5 shorter events, 0.0 us)
Async XLA Ops:
  1.9 11.8 %collective-permute-start.2 = (bf16[2,384,128]{2,1,0:T(8,128)(2,1)S(1)}, bf16[2,384,128]{2,1,0:T(8,128)(2,1)S(1)}, u32[]{:S(2)}, u32[]{:S(2)}) collective-permute-start(bf16[2,384,128]{2,1,0:T(8,128)(2,1)S(1)} %get-tuple-element.26), channel_id=1, source_target_pairs={{0,32},{32,64},{64,96},{96,128},{128,160},{160,192},{192,224},{224... | collective-permute-start | bytes 589832 | tf_op jit(solution)/shard_map/ppermute | solution.py:269
  6.8 8.0 %collective-permute-start = (bf16[96,512]{1,0:T(8,128)(2,1)S(1)}, bf16[96,512]{1,0:T(8,128)(2,1)S(1)}, u32[]{:S(2)}, u32[]{:S(2)}) collective-permute-start(bf16[96,512]{1,0:T(8,128)(2,1)S(1)} %get-tuple-element.21), channel_id=1, source_target_pairs={{0,1},{1,2},{2,3},{3,4},{4,5},{5,6},{6,7},{7,8},{8,9},{9,10},{10,1... | collective-permute-start | bytes 294920 | tf_op jit(solution)/shard_map/ppermute | solution.py:277
  10.3 5.5 %collective-permute-start.1 = (bf16[96,512]{1,0:T(8,128)(2,1)S(1)}, bf16[96,512]{1,0:T(8,128)(2,1)S(1)}, u32[]{:S(2)}, u32[]{:S(2)}) collective-permute-start(bf16[96,512]{1,0:T(8,128)(2,1)S(1)} %get-tuple-element.22), channel_id=1, source_target_pairs={{1,0},{2,1},{3,2},{4,3},{5,4},{6,5},{7,6},{8,7},{9,8},{10,9},{11,1... | collective-permute-start | bytes 294920 | tf_op jit(solution)/shard_map/ppermute | solution.py:278
  20.5 32.0 %copy-start = (bf16[3,3,3,96,96]{4,3,2,1,0:T(8,128)(2,1)S(1)}, bf16[3,3,3,96,96]{4,3,2,1,0:T(8,128)(2,1)}, u32[]{:S(2)}) copy-start(bf16[3,3,3,96,96]{4,3,2,1,0:T(8,128)(2,1)} %param.4) | copy-start | bytes 1492996
  21.3 19.1 %all-to-all-start = ((bf16[32,32,128]{2,1,0:T(8,128)(2,1)}), bf16[32,32,128]{2,1,0:T(8,128)(2,1)S(1)}, u32[]{:S(2)}, u32[]{:S(2)}) async-start(bf16[32,32,128]{2,1,0:T(8,128)(2,1)} %bitcast.6), calls=%async_computation | async-start | bytes 524288 | tf_op jit(solution)/shard_map/all_to_all | solution.py:315
  35.9 16.6 %collective-permute-start.3 = (bf16[576,256]{1,0:T(8,128)(2,1)S(1)}, bf16[576,256]{1,0:T(8,128)(2,1)}, u32[]{:S(2)}, u32[]{:S(2)}) collective-permute-start(bf16[576,256]{1,0:T(8,128)(2,1)S(1)} %get-tuple-element.29), channel_id=1, source_target_pairs={{32,0},{64,32},{96,64},{128,96},{160,128},{192,160},{224,192},{256... | collective-permute-start | bytes 884744 | tf_op jit(solution)/shard_map/ppermute | solution.py:305
  41.0 15.4 %all-to-all-start.1 = ((bf16[8,32,128]{2,1,0:T(8,128)(2,1)}), bf16[8,32,128]{2,1,0:T(8,128)(2,1)S(1)}, u32[]{:S(2)}, u32[]{:S(2)}) async-start(bf16[8,32,128]{2,1,0:T(8,128)(2,1)} %plane_sum.1), calls=%async_computation.1 | async-start | bytes 131072 | tf_op jit(solution)/shard_map/all_to_all | solution.py:317

commit v10 on v8

--- a/solution.py
+++ b/solution.py
@@ -205,13 +205,14 @@
         for half in range(2)
     ]
     for t in range(3):
-        for c in range(3):
-            for half in range(2):
+        for half in range(2):
+            for c in range(3):
                 column = blocks[half][:, (t * 3 + c) * CH : (t * 3 + c + 1) * CH]
                 for k in range(3):
                     held[t * 9 + (2 - k) * 3 + c, half * HALF : (half + 1) * HALF] = column[k * HALF : (k + 1) * HALF]
-        copies.append(pltpu.make_async_copy(held.at[pl.ds(t * 9, 9)], out.at[pl.ds(t * 9, 9)], sems.at[t]))
-        copies[-1].start()
+            place = (pl.ds(t * 9, 9), pl.ds(half * HALF, HALF))
+            copies.append(pltpu.make_async_copy(held.at[place], out.at[place], sems.at[2 * t + half]))
+            copies[-1].start()
     for copy in copies:
         copy.wait()
 
@@ -310,7 +311,7 @@
         [((27, CH, CH), F32)],
         (whole,),
         out_hbm=(0,),
-        scratch=[pltpu.VMEM((27, CH, CH), F32), pltpu.SemaphoreType.DMA((3,))],
+        scratch=[pltpu.VMEM((27, CH, CH), F32), pltpu.SemaphoreType.DMA((6,))],
     )
     return (input_grad.reshape(F, CH, H, W), weight_grad.reshape(3, 3, 3, CH, CH))
 

time: 73.9 us -> 73.9 us (level)
  no operation moved by 1% of the time
where the time goes in v10:
time: 73.9 us; the launch traced here: 73.4 us
  starting transfers between devices  37.7 us (51%)
  blocking collectives  20.9 us (28%)
  Pallas kernels  11.2 us (15%)
  waiting for transfers between devices  2.92 us (4%)
  between operations  0.74 us (1%)
    all_to_all x1, starting transfers between devices, local(): lax.all_to_all(packed.reshape(near, PACKED // near, W), NEAR, 0, 0, axis_...  14.2 us
    all_to_all x1, starting transfers between devices, local(): lax.all_to_all(slabs, 'z_pair', 0, 0, axis_index_groups=turned(depth, 4))  11.5 us
    all_to_all x1, blocking collectives, local(): lax.all_to_all(slots, NEAR, 0, 0, axis_index_groups=turned(near, 24))  11.3 us
    pallas_call x11, Pallas kernels, call(): pl.pallas_call(kernel, out_shape=tuple((jax.ShapeDtypeStruct(shape, dtype...  11.2 us
    all_gather x1, blocking collectives, local(): whole = lax.all_gather(own_half, 'core')  5.44 us
    ppermute x1, starting transfers between devices, local(): before = lax.ppermute(last_frames, TM, forward)  4.51 us
    all_gather x1, blocking collectives, local(): exchanged = lax.all_gather(given, 'core')  4.19 us
    ppermute x1, starting transfers between devices, local(): above = lax.ppermute(bottom, ROWS, [(i, i + 1) for i in range(rows - 1)])  3.54 us
  transfers between devices with their start and end apart: 6, of which 2 were waited for; matrix products, arithmetic and copies ran while one was open for 0% of the time, Pallas kernels for 10%

profile of v10, /device:TPU:1, one launch (start us, length us, event | category | flops | bytes accessed | tf_op | source)
XLA Modules:
  0.0 73.4 jit_solution(2722594520935414853)
XLA Ops:
  0.6 1.2 %load.1 = (bf16[2,384,128]{2,1,0:T(8,128)(2,1)S(1)}, bf16[4,384,128]{2,1,0:T(8,128)(2,1)S(1)}, bf16[4,384,128]{2,1,0:T(8,128)(2,1)S(1)}) custom-call(bf16[4,384,128]{2,1,0:T(8,128)(2,1)} %bitcast.13, bf16[4,384,128]{2,1,0:T(8,128)(2,1)} %bitcast.14), custom_call_target="tpu_custom_call" | custom-call | tf_op jit(solution)/shard_map/load/pallas_call | solution.py:222
  1.9 4.5 %collective-permute-start.2 = (bf16[2,384,128]{2,1,0:T(8,128)(2,1)S(1)}, bf16[2,384,128]{2,1,0:T(8,128)(2,1)S(1)}, u32[]{:S(2)}, u32[]{:S(2)}) collective-permute-start(bf16[2,384,128]{2,1,0:T(8,128)(2,1)S(1)} %get-tuple-element.26), channel_id=1, source_target_pairs={{0,32},{32,64},{64,96},{96,128},{128,160},{160,192},{192,224},{224... | collective-permute-start | bytes 589832 | tf_op jit(solution)/shard_map/ppermute | solution.py:259
  6.4 0.4 cot_rows.1
  6.8 3.5 %collective-permute-start = (bf16[96,512]{1,0:T(8,128)(2,1)S(1)}, bf16[96,512]{1,0:T(8,128)(2,1)S(1)}, u32[]{:S(2)}, u32[]{:S(2)}) collective-permute-start(bf16[96,512]{1,0:T(8,128)(2,1)S(1)} %get-tuple-element.20), channel_id=1, source_target_pairs={{0,1},{1,2},{2,3},{3,4},{4,5},{5,6},{6,7},{7,8},{8,9},{9,10},{10,1... | collective-permute-start | bytes 294920 | tf_op jit(solution)/shard_map/ppermute | solution.py:267
  10.4 1.3 %collective-permute-start.1 = (bf16[96,512]{1,0:T(8,128)(2,1)S(1)}, bf16[96,512]{1,0:T(8,128)(2,1)S(1)}, u32[]{:S(2)}, u32[]{:S(2)}) collective-permute-start(bf16[96,512]{1,0:T(8,128)(2,1)S(1)} %get-tuple-element.21), channel_id=1, source_target_pairs={{1,0},{2,1},{3,2},{4,3},{5,4},{6,5},{7,6},{8,7},{9,8},{10,9},{11,1... | collective-permute-start | bytes 294920 | tf_op jit(solution)/shard_map/ppermute | solution.py:268
  11.7 0.8 %active.1 = (bf16[4,288,512]{2,1,0:T(8,128)(2,1)S(1)}, f32[4,96,512]{2,1,0:T(8,128)S(1)}, f32[4,1,512]{2,1,0:T(1,128)S(1)}) custom-call(bf16[4,384,128]{2,1,0:T(8,128)(2,1)S(1)} %get-tuple-element.23.feat, bf16[384,384]{1,0:T(8,128)(2,1)S(1)} %get-tuple-element.24.order), custom_call_target="tpu_custom_call" | custom-call | tf_op jit(solution)/shard_map/active/pallas_call | solution.py:222
  12.4 1.3 %own_cells.1.inner_sum = f32[288,864]{1,0:T(8,128)S(1)} custom-call(bf16[384,512]{1,0:T(8,128)(2,1)S(1)} %get-tuple-element.22.own, bf16[4,288,512]{2,1,0:T(8,128)(2,1)S(1)} %get-tuple-element.25.act), custom_call_target="tpu_custom_call" | custom-call | tf_op jit(solution)/shard_map/own_cells/pallas_call | solution.py:222
  13.7 0.0 collective-permute-done.2.before
  13.7 1.1 %frames_before.1 = (f32[288,864]{1,0:T(8,128)S(1)}, bf16[2,288,256]{2,1,0:T(8,128)(2,1)S(1)}) custom-call(bf16[2,384,128]{2,1,0:T(8,128)(2,1)S(1)} %collective-permute-done.2.before, bf16[384,512]{1,0:T(8,128)(2,1)S(1)} %get-tuple-element.22.own, bf16[384,384]{1,0:T(8,128)(2,1)S(1)} %get-tuple-element.24.order, f32[288,864]{1,0:T(8,128)S(1)} %own_cells.1.inner_sum), custom_call_target="tpu_custom_call" | custom-call | tf_op jit(solution)/shard_map/frames_before/pallas_call | solution.py:222
  14.8 0.0 collective-permute-done.above
  14.8 1.1 %collective-permute-done.1.below = bf16[96,512]{1,0:T(8,128)(2,1)S(1)} collective-permute-done((bf16[96,512]{1,0:T(8,128)(2,1)S(1)}, bf16[96,512]{1,0:T(8,128)(2,1)S(1)}, u32[]{:S(2)}, u32[]{:S(2)}) %collective-permute-start.1) | collective-permute-done | bytes 98336 | tf_op jit(solution)/shard_map/ppermute | solution.py:268
  15.9 0.7 edge_rows.1
  16.6 4.2 %all-gather = bf16[2048,128]{1,0:T(8,128)(2,1)S(1)} all-gather(bf16[1024,128]{1,0:T(8,128)(2,1)S(1)} %get-tuple-element.34), channel_id=2, replica_groups=mesh['y_hi'=2,'x'=4,'core'=2,'y_lo'=2,'z_pair'=8,'z_in'=2] {'core'}, dimensions={0}, use_global_device_ids=true | all-gather | bytes 786432 | tf_op jit(solution)/shard_map/all_gather | solution.py:291
  20.8 0.7 %core_sum.1 = bf16[1024,128]{1,0:T(8,128)(2,1)} custom-call(s32[1]{0:T(128)} %bitcast.2.core, f32[1024,128]{1,0:T(8,128)S(1)} %get-tuple-element.33.kept, bf16[2,1024,128]{2,1,0:T(8,128)(2,1)S(1)} %bitcast.9), custom_call_target="tpu_custom_call" | custom-call | tf_op jit(solution)/shard_map/core_sum/pallas_call | solution.py:222
  21.6 14.2 %all-to-all-start = ((bf16[32,32,128]{2,1,0:T(8,128)(2,1)}), bf16[32,32,128]{2,1,0:T(8,128)(2,1)S(1)}, u32[]{:S(2)}, u32[]{:S(2)}) async-start(bf16[32,32,128]{2,1,0:T(8,128)(2,1)} %bitcast.6), calls=%async_computation | async-start | bytes 524288 | tf_op jit(solution)/shard_map/all_to_all | solution.py:302
  35.8 2.6 %collective-permute-start.3 = (bf16[576,256]{1,0:T(8,128)(2,1)S(1)}, bf16[576,256]{1,0:T(8,128)(2,1)S(1)}, u32[]{:S(2)}, u32[]{:S(2)}) collective-permute-start(bf16[576,256]{1,0:T(8,128)(2,1)S(1)} %get-tuple-element.29), channel_id=1, source_target_pairs={{32,0},{64,32},{96,64},{128,96},{160,128},{192,160},{224,192},{256... | collective-permute-start | bytes 884744 | tf_op jit(solution)/shard_map/ppermute | solution.py:292
  38.4 1.8 %all-to-all-done.parts = bf16[32,32,128]{2,1,0:T(8,128)(2,1)S(1)} async-done(((bf16[32,32,128]{2,1,0:T(8,128)(2,1)}), bf16[32,32,128]{2,1,0:T(8,128)(2,1)S(1)}, u32[]{:S(2)}, u32[]{:S(2)}) %all-to-all-start) | async-done | bytes 262176 | tf_op jit(solution)/shard_map/all_to_all | solution.py:302
  40.3 0.7 plane_sum.1
  40.9 11.5 %all-to-all-start.1 = ((bf16[8,32,128]{2,1,0:T(8,128)(2,1)}), bf16[8,32,128]{2,1,0:T(8,128)(2,1)S(1)}, u32[]{:S(2)}, u32[]{:S(2)}) async-start(bf16[8,32,128]{2,1,0:T(8,128)(2,1)} %plane_sum.1), calls=%async_computation.1 | async-start | bytes 131072 | tf_op jit(solution)/shard_map/all_to_all | solution.py:304
  52.4 3.0 %input_grad.1 = (bf16[4,384,128]{2,1,0:T(8,128)(2,1)}, f32[8,128]{1,0:T(8,128)S(1)}) custom-call(bf16[96,512]{1,0:T(8,128)(2,1)S(1)} %collective-permute-done.above, bf16[96,512]{1,0:T(8,128)(2,1)S(1)} %collective-permute-done.1.below, bf16[384,512]{1,0:T(8,128)(2,1)S(1)} %get-tuple-element.22.own, bf16[576,256]{1,0:T(8,128)(2,1)S(1)} %collective-permute-done.3.later, ...), custom_call_target="tpu_custom_call" | custom-call | flops 2147483648 | tf_op jit(solution)/shard_map/input_grad/pallas_call | solution.py:222
  55.4 0.0 all-to-all-done.1.parts
  55.4 11.3 %all_to_all.15 = bf16[32,32,128]{2,1,0:T(8,128)(2,1)S(1)} all-to-all(bf16[32,32,128]{2,1,0:T(8,128)(2,1)S(1)} %depth_sum.1), channel_id=1, replica_groups={{384,385,400,401,448,449,464,465,0,1,16,17,64,65,80,81,128,129,144,145,..., dimensions={0} | all-to-all | bytes 524288 | tf_op jit(solution)/shard_map/all_to_all | solution.py:306
  66.7 5.4 %all_gather.11.refs_0_ = bf16[2,1024,128]{2,1,0:T(8,128)(2,1)S(1)} all-gather(bf16[1,1024,128]{2,1,0:T(8,128)(2,1)S(1)} %bitcast.12), channel_id=1, replica_groups=mesh['y_hi'=2,'x'=4,'core'=2,'y_lo'=2,'z_pair'=8,'z_in'=2] {'core'}, dimensions={0}, use_global_device_ids=true | all-gather | bytes 786432 | tf_op jit(solution)/shard_map/all_gather | solution.py:307
  72.2 1.2 %unpack.1 = f32[27,96,96]{2,1,0:T(8,128)} custom-call(bf16[2,1024,128]{2,1,0:T(8,128)(2,1)S(1)} %all_gather.11.refs_0_), custom_call_target="tpu_custom_call" | custom-call | tf_op jit(solution)/shard_map/unpack/pallas_call | solution.py:222
  (4 shorter events, 0.0 us)
Async XLA Ops:
  1.9 11.8 %collective-permute-start.2 = (bf16[2,384,128]{2,1,0:T(8,128)(2,1)S(1)}, bf16[2,384,128]{2,1,0:T(8,128)(2,1)S(1)}, u32[]{:S(2)}, u32[]{:S(2)}) collective-permute-start(bf16[2,384,128]{2,1,0:T(8,128)(2,1)S(1)} %get-tuple-element.26), channel_id=1, source_target_pairs={{0,32},{32,64},{64,96},{96,128},{128,160},{160,192},{192,224},{224... | collective-permute-start | bytes 589832 | tf_op jit(solution)/shard_map/ppermute | solution.py:259
  6.8 8.0 %collective-permute-start = (bf16[96,512]{1,0:T(8,128)(2,1)S(1)}, bf16[96,512]{1,0:T(8,128)(2,1)S(1)}, u32[]{:S(2)}, u32[]{:S(2)}) collective-permute-start(bf16[96,512]{1,0:T(8,128)(2,1)S(1)} %get-tuple-element.20), channel_id=1, source_target_pairs={{0,1},{1,2},{2,3},{3,4},{4,5},{5,6},{6,7},{7,8},{8,9},{9,10},{10,1... | collective-permute-start | bytes 294920 | tf_op jit(solution)/shard_map/ppermute | solution.py:267
  10.4 5.5 %collective-permute-start.1 = (bf16[96,512]{1,0:T(8,128)(2,1)S(1)}, bf16[96,512]{1,0:T(8,128)(2,1)S(1)}, u32[]{:S(2)}, u32[]{:S(2)}) collective-permute-start(bf16[96,512]{1,0:T(8,128)(2,1)S(1)} %get-tuple-element.21), channel_id=1, source_target_pairs={{1,0},{2,1},{3,2},{4,3},{5,4},{6,5},{7,6},{8,7},{9,8},{10,9},{11,1... | collective-permute-start | bytes 294920 | tf_op jit(solution)/shard_map/ppermute | solution.py:268
  20.8 31.6 %copy-start = (bf16[3,3,3,96,96]{4,3,2,1,0:T(8,128)(2,1)S(1)}, bf16[3,3,3,96,96]{4,3,2,1,0:T(8,128)(2,1)}, u32[]{:S(2)}) copy-start(bf16[3,3,3,96,96]{4,3,2,1,0:T(8,128)(2,1)} %param.4) | copy-start | bytes 1492996
  21.6 18.7 %all-to-all-start = ((bf16[32,32,128]{2,1,0:T(8,128)(2,1)}), bf16[32,32,128]{2,1,0:T(8,128)(2,1)S(1)}, u32[]{:S(2)}, u32[]{:S(2)}) async-start(bf16[32,32,128]{2,1,0:T(8,128)(2,1)} %bitcast.6), calls=%async_computation | async-start | bytes 524288 | tf_op jit(solution)/shard_map/all_to_all | solution.py:302
  35.8 16.6 %collective-permute-start.3 = (bf16[576,256]{1,0:T(8,128)(2,1)S(1)}, bf16[576,256]{1,0:T(8,128)(2,1)S(1)}, u32[]{:S(2)}, u32[]{:S(2)}) collective-permute-start(bf16[576,256]{1,0:T(8,128)(2,1)S(1)} %get-tuple-element.29), channel_id=1, source_target_pairs={{32,0},{64,32},{96,64},{128,96},{160,128},{192,160},{224,192},{256... | collective-permute-start | bytes 884744 | tf_op jit(solution)/shard_map/ppermute | solution.py:292
  40.9 14.5 %all-to-all-start.1 = ((bf16[8,32,128]{2,1,0:T(8,128)(2,1)}), bf16[8,32,128]{2,1,0:T(8,128)(2,1)S(1)}, u32[]{:S(2)}, u32[]{:S(2)}) async-start(bf16[8,32,128]{2,1,0:T(8,128)(2,1)} %plane_sum.1), calls=%async_computation.1 | async-start | bytes 131072 | tf_op jit(solution)/shard_map/all_to_all | solution.py:304

commit v11 on v8

--- a/solution.py
+++ b/solution.py
@@ -7,7 +7,7 @@
 
 TM = ("y_hi", "x", "core")
 ROWS = ("y_lo", "z_pair", "z_in")
-NEAR = ("y_hi", "x", "y_lo", "z_in")
+NEAR = ("z_in", "y_hi", "x", "y_lo")
 CH = 96
 W = 128
 F = 4
@@ -298,11 +298,11 @@
     )
 
     (packed,) = call(add_kernel, "core_sum", [((PACKED, W), BF16)], (kept, exchanged), smem=(core,))
-    parts = lax.all_to_all(packed.reshape(near, PACKED // near, W), NEAR, 0, 0, axis_index_groups=turned(near, 24))
+    parts = lax.all_to_all(packed.reshape(near, PACKED // near, W), NEAR, 0, 0, axis_index_groups=turned(near, 12))
     slabs = sum_to_slots(parts, depth, "plane_sum")
     slabs = lax.all_to_all(slabs, "z_pair", 0, 0, axis_index_groups=turned(depth, 4))
     slots = sum_to_slots(slabs, near, "depth_sum", after=(done,))
-    own_half = lax.all_to_all(slots, NEAR, 0, 0, axis_index_groups=turned(near, 24)).reshape(PACKED, W)
+    own_half = lax.all_to_all(slots, NEAR, 0, 0, axis_index_groups=turned(near, 12)).reshape(PACKED, W)
     whole = lax.all_gather(own_half, "core")
     (weight_grad,) = call(
         lambda *refs: unpack_kernel(1.0 / float(cells) ** 0.5, *refs),

time: 73.9 us -> 73.9 us (level)
  no operation moved by 1% of the time
where the time goes in v11:
time: 73.9 us; the launch traced here: 73.5 us
  starting transfers between devices  37.7 us (51%)
  blocking collectives  20.9 us (28%)
  Pallas kernels  11.2 us (15%)
  waiting for transfers between devices  2.91 us (4%)
  between operations  0.74 us (1%)
    all_to_all x1, starting transfers between devices, local(): lax.all_to_all(packed.reshape(near, PACKED // near, W), NEAR, 0, 0, axis_...  14.2 us
    all_to_all x1, starting transfers between devices, local(): lax.all_to_all(slabs, 'z_pair', 0, 0, axis_index_groups=turned(depth, 4))  11.5 us
    all_to_all x1, blocking collectives, local(): lax.all_to_all(slots, NEAR, 0, 0, axis_index_groups=turned(near, 12))  11.3 us
    pallas_call x11, Pallas kernels, call(): pl.pallas_call(kernel, out_shape=tuple((jax.ShapeDtypeStruct(shape, dtype...  11.2 us
    all_gather x1, blocking collectives, local(): whole = lax.all_gather(own_half, 'core')  5.42 us
    ppermute x1, starting transfers between devices, local(): before = lax.ppermute(last_frames, TM, forward)  4.51 us
    all_gather x1, blocking collectives, local(): exchanged = lax.all_gather(given, 'core')  4.19 us
    ppermute x1, starting transfers between devices, local(): above = lax.ppermute(bottom, ROWS, [(i, i + 1) for i in range(rows - 1)])  3.54 us
  transfers between devices with their start and end apart: 6, of which 2 were waited for; matrix products, arithmetic and copies ran while one was open for 0% of the time, Pallas kernels for 10%

profile of v11, /device:TPU:1, one launch (start us, length us, event | category | flops | bytes accessed | tf_op | source)
XLA Modules:
  0.0 73.5 jit_solution(16877753555935016767)
XLA Ops:
  0.6 1.2 %load.1 = (bf16[2,384,128]{2,1,0:T(8,128)(2,1)S(1)}, bf16[4,384,128]{2,1,0:T(8,128)(2,1)S(1)}, bf16[4,384,128]{2,1,0:T(8,128)(2,1)S(1)}) custom-call(bf16[4,384,128]{2,1,0:T(8,128)(2,1)} %bitcast.13, bf16[4,384,128]{2,1,0:T(8,128)(2,1)} %bitcast.14), custom_call_target="tpu_custom_call" | custom-call | tf_op jit(solution)/shard_map/load/pallas_call | solution.py:221
  1.9 4.5 %collective-permute-start.2 = (bf16[2,384,128]{2,1,0:T(8,128)(2,1)S(1)}, bf16[2,384,128]{2,1,0:T(8,128)(2,1)S(1)}, u32[]{:S(2)}, u32[]{:S(2)}) collective-permute-start(bf16[2,384,128]{2,1,0:T(8,128)(2,1)S(1)} %get-tuple-element.26), channel_id=1, source_target_pairs={{0,32},{32,64},{64,96},{96,128},{128,160},{160,192},{192,224},{224... | collective-permute-start | bytes 589832 | tf_op jit(solution)/shard_map/ppermute | solution.py:258
  6.4 0.4 cot_rows.1
  6.8 3.5 %collective-permute-start = (bf16[96,512]{1,0:T(8,128)(2,1)S(1)}, bf16[96,512]{1,0:T(8,128)(2,1)S(1)}, u32[]{:S(2)}, u32[]{:S(2)}) collective-permute-start(bf16[96,512]{1,0:T(8,128)(2,1)S(1)} %get-tuple-element.20), channel_id=1, source_target_pairs={{0,1},{1,2},{2,3},{3,4},{4,5},{5,6},{6,7},{7,8},{8,9},{9,10},{10,1... | collective-permute-start | bytes 294920 | tf_op jit(solution)/shard_map/ppermute | solution.py:266
  10.4 1.3 %collective-permute-start.1 = (bf16[96,512]{1,0:T(8,128)(2,1)S(1)}, bf16[96,512]{1,0:T(8,128)(2,1)S(1)}, u32[]{:S(2)}, u32[]{:S(2)}) collective-permute-start(bf16[96,512]{1,0:T(8,128)(2,1)S(1)} %get-tuple-element.21), channel_id=1, source_target_pairs={{1,0},{2,1},{3,2},{4,3},{5,4},{6,5},{7,6},{8,7},{9,8},{10,9},{11,1... | collective-permute-start | bytes 294920 | tf_op jit(solution)/shard_map/ppermute | solution.py:267
  11.7 0.8 %active.1 = (bf16[4,288,512]{2,1,0:T(8,128)(2,1)S(1)}, f32[4,96,512]{2,1,0:T(8,128)S(1)}, f32[4,1,512]{2,1,0:T(1,128)S(1)}) custom-call(bf16[4,384,128]{2,1,0:T(8,128)(2,1)S(1)} %get-tuple-element.23.feat, bf16[384,384]{1,0:T(8,128)(2,1)S(1)} %get-tuple-element.24.order), custom_call_target="tpu_custom_call" | custom-call | tf_op jit(solution)/shard_map/active/pallas_call | solution.py:221
  12.4 1.3 %own_cells.1.inner_sum = f32[288,864]{1,0:T(8,128)S(1)} custom-call(bf16[384,512]{1,0:T(8,128)(2,1)S(1)} %get-tuple-element.22.own, bf16[4,288,512]{2,1,0:T(8,128)(2,1)S(1)} %get-tuple-element.25.act), custom_call_target="tpu_custom_call" | custom-call | tf_op jit(solution)/shard_map/own_cells/pallas_call | solution.py:221
  13.7 0.0 collective-permute-done.2.before
  13.7 1.1 %frames_before.1 = (f32[288,864]{1,0:T(8,128)S(1)}, bf16[2,288,256]{2,1,0:T(8,128)(2,1)S(1)}) custom-call(bf16[2,384,128]{2,1,0:T(8,128)(2,1)S(1)} %collective-permute-done.2.before, bf16[384,512]{1,0:T(8,128)(2,1)S(1)} %get-tuple-element.22.own, bf16[384,384]{1,0:T(8,128)(2,1)S(1)} %get-tuple-element.24.order, f32[288,864]{1,0:T(8,128)S(1)} %own_cells.1.inner_sum), custom_call_target="tpu_custom_call" | custom-call | tf_op jit(solution)/shard_map/frames_before/pallas_call | solution.py:221
  14.8 0.0 collective-permute-done.above
  14.8 1.1 %collective-permute-done.1.below = bf16[96,512]{1,0:T(8,128)(2,1)S(1)} collective-permute-done((bf16[96,512]{1,0:T(8,128)(2,1)S(1)}, bf16[96,512]{1,0:T(8,128)(2,1)S(1)}, u32[]{:S(2)}, u32[]{:S(2)}) %collective-permute-start.1) | collective-permute-done | bytes 98336 | tf_op jit(solution)/shard_map/ppermute | solution.py:267
  15.9 0.7 edge_rows.1
  16.6 4.2 %all-gather = bf16[2048,128]{1,0:T(8,128)(2,1)S(1)} all-gather(bf16[1024,128]{1,0:T(8,128)(2,1)S(1)} %get-tuple-element.34), channel_id=2, replica_groups=mesh['y_hi'=2,'x'=4,'core'=2,'y_lo'=2,'z_pair'=8,'z_in'=2] {'core'}, dimensions={0}, use_global_device_ids=true | all-gather | bytes 786432 | tf_op jit(solution)/shard_map/all_gather | solution.py:290
  20.8 0.7 %core_sum.1 = bf16[1024,128]{1,0:T(8,128)(2,1)} custom-call(s32[1]{0:T(128)} %bitcast.2.core, f32[1024,128]{1,0:T(8,128)S(1)} %get-tuple-element.33.kept, bf16[2,1024,128]{2,1,0:T(8,128)(2,1)S(1)} %bitcast.9), custom_call_target="tpu_custom_call" | custom-call | tf_op jit(solution)/shard_map/core_sum/pallas_call | solution.py:221
  21.6 14.2 %all-to-all-start = ((bf16[32,32,128]{2,1,0:T(8,128)(2,1)}), bf16[32,32,128]{2,1,0:T(8,128)(2,1)S(1)}, u32[]{:S(2)}, u32[]{:S(2)}) async-start(bf16[32,32,128]{2,1,0:T(8,128)(2,1)} %bitcast.6), calls=%async_computation | async-start | bytes 524288 | tf_op jit(solution)/shard_map/all_to_all | solution.py:301
  35.8 2.6 %collective-permute-start.3 = (bf16[576,256]{1,0:T(8,128)(2,1)S(1)}, bf16[576,256]{1,0:T(8,128)(2,1)S(1)}, u32[]{:S(2)}, u32[]{:S(2)}) collective-permute-start(bf16[576,256]{1,0:T(8,128)(2,1)S(1)} %get-tuple-element.29), channel_id=1, source_target_pairs={{32,0},{64,32},{96,64},{128,96},{160,128},{192,160},{224,192},{256... | collective-permute-start | bytes 884744 | tf_op jit(solution)/shard_map/ppermute | solution.py:291
  38.4 1.8 %all-to-all-done.parts = bf16[32,32,128]{2,1,0:T(8,128)(2,1)S(1)} async-done(((bf16[32,32,128]{2,1,0:T(8,128)(2,1)}), bf16[32,32,128]{2,1,0:T(8,128)(2,1)S(1)}, u32[]{:S(2)}, u32[]{:S(2)}) %all-to-all-start) | async-done | bytes 262176 | tf_op jit(solution)/shard_map/all_to_all | solution.py:301
  40.3 0.7 plane_sum.1
  40.9 11.5 %all-to-all-start.1 = ((bf16[8,32,128]{2,1,0:T(8,128)(2,1)}), bf16[8,32,128]{2,1,0:T(8,128)(2,1)S(1)}, u32[]{:S(2)}, u32[]{:S(2)}) async-start(bf16[8,32,128]{2,1,0:T(8,128)(2,1)} %plane_sum.1), calls=%async_computation.1 | async-start | bytes 131072 | tf_op jit(solution)/shard_map/all_to_all | solution.py:303
  52.4 3.0 %input_grad.1 = (bf16[4,384,128]{2,1,0:T(8,128)(2,1)}, f32[8,128]{1,0:T(8,128)S(1)}) custom-call(bf16[96,512]{1,0:T(8,128)(2,1)S(1)} %collective-permute-done.above, bf16[96,512]{1,0:T(8,128)(2,1)S(1)} %collective-permute-done.1.below, bf16[384,512]{1,0:T(8,128)(2,1)S(1)} %get-tuple-element.22.own, bf16[576,256]{1,0:T(8,128)(2,1)S(1)} %collective-permute-done.3.later, ...), custom_call_target="tpu_custom_call" | custom-call | flops 2147483648 | tf_op jit(solution)/shard_map/input_grad/pallas_call | solution.py:221
  55.4 0.0 all-to-all-done.1.parts
  55.4 11.3 %all_to_all.15 = bf16[32,32,128]{2,1,0:T(8,128)(2,1)S(1)} all-to-all(bf16[32,32,128]{2,1,0:T(8,128)(2,1)S(1)} %depth_sum.1), channel_id=1, replica_groups={{384,400,448,464,1,17,65,81,129,145,193,209,257,273,321,337,385,401,449..., dimensions={0} | all-to-all | bytes 524288 | tf_op jit(solution)/shard_map/all_to_all | solution.py:305
  66.7 5.4 %all_gather.11.refs_0_ = bf16[2,1024,128]{2,1,0:T(8,128)(2,1)S(1)} all-gather(bf16[1,1024,128]{2,1,0:T(8,128)(2,1)S(1)} %bitcast.12), channel_id=1, replica_groups=mesh['y_hi'=2,'x'=4,'core'=2,'y_lo'=2,'z_pair'=8,'z_in'=2] {'core'}, dimensions={0}, use_global_device_ids=true | all-gather | bytes 786432 | tf_op jit(solution)/shard_map/all_gather | solution.py:306
  72.2 1.3 %unpack.1 = f32[27,96,96]{2,1,0:T(8,128)} custom-call(bf16[2,1024,128]{2,1,0:T(8,128)(2,1)S(1)} %all_gather.11.refs_0_), custom_call_target="tpu_custom_call" | custom-call | tf_op jit(solution)/shard_map/unpack/pallas_call | solution.py:221
  (4 shorter events, 0.0 us)
Async XLA Ops:
  1.9 11.8 %collective-permute-start.2 = (bf16[2,384,128]{2,1,0:T(8,128)(2,1)S(1)}, bf16[2,384,128]{2,1,0:T(8,128)(2,1)S(1)}, u32[]{:S(2)}, u32[]{:S(2)}) collective-permute-start(bf16[2,384,128]{2,1,0:T(8,128)(2,1)S(1)} %get-tuple-element.26), channel_id=1, source_target_pairs={{0,32},{32,64},{64,96},{96,128},{128,160},{160,192},{192,224},{224... | collective-permute-start | bytes 589832 | tf_op jit(solution)/shard_map/ppermute | solution.py:258
  6.8 8.0 %collective-permute-start = (bf16[96,512]{1,0:T(8,128)(2,1)S(1)}, bf16[96,512]{1,0:T(8,128)(2,1)S(1)}, u32[]{:S(2)}, u32[]{:S(2)}) collective-permute-start(bf16[96,512]{1,0:T(8,128)(2,1)S(1)} %get-tuple-element.20), channel_id=1, source_target_pairs={{0,1},{1,2},{2,3},{3,4},{4,5},{5,6},{6,7},{7,8},{8,9},{9,10},{10,1... | collective-permute-start | bytes 294920 | tf_op jit(solution)/shard_map/ppermute | solution.py:266
  10.4 5.5 %collective-permute-start.1 = (bf16[96,512]{1,0:T(8,128)(2,1)S(1)}, bf16[96,512]{1,0:T(8,128)(2,1)S(1)}, u32[]{:S(2)}, u32[]{:S(2)}) collective-permute-start(bf16[96,512]{1,0:T(8,128)(2,1)S(1)} %get-tuple-element.21), channel_id=1, source_target_pairs={{1,0},{2,1},{3,2},{4,3},{5,4},{6,5},{7,6},{8,7},{9,8},{10,9},{11,1... | collective-permute-start | bytes 294920 | tf_op jit(solution)/shard_map/ppermute | solution.py:267
  20.8 31.6 %copy-start = (bf16[3,3,3,96,96]{4,3,2,1,0:T(8,128)(2,1)S(1)}, bf16[3,3,3,96,96]{4,3,2,1,0:T(8,128)(2,1)}, u32[]{:S(2)}) copy-start(bf16[3,3,3,96,96]{4,3,2,1,0:T(8,128)(2,1)} %param.4) | copy-start | bytes 1492996
  21.6 18.7 %all-to-all-start = ((bf16[32,32,128]{2,1,0:T(8,128)(2,1)}), bf16[32,32,128]{2,1,0:T(8,128)(2,1)S(1)}, u32[]{:S(2)}, u32[]{:S(2)}) async-start(bf16[32,32,128]{2,1,0:T(8,128)(2,1)} %bitcast.6), calls=%async_computation | async-start | bytes 524288 | tf_op jit(solution)/shard_map/all_to_all | solution.py:301
  35.8 16.6 %collective-permute-start.3 = (bf16[576,256]{1,0:T(8,128)(2,1)S(1)}, bf16[576,256]{1,0:T(8,128)(2,1)S(1)}, u32[]{:S(2)}, u32[]{:S(2)}) collective-permute-start(bf16[576,256]{1,0:T(8,128)(2,1)S(1)} %get-tuple-element.29), channel_id=1, source_target_pairs={{32,0},{64,32},{96,64},{128,96},{160,128},{192,160},{224,192},{256... | collective-permute-start | bytes 884744 | tf_op jit(solution)/shard_map/ppermute | solution.py:291
  40.9 14.5 %all-to-all-start.1 = ((bf16[8,32,128]{2,1,0:T(8,128)(2,1)}), bf16[8,32,128]{2,1,0:T(8,128)(2,1)S(1)}, u32[]{:S(2)}, u32[]{:S(2)}) async-start(bf16[8,32,128]{2,1,0:T(8,128)(2,1)} %plane_sum.1), calls=%async_computation.1 | async-start | bytes 131072 | tf_op jit(solution)/shard_map/all_to_all | solution.py:303
